TPU v7x, 32 devices: a whole 2x2x4 slice. The times are simulated.
32 devices in a mesh: wave: 4 (over y, core), tx: 2 (over x), ty: 4 (over z).
Axes of the slice: x: 2, y: 2, z: 4, core: 2. Of those that a mesh axis runs over, the one named last changes fastest.
Arguments:
- initial_fields: float32 [4, 2, 12, 32, 2048], P('wave', None, None, 'tx', 'ty'), may hold values from -6 to 6
- source_profiles: float32 [4, 2, 3, 2048], P('wave'), may hold values from -6 to 6
- source_waveforms: float32 [4, 2, 5], P('wave'), may hold values from -3 to 3
- material_map: int32 [32, 2048], P('tx', 'ty'), may hold values from 0 to 2
- design_density: float32 [32, 2048], P('tx', 'ty'), may hold values from 0 to 1
- material_table: float32 [3, 4], replicated, may hold values from 0.02 to 12, as said below
- plane_indices: int32 [2], replicated, may hold values from 0 to 31
- design_box: int32 [6], replicated, may hold values from 0 to 64, as said below
Outputs:
- density_gradient: float32 [32, 2048], P('tx', 'ty')
- final_electric: float32 [4, 2, 3, 32, 2048], P('wave', None, None, 'tx', 'ty')
Inputs may be any that keep to these rules, and one draw needn't show every extreme that they name: `material_map`: material ids are below 3. `material_table`: column 0 lies in [1, 12], column 1 in [0.5, 3], column 2 in [0.3, 1.5], column 3 in [0.02, 0.5]. `plane_indices`: entry 0 is the source plane of the forward run, entry 1 the monitor plane where the adjoint run's source enters. `design_box`: x0 <= 4, y0 <= 4, x1 = 32, y1 = 32, z0 = 0, z1 = 64.
All inputs are finite; a program needn't handle non-finite values.
Results may differ from a plain program's by a relative error of at most 0.0001.
Values sent between devices are 32-bit elements; how exact they have to be, the bound alone decides.
No kernel may reach another device: no remote copies, remote signals or barrier semaphores. Data moves between devices by JAX's collectives and lax.ppermute only.
A program may use at most 64 MiB of HBM per device.

v0:
```python
import jax
import jax.numpy as jnp
from jax import lax
from jax.sharding import PartitionSpec as P

NZ = 64
STEPS = 5
NMAT = 3


time_step = 0.5
contrast = 2.0


def shifted_2(value, axis, steps):
    count = lax.axis_size(axis)
    initial, last = (max(0, -steps), min(count, count - steps))
    return lax.ppermute(value, axis, [(source, source + steps) for source in range(initial, last)])


def ahead_rows(values, border):
    return jnp.concatenate([values[:, 1:], border], axis=1)


def behind_rows(values, border):
    return jnp.concatenate([border, values[:, :-1]], axis=1)


def ahead_lines(values, border):
    width = border.shape[2]
    return jnp.concatenate([values[:, :, width:], border], axis=2)


def behind_lines(values, border):
    width = border.shape[2]
    return jnp.concatenate([border, values[:, :, :-width]], axis=2)


def ahead_depth(values, depth_last):
    shifted = jnp.concatenate([values[:, :, 1:], jnp.zeros_like(values[:, :, :1])], axis=2)
    return jnp.where(depth_last, 0.0, shifted)


def behind_depth(values, depth_first):
    shifted = jnp.concatenate([jnp.zeros_like(values[:, :, :1]), values[:, :, :-1]], axis=2)
    return jnp.where(depth_first, 0.0, shifted)


def curl_electric(field, rows_ahead, lines_ahead, depth_last):
    part_one, part_two, part_three = (field[:, 0], field[:, 1], field[:, 2])
    curl_one = (
        ahead_lines(part_three, lines_ahead[:, 1])
        - part_three
        - (ahead_depth(part_two, depth_last) - part_two)
    )
    curl_two = (
        ahead_depth(part_one, depth_last)
        - part_one
        - (ahead_rows(part_three, rows_ahead[:, 1]) - part_three)
    )
    curl_three = (
        ahead_rows(part_two, rows_ahead[:, 0])
        - part_two
        - (ahead_lines(part_one, lines_ahead[:, 0]) - part_one)
    )
    return jnp.stack([curl_one, curl_two, curl_three], axis=1)


def curl_magnetic(field, rows_behind, lines_behind, depth_first):
    part_one, part_two, part_three = (field[:, 0], field[:, 1], field[:, 2])
    curl_one = (
        part_three
        - behind_lines(part_three, lines_behind[:, 1])
        - (part_two - behind_depth(part_two, depth_first))
    )
    curl_two = (
        part_one
        - behind_depth(part_one, depth_first)
        - (part_three - behind_rows(part_three, rows_behind[:, 1]))
    )
    curl_three = (
        part_two
        - behind_rows(part_two, rows_behind[:, 0])
        - (part_one - behind_lines(part_one, lines_behind[:, 0]))
    )
    return jnp.stack([curl_one, curl_two, curl_three], axis=1)


def electric_borders(field):
    rows_ahead = shifted_2(field[:, 1:, :1, :], "tx", -1)
    flat_part = field[:, 0::2, :, :NZ].reshape(field.shape[0], 2, field.shape[2] * NZ)
    lines_ahead = shifted_2(flat_part, "ty", -1)
    return (rows_ahead, lines_ahead.reshape(field.shape[0], 2, field.shape[2], NZ))


def magnetic_borders(field):
    rows_behind = shifted_2(field[:, 1:, -1:, :], "tx", 1)
    flat_part = field[:, 0::2, :, -NZ:].reshape(field.shape[0], 2, field.shape[2] * NZ)
    lines_behind = shifted_2(flat_part, "ty", 1)
    return (rows_behind, lines_behind.reshape(field.shape[0], 2, field.shape[2], NZ))


def design_mask(grid_rows, grid_flat, design_box):
    lines = grid_flat // NZ
    depth_ids = grid_flat % NZ
    in_rows = (grid_rows >= design_box[0]) & (grid_rows < design_box[1])
    in_lines = (
        (lines >= design_box[2])
        & (lines < design_box[3])
        & (depth_ids >= design_box[4])
        & (depth_ids < design_box[5])
    )
    return (in_rows[:, None] & in_lines[None, :]).astype(jnp.float32)


def coefficients(material_map, design_density, material_table, inside_design):
    damping = material_table[:, 3]
    denom = 1.0 + 0.25 * damping
    decay = (1.0 - 0.25 * damping) / denom
    drive = material_table[:, 2] * material_table[:, 2] * time_step / denom
    coupled = drive * material_table[:, 1]
    permittivity = jnp.zeros(material_map.shape, jnp.float32)
    decay_map = jnp.zeros(material_map.shape, jnp.float32)
    drive_map = jnp.zeros(material_map.shape, jnp.float32)
    coupled_map = jnp.zeros(material_map.shape, jnp.float32)
    for material_id in range(NMAT):
        chosen = (material_map == material_id).astype(jnp.float32)
        permittivity = permittivity + chosen * material_table[material_id, 0]
        decay_map = decay_map + chosen * decay[material_id]
        drive_map = drive_map + chosen * drive[material_id]
        coupled_map = coupled_map + chosen * coupled[material_id]
    permittivity = permittivity + inside_design * design_density * contrast
    return jnp.stack([time_step / permittivity, decay_map, drive_map, coupled_map])


def advance(
    electric,
    magnetic,
    polarization,
    current,
    coeffs,
    inside,
    depth_last,
    depth_first,
    source,
    get_electric,
    get_magnetic,
):
    rows_ahead, lines_ahead = get_electric(electric)
    magnetic = (
        magnetic - time_step * curl_electric(electric, rows_ahead, lines_ahead, depth_last)
    ) * inside
    current = coeffs[1] * current + coeffs[3] * electric - coeffs[2] * polarization
    polarization = polarization + time_step * current
    rows_behind, lines_behind = get_magnetic(magnetic)
    electric = electric + coeffs[0] * (
        curl_magnetic(magnetic, rows_behind, lines_behind, depth_first) - current - source
    )
    return (electric, magnetic, polarization, current)


def on_device(
    initial_fields,
    source_profiles,
    source_waveforms,
    material_map,
    design_density,
    material_table,
    plane_indices,
    design_box,
):
    rows_here, flat_here = material_map.shape
    tile_row = lax.axis_index("tx")
    tile_col = lax.axis_index("ty")
    grid_rows = tile_row * rows_here + jnp.arange(rows_here, dtype=jnp.int32)
    grid_flat = tile_col * flat_here + jnp.arange(flat_here, dtype=jnp.int32)
    inside_design = design_mask(grid_rows, grid_flat, design_box)
    coeffs = coefficients(material_map, design_density, material_table, inside_design)
    fields = initial_fields[0]
    profiles = source_profiles[0]
    waveforms = source_waveforms[0]
    inside = 1.0
    profiles_here = lax.dynamic_slice_in_dim(profiles, tile_col * flat_here, flat_here, axis=2)
    depth_ids = grid_flat % NZ
    depth_last = depth_ids == NZ - 1
    depth_first = depth_ids == 0
    plane_rows = (grid_rows[None, :] == plane_indices[:, None]).astype(jnp.float32)
    electric = fields[:, 0:3]
    magnetic = fields[:, 3:6]
    polarization = fields[:, 6:9]
    current = fields[:, 9:12]
    forward_history = [electric[0]]
    adjoint_history = [electric[1]]
    for step_index in range(STEPS):
        source = (
            waveforms[:, step_index][:, None, None, None]
            * profiles_here[:, :, None, :]
            * plane_rows[:, None, :, None]
        )
        electric, magnetic, polarization, current = advance(
            electric,
            magnetic,
            polarization,
            current,
            coeffs,
            inside,
            depth_last,
            depth_first,
            source,
            electric_borders,
            magnetic_borders,
        )
        forward_history.append(electric[0])
        adjoint_history.append(electric[1])
    partial_value = jnp.zeros((rows_here, flat_here), jnp.float32)
    for pair_index in range(1, STEPS + 1):
        partial_value = partial_value + jnp.sum(
            adjoint_history[STEPS + 1 - pair_index]
            * (forward_history[pair_index] - forward_history[pair_index - 1]),
            axis=0,
        )
    collected = lax.psum(partial_value, "wave")
    density_gradient = contrast * inside_design * collected
    return (density_gradient, electric[None])


def solution(mesh):
    placed = (
        P("wave", None, None, "tx", "ty"),
        P("wave", None, None, None),
        P("wave", None, None),
        P("tx", "ty"),
        P("tx", "ty"),
        P(),
        P(),
        P(),
    )
    return jax.shard_map(
        on_device,
        mesh=mesh,
        in_specs=placed,
        out_specs=(P("tx", "ty"), P("wave", None, None, "tx", "ty")),
        check_vma=False,
    )
```

profile of v0, /device:TPU:0, one launch (start us, length us, event | category | flops | bytes accessed | tf_op | source)
XLA Modules:
  0.0 126.0 jit_solution(17983421215603182221)
XLA Ops:
  2.0 1.3 %collective-permute-start = (f32[2,2,1024]{2,0,1:T(2,128)S(1)}, f32[2,2,1024]{2,0,1:T(2,128)S(1)}, u32[]{:S(2)}, u32[]{:S(2)}) collective-permute-start(f32[2,2,1024]{2,0,1:T(2,128)S(1)} %reshape.295), channel_id=1, source_target_pairs={{1,0},{2,1},{3,2},{5,4},{6,5},{7,6},{9,8},{10,9},{11,10},{13,12},{... | collective-permute-start | bytes 49160 | tf_op jit(solution)/shard_map/ppermute | solution.py:18
  3.3 1.3 %collective-permute-start.1 = (f32[2,2,1,512]{3,2,0,1:T(1,128)S(1)}, f32[2,2,1,512]{3,2,0,1:T(1,128)S(1)}, u32[]{:S(2)}, u32[]{:S(2)}) collective-permute-start(f32[2,2,1,512]{3,2,0,1:T(1,128)S(1)} %slice.789), channel_id=1, source_target_pairs={{4,0},{5,1},{6,2},{7,3},{12,8},{13,9},{14,10},{15,11},{20,16},{21,... | collective-permute-start | bytes 24584 | tf_op jit(solution)/shard_map/ppermute | solution.py:18
  10.1 2.5 %compare_and_fusion = pred[512]{0:T(512)(128)(4,1)S(1)} fusion(s32[]{:T(128)} %bitcast.5, s32[]{:T(128)} %bitcast.4, s32[]{:T(128)} %bitcast.3, s32[]{:T(128)} %bitcast.2, s32[]{:T(128)S(6)} %mul.416), kind=kLoop, calls=%fused_computation.258 | loop fusion | flops 13824 | bytes 532 | tf_op jit(solution)/shard_map/and | solution.py:108
  13.2 1.9 %fusion.80 = (f32[16,512]{1,0:T(8,128)S(1)}, pred[16,512]{1,0:T(8,128)(4,1)S(1)}, pred[16,512]{1,0:T(8,128)(4,1)S(1)}, pred[16,512]{1,0:T(8,128)(4,1)S(1)}) fusion(f32[16,512]{1,0:T(8,128)S(1)} %copy-done.9, f32[]{:T(128)} %bitcast.9, f32[]{:T(128)} %bitcast.8, f32[]{:T(128)} %bitcast.7, pred[512]{0:T(512)(128)(4,1)S(1)} %compare_and_fusion, ...), kind=kLoop, calls=%fused_computation.208 | loop fusion | flops 106496 | bytes 123420 | tf_op jit(solution)/shard_map/div | solution.py:133
  16.0 5.7 %select_add_fusion.2 = (f32[16,512]{1,0:T(8,128)S(1)}, f32[16,512]{1,0:T(8,128)S(1)}, f32[16,512]{1,0:T(8,128)S(1)}) fusion(pred[16,512]{1,0:T(8,128)(4,1)S(1)} %get-tuple-element.20, pred[16,512]{1,0:T(8,128)(4,1)S(1)} %get-tuple-element.19, pred[16,512]{1,0:T(8,128)(4,1)S(1)} %get-tuple-element.18, f32[]{:T(128)} %bitcast.30, f32[]{:T(128)} %bitcast.29, ...), kind=kLoop, calls=%fused_computation.212 | loop fusion | flops 122880 | bytes 122916 | tf_op jit(solution)/shard_map/add | solution.py:129
  22.6 5.6 %collective-permute-start.2 = (f32[2,2,1024]{2,0,1:T(2,128)S(1)}, f32[2,2,1024]{2,0,1:T(2,128)S(1)}, u32[]{:S(2)}, u32[]{:S(2)}) collective-permute-start(f32[2,2,1024]{2,0,1:T(2,128)S(1)} %reshape.297), channel_id=1, source_target_pairs={{0,1},{1,2},{2,3},{4,5},{5,6},{6,7},{8,9},{9,10},{10,11},{12,13},{... | collective-permute-start | bytes 49160 | tf_op jit(solution)/shard_map/ppermute | solution.py:18
  28.2 4.5 %collective-permute-start.3 = (f32[2,2,1,512]{3,2,0,1:T(1,128)S(1)}, f32[2,2,1,512]{3,2,0,1:T(1,128)S(1)}, u32[]{:S(2)}, u32[]{:S(2)}) collective-permute-start(f32[2,2,1,512]{3,2,0,1:T(1,128)S(1)} %slice.802), channel_id=1, source_target_pairs={{0,4},{1,5},{2,6},{3,7},{8,12},{9,13},{10,14},{11,15},{16,20},{17,... | collective-permute-start | bytes 24584 | tf_op jit(solution)/shard_map/ppermute | solution.py:18
  32.8 1.3 %collective-permute-done.3 = f32[2,2,1,512]{3,2,0,1:T(1,128)S(1)} collective-permute-done((f32[2,2,1,512]{3,2,0,1:T(1,128)S(1)}, f32[2,2,1,512]{3,2,0,1:T(1,128)S(1)}, u32[]{:S(2)}, u32[]{:S(2)}) %collective-permute-start.3) | collective-permute-done | bytes 8224 | tf_op jit(solution)/shard_map/ppermute | solution.py:18
  34.7 1.3 %collective-permute-start.5 = (f32[2,2,1,512]{3,1,2,0:T(2,128)S(1)}, f32[2,2,1,512]{3,1,2,0:T(2,128)S(1)}, u32[]{:S(2)}, u32[]{:S(2)}) collective-permute-start(f32[2,2,1,512]{3,1,2,0:T(2,128)S(1)} %copy.139), channel_id=1, source_target_pairs={{4,0},{5,1},{6,2},{7,3},{12,8},{13,9},{14,10},{15,11},{20,16},{21,... | collective-permute-start | bytes 24584 | tf_op jit(solution)/shard_map/ppermute | solution.py:18
  36.3 1.3 %collective-permute-start.4 = (f32[2,2,1024]{2,0,1:T(2,128)S(1)}, f32[2,2,1024]{2,0,1:T(2,128)S(1)}, u32[]{:S(2)}, u32[]{:S(2)}) collective-permute-start(f32[2,2,1024]{2,0,1:T(2,128)S(1)} %copy.82), channel_id=1, source_target_pairs={{1,0},{2,1},{3,2},{5,4},{6,5},{7,6},{9,8},{10,9},{11,10},{13,12},{... | collective-permute-start | bytes 49160 | tf_op jit(solution)/shard_map/ppermute | solution.py:18
  37.6 2.6 %collective-permute-done.5 = f32[2,2,1,512]{3,1,2,0:T(2,128)S(1)} collective-permute-done((f32[2,2,1,512]{3,1,2,0:T(2,128)S(1)}, f32[2,2,1,512]{3,1,2,0:T(2,128)S(1)}, u32[]{:S(2)}, u32[]{:S(2)}) %collective-permute-start.5) | collective-permute-done | bytes 8224 | tf_op jit(solution)/shard_map/ppermute | solution.py:18
  40.2 1.7 %collective-permute-done.4 = f32[2,2,1024]{2,0,1:T(2,128)S(1)} collective-permute-done((f32[2,2,1024]{2,0,1:T(2,128)S(1)}, f32[2,2,1024]{2,0,1:T(2,128)S(1)}, u32[]{:S(2)}, u32[]{:S(2)}) %collective-permute-start.4) | collective-permute-done | bytes 16416 | tf_op jit(solution)/shard_map/ppermute | solution.py:18
  42.5 3.9 %collective-permute-start.6 = (f32[2,2,1024]{2,0,1:T(2,128)S(1)}, f32[2,2,1024]{2,0,1:T(2,128)S(1)}, u32[]{:S(2)}, u32[]{:S(2)}) collective-permute-start(f32[2,2,1024]{2,0,1:T(2,128)S(1)} %reshape.301), channel_id=1, source_target_pairs={{0,1},{1,2},{2,3},{4,5},{5,6},{6,7},{8,9},{9,10},{10,11},{12,13},{... | collective-permute-start | bytes 49160 | tf_op jit(solution)/shard_map/ppermute | solution.py:18
  46.4 4.5 %collective-permute-start.7 = (f32[2,2,1,512]{3,2,0,1:T(1,128)S(1)}, f32[2,2,1,512]{3,2,0,1:T(1,128)S(1)}, u32[]{:S(2)}, u32[]{:S(2)}) collective-permute-start(f32[2,2,1,512]{3,2,0,1:T(1,128)S(1)} %slice.832), channel_id=1, source_target_pairs={{0,4},{1,5},{2,6},{3,7},{8,12},{9,13},{10,14},{11,15},{16,20},{17,... | collective-permute-start | bytes 24584 | tf_op jit(solution)/shard_map/ppermute | solution.py:18
  51.0 1.3 %collective-permute-done.7 = f32[2,2,1,512]{3,2,0,1:T(1,128)S(1)} collective-permute-done((f32[2,2,1,512]{3,2,0,1:T(1,128)S(1)}, f32[2,2,1,512]{3,2,0,1:T(1,128)S(1)}, u32[]{:S(2)}, u32[]{:S(2)}) %collective-permute-start.7) | collective-permute-done | bytes 8224 | tf_op jit(solution)/shard_map/ppermute | solution.py:18
  54.7 1.3 %collective-permute-start.8 = (f32[2,2,1024]{2,0,1:T(2,128)S(1)}, f32[2,2,1024]{2,0,1:T(2,128)S(1)}, u32[]{:S(2)}, u32[]{:S(2)}) collective-permute-start(f32[2,2,1024]{2,0,1:T(2,128)S(1)} %copy.95), channel_id=1, source_target_pairs={{1,0},{2,1},{3,2},{5,4},{6,5},{7,6},{9,8},{10,9},{11,10},{13,12},{... | collective-permute-start | bytes 49160 | tf_op jit(solution)/shard_map/ppermute | solution.py:18
  56.0 2.6 %collective-permute-done.9 = f32[2,2,1,512]{3,2,0,1:T(1,128)S(1)} collective-permute-done((f32[2,2,1,512]{3,2,0,1:T(1,128)S(1)}, f32[2,2,1,512]{3,2,0,1:T(1,128)S(1)}, u32[]{:S(2)}, u32[]{:S(2)}) %collective-permute-start.9) | collective-permute-done | bytes 8224 | tf_op jit(solution)/shard_map/ppermute | solution.py:18
  58.5 1.8 %collective-permute-done.8 = f32[2,2,1024]{2,0,1:T(2,128)S(1)} collective-permute-done((f32[2,2,1024]{2,0,1:T(2,128)S(1)}, f32[2,2,1024]{2,0,1:T(2,128)S(1)}, u32[]{:S(2)}, u32[]{:S(2)}) %collective-permute-start.8) | collective-permute-done | bytes 16416 | tf_op jit(solution)/shard_map/ppermute | solution.py:18
  60.9 3.5 %collective-permute-start.10 = (f32[2,2,1024]{2,0,1:T(2,128)S(1)}, f32[2,2,1024]{2,0,1:T(2,128)S(1)}, u32[]{:S(2)}, u32[]{:S(2)}) collective-permute-start(f32[2,2,1024]{2,0,1:T(2,128)S(1)} %reshape.305), channel_id=1, source_target_pairs={{0,1},{1,2},{2,3},{4,5},{5,6},{6,7},{8,9},{9,10},{10,11},{12,13},{... | collective-permute-start | bytes 49160 | tf_op jit(solution)/shard_map/ppermute | solution.py:18
  64.4 4.5 %collective-permute-start.11 = (f32[2,2,1,512]{3,2,0,1:T(1,128)S(1)}, f32[2,2,1,512]{3,2,0,1:T(1,128)S(1)}, u32[]{:S(2)}, u32[]{:S(2)}) collective-permute-start(f32[2,2,1,512]{3,2,0,1:T(1,128)S(1)} %slice.860), channel_id=1, source_target_pairs={{0,4},{1,5},{2,6},{3,7},{8,12},{9,13},{10,14},{11,15},{16,20},{17,... | collective-permute-start | bytes 24584 | tf_op jit(solution)/shard_map/ppermute | solution.py:18
  69.0 1.3 %collective-permute-done.11 = f32[2,2,1,512]{3,2,0,1:T(1,128)S(1)} collective-permute-done((f32[2,2,1,512]{3,2,0,1:T(1,128)S(1)}, f32[2,2,1,512]{3,2,0,1:T(1,128)S(1)}, u32[]{:S(2)}, u32[]{:S(2)}) %collective-permute-start.11) | collective-permute-done | bytes 8224 | tf_op jit(solution)/shard_map/ppermute | solution.py:18
  70.9 1.3 %collective-permute-start.13 = (f32[2,2,1,512]{3,1,2,0:T(2,128)S(1)}, f32[2,2,1,512]{3,1,2,0:T(2,128)S(1)}, u32[]{:S(2)}, u32[]{:S(2)}) collective-permute-start(f32[2,2,1,512]{3,1,2,0:T(2,128)S(1)} %copy.143), channel_id=1, source_target_pairs={{4,0},{5,1},{6,2},{7,3},{12,8},{13,9},{14,10},{15,11},{20,16},{21,... | collective-permute-start | bytes 24584 | tf_op jit(solution)/shard_map/ppermute | solution.py:18
  74.0 2.5 %collective-permute-done.13 = f32[2,2,1,512]{3,1,2,0:T(2,128)S(1)} collective-permute-done((f32[2,2,1,512]{3,1,2,0:T(2,128)S(1)}, f32[2,2,1,512]{3,1,2,0:T(2,128)S(1)}, u32[]{:S(2)}, u32[]{:S(2)}) %collective-permute-start.13) | collective-permute-done | bytes 8224 | tf_op jit(solution)/shard_map/ppermute | solution.py:18
  76.4 1.9 %collective-permute-done.12 = f32[2,2,1024]{2,0,1:T(2,128)S(1)} collective-permute-done((f32[2,2,1024]{2,0,1:T(2,128)S(1)}, f32[2,2,1024]{2,0,1:T(2,128)S(1)}, u32[]{:S(2)}, u32[]{:S(2)}) %collective-permute-start.12) | collective-permute-done | bytes 16416 | tf_op jit(solution)/shard_map/ppermute | solution.py:18
  79.5 1.9 %collective-permute-start.14 = (f32[2,2,1024]{2,0,1:T(2,128)S(1)}, f32[2,2,1024]{2,0,1:T(2,128)S(1)}, u32[]{:S(2)}, u32[]{:S(2)}) collective-permute-start(f32[2,2,1024]{2,0,1:T(2,128)S(1)} %reshape.309), channel_id=1, source_target_pairs={{0,1},{1,2},{2,3},{4,5},{5,6},{6,7},{8,9},{9,10},{10,11},{12,13},{... | collective-permute-start | bytes 49160 | tf_op jit(solution)/shard_map/ppermute | solution.py:18
  81.4 4.5 %collective-permute-start.15 = (f32[2,2,1,512]{3,2,0,1:T(1,128)S(1)}, f32[2,2,1,512]{3,2,0,1:T(1,128)S(1)}, u32[]{:S(2)}, u32[]{:S(2)}) collective-permute-start(f32[2,2,1,512]{3,2,0,1:T(1,128)S(1)} %slice.888), channel_id=1, source_target_pairs={{0,4},{1,5},{2,6},{3,7},{8,12},{9,13},{10,14},{11,15},{16,20},{17,... | collective-permute-start | bytes 24584 | tf_op jit(solution)/shard_map/ppermute | solution.py:18
  86.0 1.3 %collective-permute-done.15 = f32[2,2,1,512]{3,2,0,1:T(1,128)S(1)} collective-permute-done((f32[2,2,1,512]{3,2,0,1:T(1,128)S(1)}, f32[2,2,1,512]{3,2,0,1:T(1,128)S(1)}, u32[]{:S(2)}, u32[]{:S(2)}) %collective-permute-start.15) | collective-permute-done | bytes 8224 | tf_op jit(solution)/shard_map/ppermute | solution.py:18
  97.2 3.0 %collective-permute-done.16 = f32[2,2,1024]{2,0,1:T(2,128)S(1)} collective-permute-done((f32[2,2,1024]{2,0,1:T(2,128)S(1)}, f32[2,2,1024]{2,0,1:T(2,128)S(1)}, u32[]{:S(2)}, u32[]{:S(2)}) %collective-permute-start.16) | collective-permute-done | bytes 16416 | tf_op jit(solution)/shard_map/ppermute | solution.py:18
  104.1 1.9 %collective-permute-start.18 = (f32[2,2,1024]{2,0,1:T(2,128)S(1)}, f32[2,2,1024]{2,0,1:T(2,128)S(1)}, u32[]{:S(2)}, u32[]{:S(2)}) collective-permute-start(f32[2,2,1024]{2,0,1:T(2,128)S(1)} %copy.127), channel_id=1, source_target_pairs={{0,1},{1,2},{2,3},{4,5},{5,6},{6,7},{8,9},{9,10},{10,11},{12,13},{... | collective-permute-start | bytes 49160 | tf_op jit(solution)/shard_map/ppermute | solution.py:18
  106.0 5.1 %collective-permute-start.19 = (f32[2,2,1,512]{3,2,1,0:T(1,128)S(1)}, f32[2,2,1,512]{3,2,1,0:T(1,128)S(1)}, u32[]{:S(2)}, u32[]{:S(2)}) collective-permute-start(f32[2,2,1,512]{3,2,1,0:T(1,128)S(1)} %slice.916), channel_id=1, source_target_pairs={{0,4},{1,5},{2,6},{3,7},{8,12},{9,13},{10,14},{11,15},{16,20},{17,... | collective-permute-start | bytes 24584 | tf_op jit(solution)/shard_map/ppermute | solution.py:18
  111.2 1.3 %collective-permute-done.19 = f32[2,2,1,512]{3,2,1,0:T(1,128)S(1)} collective-permute-done((f32[2,2,1,512]{3,2,1,0:T(1,128)S(1)}, f32[2,2,1,512]{3,2,1,0:T(1,128)S(1)}, u32[]{:S(2)}, u32[]{:S(2)}) %collective-permute-start.19) | collective-permute-done | bytes 8224 | tf_op jit(solution)/shard_map/ppermute | solution.py:18
  115.0 10.3 %psum.7 = f32[16,512]{1,0:T(8,128)S(1)} all-reduce(f32[16,512]{1,0:T(8,128)S(1)} %add_add_fusion), channel_id=1, replica_groups=mesh['wave'=4,'tx'=2,'ty'=4] {'wave'}, use_global_device_ids=true, to_apply=%region_5.6 | all-reduce | flops 8192 | bytes 65536 | tf_op jit(solution)/shard_map/psum | solution.py:222
  (236 shorter events, 33.4 us)
Async XLA Ops:
  2.0 20.0 %collective-permute-start = (f32[2,2,1024]{2,0,1:T(2,128)S(1)}, f32[2,2,1024]{2,0,1:T(2,128)S(1)}, u32[]{:S(2)}, u32[]{:S(2)}) collective-permute-start(f32[2,2,1024]{2,0,1:T(2,128)S(1)} %reshape.295), channel_id=1, source_target_pairs={{1,0},{2,1},{3,2},{5,4},{6,5},{7,6},{9,8},{10,9},{11,10},{13,12},{... | collective-permute-start | bytes 49160 | tf_op jit(solution)/shard_map/ppermute | solution.py:18
  3.3 1.3 %copy-start.11 = (f32[3,4]{1,0:T(4,128)S(1)}, f32[3,4]{1,0:T(4,128)}, u32[]{:S(2)}) copy-start(f32[3,4]{1,0:T(4,128)} %param.13) | copy-start | bytes 148
  3.3 18.6 %collective-permute-start.1 = (f32[2,2,1,512]{3,2,0,1:T(1,128)S(1)}, f32[2,2,1,512]{3,2,0,1:T(1,128)S(1)}, u32[]{:S(2)}, u32[]{:S(2)}) collective-permute-start(f32[2,2,1,512]{3,2,0,1:T(1,128)S(1)} %slice.789), channel_id=1, source_target_pairs={{4,0},{5,1},{6,2},{7,3},{12,8},{13,9},{14,10},{15,11},{20,16},{21,... | collective-permute-start | bytes 24584 | tf_op jit(solution)/shard_map/ppermute | solution.py:18
  7.2 71.2 %copy-start.16 = (pred[512]{0:T(512)(128)(4,1)}, pred[512]{0:T(512)(128)(4,1)S(1)}, u32[]{:S(2)}) copy-start(pred[512]{0:T(512)(128)(4,1)S(1)} %broadcast_compare_fusion.3) | copy-start | bytes 1540
  7.3 2.8 %copy-start.25 = (s32[2]{0:T(128)S(1)}, s32[2]{0:T(128)}, u32[]{:S(2)}) copy-start(s32[2]{0:T(128)} %param.14) | copy-start | bytes 28
  7.9 5.3 %copy-start.9 = (f32[16,512]{1,0:T(8,128)S(1)}, f32[16,512]{1,0:T(8,128)}, u32[]{:S(2)}) copy-start(f32[16,512]{1,0:T(8,128)} %param.12) | copy-start | bytes 98308
  7.9 5.3 %copy-start.10 = (s32[16,512]{1,0:T(8,128)S(1)}, s32[16,512]{1,0:T(8,128)}, u32[]{:S(2)}) copy-start(s32[16,512]{1,0:T(8,128)} %param.11) | copy-start | bytes 98308
  9.4 3.2 %copy-start.21 = (pred[16]{0:T(512)(128)(4,1)}, pred[16]{0:T(512)(128)(4,1)S(1)}, u32[]{:S(2)}) copy-start(pred[16]{0:T(512)(128)(4,1)S(1)} %compare_and_fusion.1) | copy-start | bytes 52
  10.1 78.2 %copy-start.7 = (f32[2,16]{1,0:T(2,128)}, f32[2,16]{1,0:T(2,128)S(1)}, u32[]{:S(2)}) copy-start(f32[2,16]{1,0:T(2,128)S(1)} %compare_convert_fusion) | copy-start | bytes 388
  21.7 48.8 %copy-start.18 = (pred[512]{0:T(512)(128)(4,1)}, pred[512]{0:T(512)(128)(4,1)S(1)}, u32[]{:S(2)}) copy-start(pred[512]{0:T(512)(128)(4,1)S(1)} %broadcast_compare_fusion.4) | copy-start | bytes 1540
  22.6 11.5 %collective-permute-start.2 = (f32[2,2,1024]{2,0,1:T(2,128)S(1)}, f32[2,2,1024]{2,0,1:T(2,128)S(1)}, u32[]{:S(2)}, u32[]{:S(2)}) collective-permute-start(f32[2,2,1024]{2,0,1:T(2,128)S(1)} %reshape.297), channel_id=1, source_target_pairs={{0,1},{1,2},{2,3},{4,5},{5,6},{6,7},{8,9},{9,10},{10,11},{12,13},{... | collective-permute-start | bytes 49160 | tf_op jit(solution)/shard_map/ppermute | solution.py:18
  28.2 5.9 %collective-permute-start.3 = (f32[2,2,1,512]{3,2,0,1:T(1,128)S(1)}, f32[2,2,1,512]{3,2,0,1:T(1,128)S(1)}, u32[]{:S(2)}, u32[]{:S(2)}) collective-permute-start(f32[2,2,1,512]{3,2,0,1:T(1,128)S(1)} %slice.802), channel_id=1, source_target_pairs={{0,4},{1,5},{2,6},{3,7},{8,12},{9,13},{10,14},{11,15},{16,20},{17,... | collective-permute-start | bytes 24584 | tf_op jit(solution)/shard_map/ppermute | solution.py:18
  34.7 5.5 %collective-permute-start.5 = (f32[2,2,1,512]{3,1,2,0:T(2,128)S(1)}, f32[2,2,1,512]{3,1,2,0:T(2,128)S(1)}, u32[]{:S(2)}, u32[]{:S(2)}) collective-permute-start(f32[2,2,1,512]{3,1,2,0:T(2,128)S(1)} %copy.139), channel_id=1, source_target_pairs={{4,0},{5,1},{6,2},{7,3},{12,8},{13,9},{14,10},{15,11},{20,16},{21,... | collective-permute-start | bytes 24584 | tf_op jit(solution)/shard_map/ppermute | solution.py:18
  36.3 5.6 %collective-permute-start.4 = (f32[2,2,1024]{2,0,1:T(2,128)S(1)}, f32[2,2,1024]{2,0,1:T(2,128)S(1)}, u32[]{:S(2)}, u32[]{:S(2)}) collective-permute-start(f32[2,2,1024]{2,0,1:T(2,128)S(1)} %copy.82), channel_id=1, source_target_pairs={{1,0},{2,1},{3,2},{5,4},{6,5},{7,6},{9,8},{10,9},{11,10},{13,12},{... | collective-permute-start | bytes 49160 | tf_op jit(solution)/shard_map/ppermute | solution.py:18
  42.5 9.8 %collective-permute-start.6 = (f32[2,2,1024]{2,0,1:T(2,128)S(1)}, f32[2,2,1024]{2,0,1:T(2,128)S(1)}, u32[]{:S(2)}, u32[]{:S(2)}) collective-permute-start(f32[2,2,1024]{2,0,1:T(2,128)S(1)} %reshape.301), channel_id=1, source_target_pairs={{0,1},{1,2},{2,3},{4,5},{5,6},{6,7},{8,9},{9,10},{10,11},{12,13},{... | collective-permute-start | bytes 49160 | tf_op jit(solution)/shard_map/ppermute | solution.py:18
  46.4 5.9 %collective-permute-start.7 = (f32[2,2,1,512]{3,2,0,1:T(1,128)S(1)}, f32[2,2,1,512]{3,2,0,1:T(1,128)S(1)}, u32[]{:S(2)}, u32[]{:S(2)}) collective-permute-start(f32[2,2,1,512]{3,2,0,1:T(1,128)S(1)} %slice.832), channel_id=1, source_target_pairs={{0,4},{1,5},{2,6},{3,7},{8,12},{9,13},{10,14},{11,15},{16,20},{17,... | collective-permute-start | bytes 24584 | tf_op jit(solution)/shard_map/ppermute | solution.py:18
  53.0 5.5 %collective-permute-start.9 = (f32[2,2,1,512]{3,2,0,1:T(1,128)S(1)}, f32[2,2,1,512]{3,2,0,1:T(1,128)S(1)}, u32[]{:S(2)}, u32[]{:S(2)}) collective-permute-start(f32[2,2,1,512]{3,2,0,1:T(1,128)S(1)} %slice.847), channel_id=1, source_target_pairs={{4,0},{5,1},{6,2},{7,3},{12,8},{13,9},{14,10},{15,11},{20,16},{21,... | collective-permute-start | bytes 24584 | tf_op jit(solution)/shard_map/ppermute | solution.py:18
  54.7 5.6 %collective-permute-start.8 = (f32[2,2,1024]{2,0,1:T(2,128)S(1)}, f32[2,2,1024]{2,0,1:T(2,128)S(1)}, u32[]{:S(2)}, u32[]{:S(2)}) collective-permute-start(f32[2,2,1024]{2,0,1:T(2,128)S(1)} %copy.95), channel_id=1, source_target_pairs={{1,0},{2,1},{3,2},{5,4},{6,5},{7,6},{9,8},{10,9},{11,10},{13,12},{... | collective-permute-start | bytes 49160 | tf_op jit(solution)/shard_map/ppermute | solution.py:18
  60.9 9.4 %collective-permute-start.10 = (f32[2,2,1024]{2,0,1:T(2,128)S(1)}, f32[2,2,1024]{2,0,1:T(2,128)S(1)}, u32[]{:S(2)}, u32[]{:S(2)}) collective-permute-start(f32[2,2,1024]{2,0,1:T(2,128)S(1)} %reshape.305), channel_id=1, source_target_pairs={{0,1},{1,2},{2,3},{4,5},{5,6},{6,7},{8,9},{9,10},{10,11},{12,13},{... | collective-permute-start | bytes 49160 | tf_op jit(solution)/shard_map/ppermute | solution.py:18
  64.4 5.9 %collective-permute-start.11 = (f32[2,2,1,512]{3,2,0,1:T(1,128)S(1)}, f32[2,2,1,512]{3,2,0,1:T(1,128)S(1)}, u32[]{:S(2)}, u32[]{:S(2)}) collective-permute-start(f32[2,2,1,512]{3,2,0,1:T(1,128)S(1)} %slice.860), channel_id=1, source_target_pairs={{0,4},{1,5},{2,6},{3,7},{8,12},{9,13},{10,14},{11,15},{16,20},{17,... | collective-permute-start | bytes 24584 | tf_op jit(solution)/shard_map/ppermute | solution.py:18
  70.9 5.5 %collective-permute-start.13 = (f32[2,2,1,512]{3,1,2,0:T(2,128)S(1)}, f32[2,2,1,512]{3,1,2,0:T(2,128)S(1)}, u32[]{:S(2)}, u32[]{:S(2)}) collective-permute-start(f32[2,2,1,512]{3,1,2,0:T(2,128)S(1)} %copy.143), channel_id=1, source_target_pairs={{4,0},{5,1},{6,2},{7,3},{12,8},{13,9},{14,10},{15,11},{20,16},{21,... | collective-permute-start | bytes 24584 | tf_op jit(solution)/shard_map/ppermute | solution.py:18
  72.7 5.6 %collective-permute-start.12 = (f32[2,2,1024]{2,0,1:T(2,128)S(1)}, f32[2,2,1024]{2,0,1:T(2,128)S(1)}, u32[]{:S(2)}, u32[]{:S(2)}) collective-permute-start(f32[2,2,1024]{2,0,1:T(2,128)S(1)} %copy.107), channel_id=1, source_target_pairs={{1,0},{2,1},{3,2},{5,4},{6,5},{7,6},{9,8},{10,9},{11,10},{13,12},{... | collective-permute-start | bytes 49160 | tf_op jit(solution)/shard_map/ppermute | solution.py:18
  79.5 7.8 %collective-permute-start.14 = (f32[2,2,1024]{2,0,1:T(2,128)S(1)}, f32[2,2,1024]{2,0,1:T(2,128)S(1)}, u32[]{:S(2)}, u32[]{:S(2)}) collective-permute-start(f32[2,2,1024]{2,0,1:T(2,128)S(1)} %reshape.309), channel_id=1, source_target_pairs={{0,1},{1,2},{2,3},{4,5},{5,6},{6,7},{8,9},{9,10},{10,11},{12,13},{... | collective-permute-start | bytes 49160 | tf_op jit(solution)/shard_map/ppermute | solution.py:18
  81.4 5.9 %collective-permute-start.15 = (f32[2,2,1,512]{3,2,0,1:T(1,128)S(1)}, f32[2,2,1,512]{3,2,0,1:T(1,128)S(1)}, u32[]{:S(2)}, u32[]{:S(2)}) collective-permute-start(f32[2,2,1,512]{3,2,0,1:T(1,128)S(1)} %slice.888), channel_id=1, source_target_pairs={{0,4},{1,5},{2,6},{3,7},{8,12},{9,13},{10,14},{11,15},{16,20},{17,... | collective-permute-start | bytes 24584 | tf_op jit(solution)/shard_map/ppermute | solution.py:18
  89.8 6.1 %collective-permute-start.17 = (f32[2,2,1,512]{3,2,0,1:T(1,128)}, f32[2,2,1,512]{3,2,0,1:T(1,128)}, u32[]{:S(2)}, u32[]{:S(2)}) collective-permute-start(f32[2,2,1,512]{3,2,0,1:T(1,128)} %slice.903), channel_id=1, source_target_pairs={{4,0},{5,1},{6,2},{7,3},{12,8},{13,9},{14,10},{15,11},{20,16},{21,... | collective-permute-start | bytes 24584 | tf_op jit(solution)/shard_map/ppermute | solution.py:18
  94.6 5.6 %collective-permute-start.16 = (f32[2,2,1024]{2,0,1:T(2,128)S(1)}, f32[2,2,1024]{2,0,1:T(2,128)S(1)}, u32[]{:S(2)}, u32[]{:S(2)}) collective-permute-start(f32[2,2,1024]{2,0,1:T(2,128)S(1)} %copy.120), channel_id=1, source_target_pairs={{1,0},{2,1},{3,2},{5,4},{6,5},{7,6},{9,8},{10,9},{11,10},{13,12},{... | collective-permute-start | bytes 49160 | tf_op jit(solution)/shard_map/ppermute | solution.py:18
  102.0 0.9 copy-start.6
  102.9 0.9 copy-start.4
  104.1 8.4 %collective-permute-start.18 = (f32[2,2,1024]{2,0,1:T(2,128)S(1)}, f32[2,2,1024]{2,0,1:T(2,128)S(1)}, u32[]{:S(2)}, u32[]{:S(2)}) collective-permute-start(f32[2,2,1024]{2,0,1:T(2,128)S(1)} %copy.127), channel_id=1, source_target_pairs={{0,1},{1,2},{2,3},{4,5},{5,6},{6,7},{8,9},{9,10},{10,11},{12,13},{... | collective-permute-start | bytes 49160 | tf_op jit(solution)/shard_map/ppermute | solution.py:18
  106.0 6.5 %collective-permute-start.19 = (f32[2,2,1,512]{3,2,1,0:T(1,128)S(1)}, f32[2,2,1,512]{3,2,1,0:T(1,128)S(1)}, u32[]{:S(2)}, u32[]{:S(2)}) collective-permute-start(f32[2,2,1,512]{3,2,1,0:T(1,128)S(1)} %slice.916), channel_id=1, source_target_pairs={{0,4},{1,5},{2,6},{3,7},{8,12},{9,13},{10,14},{11,15},{16,20},{17,... | collective-permute-start | bytes 24584 | tf_op jit(solution)/shard_map/ppermute | solution.py:18
  115.0 10.3 %copy-start.22 = (pred[16]{0:T(512)(128)(4,1)S(1)}, pred[16]{0:T(512)(128)(4,1)}, u32[]{:S(2)}) copy-start(pred[16]{0:T(512)(128)(4,1)} %copy-done.21) | copy-start | bytes 52
  115.0 10.3 %copy-start.24 = (pred[512]{0:T(512)(128)(4,1)S(1)}, pred[512]{0:T(512)(128)(4,1)}, u32[]{:S(2)}) copy-start(pred[512]{0:T(512)(128)(4,1)} %copy-done.23) | copy-start | bytes 1540
  (14 other events, 9.7 us)
where the time goes:
time: 127 us; the launch traced here: 126 us
  starting transfers between devices  53 us (42%)
  waiting for transfers between devices  22.7 us (18%)
  local copies, waits for them, and re-layouts  21.2 us (17%)
  other arithmetic  17.2 us (14%)
  blocking collectives  10.3 us (8%)
  between operations  1.69 us (1%)
    ppermute x20, starting transfers between devices, shifted_2(): lax.ppermute(value, axis, [(source, source + steps) for source in range(i...  53 us
    ppermute x20, waiting for transfers between devices, shifted_2(): lax.ppermute(value, axis, [(source, source + steps) for source in range(i...  22.7 us
    psum x1, blocking collectives, on_device(): collected = lax.psum(partial_value, 'wave')  10.3 us
    unnamed x55, local copies, waits for them, and re-layouts  8.55 us
    add x1, other arithmetic, coefficients(): decay_map = decay_map + chosen * decay[material_id]  5.68 us
  transfers between devices with their start and end apart: 20, of which 12 were waited for; matrix products, arithmetic and copies ran while one was open for 17% of the time, Pallas kernels for 0%

commit v1 on v0

v1 whole, which is shorter than its diff:
```python
import functools

import jax
import jax.numpy as jnp
from jax import lax
from jax.experimental import pallas as pl
from jax.experimental.pallas import tpu as pltpu
from jax.sharding import PartitionSpec as P

NZ = 64
STEPS = 5
NMAT = 3
LANES = 2 * NZ
ROWS = 16
LINES = 8
PAD = 8
EXT_ROWS = ROWS + 2 * PAD
EXT_LINES = LINES + 2 * STEPS
FIELDS = 13

time_step = 0.5
contrast = 2.0

LINE_DEPTH = (5, 5, 5, 5, 4, 5, 3, 3, 3, 4, 4, 4, 4)
ROW_DEPTH = (5, 5, 5, 4, 5, 5, 3, 3, 3, 4, 4, 4, 4)

Y_ENTRIES = [(f, k) for f in range(FIELDS) for k in range(LINE_DEPTH[f])]


def x_entries():
    start, out = 0, []
    for f in range(FIELDS):
        for line in range(LINES):
            out.append((f, line, ROW_DEPTH[f], start))
            start += ROW_DEPTH[f]
    return out, start


def corner_entries():
    start, out = 0, []
    for f in range(FIELDS):
        for k in range(LINE_DEPTH[f]):
            out.append((f, k, ROW_DEPTH[f], start))
            start += ROW_DEPTH[f]
    return out, start


X_ENTRIES, X_ROWS = x_entries()
C_ENTRIES, C_ROWS = corner_entries()


def round_up(n, m):
    return (n + m - 1) // m * m


def low_lanes(shape):
    return lax.broadcasted_iota(jnp.int32, shape, len(shape) - 1) < NZ


def half_turn(v):
    return pltpu.roll(v, NZ, v.ndim - 1)


def choose(material, table, column):
    values = [column(m) for m in range(NMAT)]
    return jnp.where(material < 0.5, values[0], jnp.where(material < 1.5, values[1], values[2]))


def pole(table):
    def denom(m):
        return 1.0 + 0.25 * table[m, 3]

    def decay(m):
        return (1.0 - 0.25 * table[m, 3]) / denom(m)

    def drive(m):
        return table[m, 2] * table[m, 2] * time_step / denom(m)

    def coupled(m):
        return drive(m) * table[m, 1]

    return decay, drive, coupled


def pack_kernel(parity, table, fields, material, density, tile, y_a, y_b, *rest):
    x_msgs, corner_msgs = rest
    decay, drive, coupled = pole(table)
    low = low_lanes((ROWS, LANES))
    for k in range(LINES // 2):
        at = slice(k * LANES, (k + 1) * LANES)

        def split(one, two):
            return jnp.where(low, one, half_turn(two)), jnp.where(low, half_turn(one), two)

        pairs = [split(fields[0, 0, f, :, at], fields[0, 1, f, :, at]) for f in range(12)]
        mat, dens = material[:, at].astype(jnp.float32), density[:, at]
        turned = half_turn(mat)
        mats = (jnp.where(low, mat, turned), jnp.where(low, turned, mat))
        mixed = split(mat, dens)
        for half in range(2):
            line = 2 * k + half
            dec = choose(mats[half], table, decay)
            dri = choose(mats[half], table, drive)
            cou = choose(mats[half], table, coupled)
            for c in range(3):
                e, p, j = pairs[c][half], pairs[6 + c][half], pairs[9 + c][half]
                j = dec * j + cou * e - dri * p
                tile[c, line] = e
                tile[3 + c, line] = pairs[3 + c][half]
                tile[6 + c, line] = p + time_step * j
                tile[9 + c, line] = j
            tile[12, line] = mixed[half]
    odd_x, odd_y = parity[0], parity[1]
    for i, (f, k) in enumerate(Y_ENTRIES):
        first, last = k, LINES - 1 - k
        y_a[i] = tile[f, jnp.where(odd_y == 1, first, last)]
        y_b[i] = tile[f, jnp.where(odd_y == 1, last, first)]

    def pack_rows(msg, entries, rows_first, line_of):
        for f, k, depth, start in entries:
            line = line_of(k)
            if rows_first:
                msg[start : start + depth, :] = tile[f, line, 0:depth, :]
            else:
                msg[start : start + depth, :] = tile[f, line, ROWS - depth : ROWS, :]

    for x_type in range(len(x_msgs)):
        for first in (False, True):
            sends_last_if = x_type if not first else 1 - x_type

            @pl.when(odd_x == sends_last_if)
            def _(x_type=x_type, first=first):
                pack_rows(x_msgs[x_type], X_ENTRIES, first, lambda k: k)
                for y_type in range(2):
                    pack_rows(
                        corner_msgs[x_type][y_type],
                        C_ENTRIES,
                        first,
                        lambda k, y_type=y_type: jnp.where(odd_y == 1 - y_type, k, LINES - 1 - k),
                    )


def main_kernel(
    place,
    waveforms,
    table,
    plane,
    box,
    profiles,
    tile,
    y_a,
    y_b,
    x_msgs,
    corner_msgs,
    electric_out,
    gradient_out,
    E,
    H,
    Pol,
    J,
    C,
    coef,
):
    odd_x, odd_y = place[0] % 2, place[1] % 2
    rows_base, lines_base = place[0] * ROWS - PAD, place[1] * LINES - STEPS
    rows_all, lines_all = place[2], place[3]

    def put(f, line, rows, value):
        c = f % 3
        if f < 3:
            E[0, c, line, rows, :] = value
        elif f < 6:
            H[c, line, rows, :] = value
        elif f < 9:
            Pol[c, line, rows, :] = value
        elif f < 12:
            J[c, line, rows, :] = value
        else:
            C[line, rows, :] = value

    E[0] = jnp.zeros(E.shape[1:], jnp.float32)
    H[...] = jnp.zeros(H.shape, jnp.float32)
    Pol[...] = jnp.zeros(Pol.shape, jnp.float32)
    J[...] = jnp.zeros(J.shape, jnp.float32)
    C[...] = jnp.zeros(C.shape, jnp.float32)
    middle = slice(PAD, PAD + ROWS)
    for f in range(FIELDS):
        for line in range(LINES):
            put(f, STEPS + line, middle, tile[f, line])

    def line_at(ahead, k):
        return jnp.where(ahead, STEPS + LINES + k, STEPS - 1 - k)

    for i, (f, k) in enumerate(Y_ENTRIES):
        put(f, line_at(odd_y == 0, k), middle, y_a[i])
        put(f, line_at(odd_y == 1, k), middle, y_b[i])
    for x_type in range(len(x_msgs)):
        for ahead in (False, True):
            want = x_type if ahead else 1 - x_type

            @pl.when(odd_x == want)
            def _(x_type=x_type, ahead=ahead):
                def rows_of(depth):
                    return slice(PAD + ROWS, PAD + ROWS + depth) if ahead else slice(PAD - depth, PAD)

                for f, line, depth, start in X_ENTRIES:
                    put(f, STEPS + line, rows_of(depth), x_msgs[x_type][start : start + depth, :])
                for y_type in range(2):
                    for f, k, depth, start in C_ENTRIES:
                        put(
                            f,
                            line_at(odd_y == y_type, k),
                            rows_of(depth),
                            corner_msgs[x_type][y_type][start : start + depth, :],
                        )

    decay, drive, coupled = pole(table)
    shape = (EXT_ROWS, LANES)
    low = low_lanes(shape)
    lane = lax.broadcasted_iota(jnp.int32, shape, 1)
    depth_id = jnp.where(low, lane, lane - NZ)
    row = lax.broadcasted_iota(jnp.int32, shape, 0) + rows_base
    first_z, last_z = depth_id == 0, depth_id == NZ - 1
    row_inside = (row >= 0) & (row < rows_all)
    row_mask = row_inside.astype(jnp.float32)
    design_rows = (
        (row >= box[0]) & (row < box[1]) & (depth_id >= box[4]) & (depth_id < box[5])
    ).astype(jnp.float32)
    source_rows = (row == jnp.where(low, plane[0], plane[1])).astype(jnp.float32)

    def line_flags(line):
        where = lines_base + line
        grid = ((where >= 0) & (where < lines_all)).astype(jnp.float32)
        design = ((where >= box[2]) & (where < box[3])).astype(jnp.float32)
        return grid, design

    def set_coefficients(line, _):
        mixed = C[line]
        turned = half_turn(mixed)
        mat = jnp.where(low, mixed, turned)
        dens = jnp.where(low, turned, mixed)
        grid, design = line_flags(line)
        permittivity = choose(mat, table, lambda m: table[m, 0]) + (design_rows * design) * dens * contrast
        coef[0, line] = time_step / permittivity * (row_mask * grid)
        coef[1, line] = choose(mat, table, decay)
        coef[2, line] = choose(mat, table, drive)
        coef[3, line] = choose(mat, table, coupled)
        return _

    lax.fori_loop(1, EXT_LINES - 1, set_coefficients, 0)

    def ahead_row(v):
        return pltpu.roll(v, EXT_ROWS - 1, 0)

    def behind_row(v):
        return pltpu.roll(v, 1, 0)

    def ahead_depth(v):
        return jnp.where(last_z, 0.0, pltpu.roll(v, LANES - 1, 1))

    def behind_depth(v):
        return jnp.where(first_z, 0.0, pltpu.roll(v, 1, 1))

    def magnetic_line(n, line):
        ex, ey, ez = E[n, 0, line], E[n, 1, line], E[n, 2, line]
        ex_next, ez_next = E[n, 0, line + 1], E[n, 2, line + 1]
        half = time_step * (row_mask * line_flags(line)[0])
        hx = H[0, line] - half * ((ez_next - ez) - (ahead_depth(ey) - ey))
        hy = H[1, line] - half * ((ahead_depth(ex) - ex) - (ahead_row(ez) - ez))
        hz = H[2, line] - half * ((ahead_row(ey) - ey) - (ex_next - ex))
        H[0, line], H[1, line], H[2, line] = hx, hy, hz
        return (hx, hy, hz), (ex, ey, ez)

    for n in range(STEPS):
        magnetic_line(n, n)
        weight = [jnp.where(low[:1], waveforms[0, n], waveforms[1, n])]

        def advance(line, _, n=n, weight=weight[0]):
            (hx, hy, hz), e = magnetic_line(n, line)
            hx_last, hz_last = H[0, line - 1], H[2, line - 1]
            curls = (
                (hz - hz_last) - (hy - behind_depth(hy)),
                (hx - behind_depth(hx)) - (hz - behind_row(hz)),
                (hy - behind_row(hy)) - (hx - hx_last),
            )
            reach = coef[0, line]
            where = jnp.clip(lines_base + line, 0, lines_all - 1)
            for c in range(3):
                if n == 0:
                    j = J[c, line]
                else:
                    p = Pol[c, line]
                    j = coef[1, line] * J[c, line] + coef[3, line] * e[c] - coef[2, line] * p
                    if n < STEPS - 1:
                        J[c, line] = j
                        Pol[c, line] = p + time_step * j
                source = source_rows * (weight * profiles[c, pl.ds(where, 1), :])
                E[n + 1, c, line] = e[c] + reach * ((curls[c] - j) - source)
            return _

        lax.fori_loop(n + 1, EXT_LINES - 1 - n, advance, 0)

    for k in range(LINES // 2):
        at = slice(k * LANES, (k + 1) * LANES)
        low16 = low[:ROWS]
        sums = []
        for half in range(2):
            line = STEPS + 2 * k + half
            total = jnp.zeros((ROWS, LANES), jnp.float32)
            for c in range(3):
                history = [E[n, c, line, middle, :] for n in range(STEPS + 1)]
                for n in range(1, STEPS + 1):
                    total = total + half_turn(history[STEPS + 1 - n]) * (history[n] - history[n - 1])
            design = line_flags(line)[1]
            sums.append(total * (contrast * design_rows[PAD : PAD + ROWS] * design))
        gradient_out[:, at] = jnp.where(low16, sums[0], half_turn(sums[1]))
        for c in range(3):
            one = E[STEPS, c, STEPS + 2 * k, middle, :]
            two = E[STEPS, c, STEPS + 2 * k + 1, middle, :]
            electric_out[0, 0, c, :, at] = jnp.where(low16, one, half_turn(two))
            electric_out[0, 1, c, :, at] = jnp.where(low16, half_turn(one), two)


def pair_of(index, kind, count):
    if kind is None:
        return index
    other = index + 1 if index % 2 == kind else index - 1
    return other if 0 <= other < count else None


def on_device(counts, initial_fields, source_profiles, source_waveforms, material_map, design_density, material_table, plane_indices, design_box):
    tx_count, ty_count = counts
    axes = ("tx", "ty")

    def swap(value, x_kind, y_kind):
        pairs = []
        for x in range(tx_count):
            for y in range(ty_count):
                ox, oy = pair_of(x, x_kind, tx_count), pair_of(y, y_kind, ty_count)
                if ox is not None and oy is not None:
                    pairs.append((x * ty_count + y, ox * ty_count + oy))
        return lax.ppermute(value, axes, pairs)

    x_kinds = (0, 1) if tx_count > 2 else (0,)
    tile_x, tile_y = lax.axis_index("tx"), lax.axis_index("ty")
    parity = jnp.stack([tile_x % 2, tile_y % 2]).astype(jnp.int32)
    place = jnp.stack([tile_x, tile_y, tile_x * 0 + tx_count * ROWS, tile_x * 0 + ty_count * LINES]).astype(jnp.int32)
    smem = pl.BlockSpec(memory_space=pltpu.SMEM)
    vmem = pl.BlockSpec(memory_space=pltpu.VMEM)

    def f32(*shape):
        return jax.ShapeDtypeStruct(shape, jnp.float32)

    x_size, c_size = round_up(X_ROWS, 8), round_up(C_ROWS, 8)
    tile, y_a, y_b, x_msgs, corner_msgs = pl.pallas_call(
        pack_kernel,
        out_shape=(
            f32(FIELDS, LINES, ROWS, LANES),
            f32(len(Y_ENTRIES), ROWS, LANES),
            f32(len(Y_ENTRIES), ROWS, LANES),
            [f32(x_size, LANES) for _ in x_kinds],
            [[f32(c_size, LANES) for _ in range(2)] for _ in x_kinds],
        ),
        in_specs=[smem, smem, vmem, vmem, vmem],
        out_specs=(
            vmem,
            vmem,
            vmem,
            [vmem for _ in x_kinds],
            [[vmem for _ in range(2)] for _ in x_kinds],
        ),
        compiler_params=pltpu.CompilerParams(vmem_limit_bytes=32 * 1024 * 1024),
        name="pack",
    )(parity, material_table, initial_fields, material_map, design_density)
    y_a, y_b = swap(y_a, None, 0), swap(y_b, None, 1)
    x_msgs = [swap(m, kind, None) for m, kind in zip(x_msgs, x_kinds)]
    corner_msgs = [[swap(m[y_kind], kind, y_kind) for y_kind in range(2)] for m, kind in zip(corner_msgs, x_kinds)]

    lines_all = ty_count * LINES
    profiles = source_profiles[0].reshape(2, 3, lines_all, NZ).transpose(1, 2, 0, 3).reshape(3, lines_all, LANES)
    ext = (EXT_LINES, EXT_ROWS, LANES)
    electric, partial = pl.pallas_call(
        main_kernel,
        out_shape=(f32(1, 2, 3, ROWS, LINES * NZ), f32(ROWS, LINES * NZ)),
        in_specs=[smem] * 5
        + [vmem] * 4
        + [[vmem for _ in x_kinds], [[vmem for _ in range(2)] for _ in x_kinds]],
        out_specs=(vmem, vmem),
        scratch_shapes=[
            pltpu.VMEM((STEPS + 1, 3) + ext, jnp.float32),
            pltpu.VMEM((3,) + ext, jnp.float32),
            pltpu.VMEM((3,) + ext, jnp.float32),
            pltpu.VMEM((3,) + ext, jnp.float32),
            pltpu.VMEM(ext, jnp.float32),
            pltpu.VMEM((4,) + ext, jnp.float32),
        ],
        compiler_params=pltpu.CompilerParams(vmem_limit_bytes=48 * 1024 * 1024),
        name="window",
    )(place, source_waveforms[0], material_table, plane_indices, design_box, profiles, tile, y_a, y_b, x_msgs, corner_msgs)

    wave_count = lax.axis_size("wave")
    if wave_count == 4:
        one, two, three = [
            lax.ppermute(partial, "wave", [(i, i ^ k) for i in range(4)]) for k in (1, 2, 3)
        ]
        gradient = (partial + one) + (two + three)
    else:
        gradient = lax.psum(partial, "wave")
    return gradient, electric


def solution(mesh):
    placed = (
        P("wave", None, None, "tx", "ty"),
        P("wave", None, None, None),
        P("wave", None, None),
        P("tx", "ty"),
        P("tx", "ty"),
        P(),
        P(),
        P(),
    )
    return jax.shard_map(
        functools.partial(on_device, (mesh.shape["tx"], mesh.shape["ty"])),
        mesh=mesh,
        in_specs=placed,
        out_specs=(P("tx", "ty"), P("wave", None, None, "tx", "ty")),
        check_vma=False,
    )
```

time: 127 us -> 44.2 us (0.35)
  the two profiles are of different devices: /device:TPU:0 before, /device:TPU:17 now
where the time goes in v1:
time: 44.2 us; the launch traced here: 43.8 us
  Pallas kernels  15.3 us (35%)
  starting transfers between devices  11.6 us (26%)
  waiting for transfers between devices  9.46 us (21%)
  local copies, waits for them, and re-layouts  5.86 us (13%)
  other arithmetic  0.78 us (2%)
  between operations  0.72 us (2%)
    pallas_call x1, Pallas kernels, on_device(): pl.pallas_call(main_kernel, out_shape=(f32(1, 2, 3, ROWS, LINES * NZ), f3...  13.6 us
    ppermute x5, starting transfers between devices, swap(): return lax.ppermute(value, axes, pairs)  7.8 us
    ppermute x5, waiting for transfers between devices, swap(): return lax.ppermute(value, axes, pairs)  6.51 us
    ppermute x3, starting transfers between devices, on_device(): lax.ppermute(partial, 'wave', [(i, i ^ k) for i in range(4)])  3.79 us
    unnamed x14, local copies, waits for them, and re-layouts  3.2 us
    ppermute x3, waiting for transfers between devices, on_device(): lax.ppermute(partial, 'wave', [(i, i ^ k) for i in range(4)])  2.94 us
    pallas_call x1, Pallas kernels, on_device(): pl.pallas_call(pack_kernel, out_shape=(f32(FIELDS, LINES, ROWS, LANES), f...  1.72 us
    another operation x2, local copies, waits for them, and re-layouts, on_device(): source_profiles[0].reshape(2, 3, lines_all, NZ).transpose(1, 2, 0, 3)  1.64 us
  transfers between devices with their start and end apart: 8, of which 4 were waited for; matrix products, arithmetic and copies ran while one was open for 6% of the time, Pallas kernels for 0%

profile of v1, /device:TPU:17, one launch (start us, length us, event | category | flops | bytes accessed | tf_op | source)
XLA Modules:
  0.0 43.8 jit_solution(13480877040941373641)
XLA Ops:
  0.7 0.1 pad_add_fusion.1.parity
  0.7 0.6 %copy-done.1 = s32[16,512]{1,0:T(8,128)S(1)} copy-done((s32[16,512]{1,0:T(8,128)S(1)}, s32[16,512]{1,0:T(8,128)}, u32[]{:S(2)}) %copy-start.1) | copy-done | bytes 32792
  1.4 1.1 %copy-done = f32[1,2,12,16,512]{4,3,2,1,0:T(8,128)S(1)} copy-done((f32[1,2,12,16,512]{4,3,2,1,0:T(8,128)S(1)}, f32[1,2,12,16,512]{4,3,2,1,0:T(8,128)}, u32[]{:S(2)}) %copy-start) | copy-done | bytes 786456
  2.5 0.8 %copy-done.2 = f32[16,512]{1,0:T(8,128)S(1)} copy-done((f32[16,512]{1,0:T(8,128)S(1)}, f32[16,512]{1,0:T(8,128)}, u32[]{:S(2)}) %copy-start.2) | copy-done | bytes 32792
  3.3 1.7 %pack.1 = (f32[13,8,16,128]{3,2,1,0:T(8,128)S(1)}, f32[54,16,128]{2,1,0:T(8,128)S(1)}, f32[54,16,128]{2,1,0:T(8,128)S(1)}, f32[432,128]{1,0:T(8,128)S(1)}, f32[232,128]{1,0:T(8,128)}, /*index=5*/f32[232,128]{1,0:T(8,128)S(1)}) custom-call(s32[2]{0:T(128)S(1)} %pad_add_fusion.1.parity, f32[3,4]{1,0:T(4,128)S(1)} %copy-done.3, ...), custom_call_target="tpu_custom_call" | custom-call | tf_op jit(solution)/shard_map/pack/pallas_call | solution.py:355
  5.0 1.3 %collective-permute-start = (f32[54,16,128]{2,1,0:T(8,128)S(1)}, f32[54,16,128]{2,1,0:T(8,128)S(1)}, u32[]{:S(2)}, u32[]{:S(2)}) collective-permute-start(f32[54,16,128]{2,1,0:T(8,128)S(1)} %get-tuple-element.11), channel_id=1, source_target_pairs={{0,1},{1,0},{2,3},{3,2},{4,5},{5,4},{6,7},{7,6},{8,9},{9,8},{10,11... | collective-permute-start | bytes 1327112 | tf_op jit(solution)/shard_map/ppermute | solution.py:342
  6.3 1.9 %collective-permute-start.1 = (f32[54,16,128]{2,1,0:T(8,128)S(1)}, f32[54,16,128]{2,1,0:T(8,128)S(1)}, u32[]{:S(2)}, u32[]{:S(2)}) collective-permute-start(f32[54,16,128]{2,1,0:T(8,128)S(1)} %get-tuple-element.12), channel_id=1, source_target_pairs={{1,2},{2,1},{5,6},{6,5},{9,10},{10,9},{13,14},{14,13},{17,18},{18,... | collective-permute-start | bytes 1327112 | tf_op jit(solution)/shard_map/ppermute | solution.py:342
  8.2 1.3 %collective-permute-start.2 = (f32[432,128]{1,0:T(8,128)S(1)}, f32[432,128]{1,0:T(8,128)S(1)}, u32[]{:S(2)}, u32[]{:S(2)}) collective-permute-start(f32[432,128]{1,0:T(8,128)S(1)} %get-tuple-element.13), channel_id=1, source_target_pairs={{0,4},{1,5},{2,6},{3,7},{4,0},{5,1},{6,2},{7,3},{8,12},{9,13},{10,... | collective-permute-start | bytes 663560 | tf_op jit(solution)/shard_map/ppermute | solution.py:342
  9.5 0.0 collective-permute-start.3
  9.5 3.3 %collective-permute-start.4 = (f32[232,128]{1,0:T(8,128)S(1)}, f32[232,128]{1,0:T(8,128)S(1)}, u32[]{:S(2)}, u32[]{:S(2)}) collective-permute-start(f32[232,128]{1,0:T(8,128)S(1)} %get-tuple-element.15), channel_id=1, source_target_pairs={{1,6},{2,5},{5,2},{6,1},{9,14},{10,13},{13,10},{14,9},{17,22},{18,... | collective-permute-start | bytes 356360 | tf_op jit(solution)/shard_map/ppermute | solution.py:342
  12.8 0.9 %reshape_squeeze.3 = f32[2,3,32,64]{3,2,0,1:T(8,128)S(1)} reshape(f32[1,2,3,2048]{3,1,2,0:T(2,128)} %param.9) | data formatting | bytes 98304 | tf_op jit(solution)/shard_map/reshape;squeeze | solution.py:380
  13.7 0.7 %copy.12 = f32[2,3,32,64]{3,0,2,1:T(2,128)} copy(f32[2,3,32,64]{3,2,0,1:T(8,128)S(1)} %reshape_squeeze.3) | data formatting | bytes 98304 | tf_op jit(solution)/shard_map/reshape;squeeze | solution.py:380
  14.5 1.0 %reshape.7.profiles = f32[3,32,128]{2,1,0:T(8,128)S(1)} reshape(f32[3,32,2,64]{3,2,1,0:T(2,128)} %bitcast.11) | data formatting | bytes 98304 | tf_op jit(solution)/shard_map/reshape | solution.py:380
  15.5 0.1 pad_add_fusion.place
  15.6 3.9 %collective-permute-done.3.corner_msgs_0__0_ = f32[232,128]{1,0:T(8,128)S(1)} collective-permute-done((f32[232,128]{1,0:T(8,128)}, f32[232,128]{1,0:T(8,128)S(1)}, u32[]{:S(2)}, u32[]{:S(2)}) %collective-permute-start.3) | collective-permute-done | bytes 118816 | tf_op jit(solution)/shard_map/ppermute | solution.py:342
  19.5 2.6 %collective-permute-done.4.corner_msgs_0__1_ = f32[232,128]{1,0:T(8,128)S(1)} collective-permute-done((f32[232,128]{1,0:T(8,128)S(1)}, f32[232,128]{1,0:T(8,128)S(1)}, u32[]{:S(2)}, u32[]{:S(2)}) %collective-permute-start.4) | collective-permute-done | bytes 118816 | tf_op jit(solution)/shard_map/ppermute | solution.py:342
  22.1 0.0 collective-permute-done.2.x_msgs_0_
  22.1 0.0 collective-permute-done.y_a
  22.1 0.0 collective-permute-done.1.y_b
  22.1 0.0 copy-start.4
  22.1 0.0 copy-start.5
  22.1 0.0 copy-done.6
  22.1 0.6 %copy-done.4 = f32[1,2,5]{2,1,0:T(2,128)S(1)} copy-done((f32[1,2,5]{2,1,0:T(2,128)S(1)}, f32[1,2,5]{2,1,0:T(2,128)}, u32[]{:S(2)}) %copy-start.4) | copy-done | bytes 64
  22.8 0.0 copy-done.5
  22.8 13.6 %window.1 = (f32[1,2,3,16,512]{4,3,2,1,0:T(8,128)}, f32[16,512]{1,0:T(8,128)S(1)}) custom-call(s32[4]{0:T(128)S(1)} %pad_add_fusion.place, f32[2,5]{1,0:T(2,128)S(1)} %bitcast.10, f32[3,4]{1,0:T(4,128)S(1)} %copy-done.3, s32[2]{0:T(128)S(1)} %copy-done.5, s32[6]{0:T(128)S(1)} %copy-done.6, f32[3,32,128]{2,1,0:T(8,128)S(1)} %reshape.7.profiles, ...), custom_call_target="tpu_custom_call" | custom-call | tf_op jit(solution)/shard_map/window/pallas_call | solution.py:382
  36.4 2.2 %collective-permute-start.5 = (f32[16,512]{1,0:T(8,128)S(1)}, f32[16,512]{1,0:T(8,128)S(1)}, u32[]{:S(2)}, u32[]{:S(2)}) collective-permute-start(f32[16,512]{1,0:T(8,128)S(1)} %get-tuple-element.16), channel_id=1, source_target_pairs={{0,8},{8,0},{16,24},{24,16},{1,9},{9,1},{17,25},{25,17},{2,10},{10... | collective-permute-start | bytes 98312 | tf_op jit(solution)/shard_map/ppermute | solution.py:404
  38.5 1.2 %collective-permute-start.6 = (f32[16,512]{1,0:T(8,128)S(1)}, f32[16,512]{1,0:T(8,128)S(1)}, u32[]{:S(2)}, u32[]{:S(2)}) collective-permute-start(f32[16,512]{1,0:T(8,128)S(1)} %get-tuple-element.16), channel_id=1, source_target_pairs={{0,16},{8,24},{16,0},{24,8},{1,17},{9,25},{17,1},{25,9},{2,18},{10... | collective-permute-start | bytes 98312 | tf_op jit(solution)/shard_map/ppermute | solution.py:404
  39.8 0.4 collective-permute-start.7
  40.2 0.0 collective-permute-done.5
  40.2 1.1 %collective-permute-done.6 = f32[16,512]{1,0:T(8,128)S(1)} collective-permute-done((f32[16,512]{1,0:T(8,128)S(1)}, f32[16,512]{1,0:T(8,128)S(1)}, u32[]{:S(2)}, u32[]{:S(2)}) %collective-permute-start.6) | collective-permute-done | bytes 32800 | tf_op jit(solution)/shard_map/ppermute | solution.py:404
  41.3 1.8 %collective-permute-done.7 = f32[16,512]{1,0:T(8,128)S(1)} collective-permute-done((f32[16,512]{1,0:T(8,128)S(1)}, f32[16,512]{1,0:T(8,128)S(1)}, u32[]{:S(2)}, u32[]{:S(2)}) %collective-permute-start.7) | collective-permute-done | bytes 32800 | tf_op jit(solution)/shard_map/ppermute | solution.py:404
  43.1 0.6 %add_add_fusion = f32[16,512]{1,0:T(8,128)} fusion(f32[16,512]{1,0:T(8,128)S(1)} %collective-permute-done.6, f32[16,512]{1,0:T(8,128)S(1)} %collective-permute-done.7, f32[16,512]{1,0:T(8,128)S(1)} %get-tuple-element.16, f32[16,512]{1,0:T(8,128)S(1)} %collective-permute-done.5), kind=kLoop, calls=%fused_computation.1 | loop fusion | flops 24576 | bytes 163840 | tf_op jit(solution)/shard_map/add | solution.py:406
  (7 shorter events, 0.0 us)
Async XLA Ops:
  0.6 0.8 %copy-start.1 = (s32[16,512]{1,0:T(8,128)S(1)}, s32[16,512]{1,0:T(8,128)}, u32[]{:S(2)}) copy-start(s32[16,512]{1,0:T(8,128)} %material.1) | copy-start | bytes 98308
  0.7 0.7 %copy-start.3 = (f32[3,4]{1,0:T(4,128)S(1)}, f32[3,4]{1,0:T(4,128)}, u32[]{:S(2)}) copy-start(f32[3,4]{1,0:T(4,128)} %table.3) | copy-start | bytes 148
  1.4 1.1 %copy-start = (f32[1,2,12,16,512]{4,3,2,1,0:T(8,128)S(1)}, f32[1,2,12,16,512]{4,3,2,1,0:T(8,128)}, u32[]{:S(2)}) copy-start(f32[1,2,12,16,512]{4,3,2,1,0:T(8,128)} %fields.1) | copy-start | bytes 2359300
  2.5 0.8 %copy-start.2 = (f32[16,512]{1,0:T(8,128)S(1)}, f32[16,512]{1,0:T(8,128)}, u32[]{:S(2)}) copy-start(f32[16,512]{1,0:T(8,128)} %density.1) | copy-start | bytes 98308
  5.0 17.1 %collective-permute-start = (f32[54,16,128]{2,1,0:T(8,128)S(1)}, f32[54,16,128]{2,1,0:T(8,128)S(1)}, u32[]{:S(2)}, u32[]{:S(2)}) collective-permute-start(f32[54,16,128]{2,1,0:T(8,128)S(1)} %get-tuple-element.11), channel_id=1, source_target_pairs={{0,1},{1,0},{2,3},{3,2},{4,5},{5,4},{6,7},{7,6},{8,9},{9,8},{10,11... | collective-permute-start | bytes 1327112 | tf_op jit(solution)/shard_map/ppermute | solution.py:342
  6.3 15.8 %collective-permute-start.1 = (f32[54,16,128]{2,1,0:T(8,128)S(1)}, f32[54,16,128]{2,1,0:T(8,128)S(1)}, u32[]{:S(2)}, u32[]{:S(2)}) collective-permute-start(f32[54,16,128]{2,1,0:T(8,128)S(1)} %get-tuple-element.12), channel_id=1, source_target_pairs={{1,2},{2,1},{5,6},{6,5},{9,10},{10,9},{13,14},{14,13},{17,18},{18,... | collective-permute-start | bytes 1327112 | tf_op jit(solution)/shard_map/ppermute | solution.py:342
  8.2 13.9 %collective-permute-start.2 = (f32[432,128]{1,0:T(8,128)S(1)}, f32[432,128]{1,0:T(8,128)S(1)}, u32[]{:S(2)}, u32[]{:S(2)}) collective-permute-start(f32[432,128]{1,0:T(8,128)S(1)} %get-tuple-element.13), channel_id=1, source_target_pairs={{0,4},{1,5},{2,6},{3,7},{4,0},{5,1},{6,2},{7,3},{8,12},{9,13},{10,... | collective-permute-start | bytes 663560 | tf_op jit(solution)/shard_map/ppermute | solution.py:342
  9.5 10.0 %collective-permute-start.3 = (f32[232,128]{1,0:T(8,128)}, f32[232,128]{1,0:T(8,128)S(1)}, u32[]{:S(2)}, u32[]{:S(2)}) collective-permute-start(f32[232,128]{1,0:T(8,128)} %get-tuple-element.14), channel_id=1, source_target_pairs={{0,5},{1,4},{2,7},{3,6},{4,1},{5,0},{6,3},{7,2},{8,13},{9,12},{10,... | collective-permute-start | bytes 356360 | tf_op jit(solution)/shard_map/ppermute | solution.py:342
  9.5 12.6 %collective-permute-start.4 = (f32[232,128]{1,0:T(8,128)S(1)}, f32[232,128]{1,0:T(8,128)S(1)}, u32[]{:S(2)}, u32[]{:S(2)}) collective-permute-start(f32[232,128]{1,0:T(8,128)S(1)} %get-tuple-element.15), channel_id=1, source_target_pairs={{1,6},{2,5},{5,2},{6,1},{9,14},{10,13},{13,10},{14,9},{17,22},{18,... | collective-permute-start | bytes 356360 | tf_op jit(solution)/shard_map/ppermute | solution.py:342
  14.5 7.6 %copy-start.6 = (s32[6]{0:T(128)S(1)}, s32[6]{0:T(128)}, u32[]{:S(2)}) copy-start(s32[6]{0:T(128)} %box.1) | copy-start | bytes 76
  22.1 0.7 %copy-start.4 = (f32[1,2,5]{2,1,0:T(2,128)S(1)}, f32[1,2,5]{2,1,0:T(2,128)}, u32[]{:S(2)}) copy-start(f32[1,2,5]{2,1,0:T(2,128)} %param.10) | copy-start | bytes 124
  22.1 0.7 %copy-start.5 = (s32[2]{0:T(128)S(1)}, s32[2]{0:T(128)}, u32[]{:S(2)}) copy-start(s32[2]{0:T(128)} %plane.1) | copy-start | bytes 28
  36.4 3.8 %collective-permute-start.5 = (f32[16,512]{1,0:T(8,128)S(1)}, f32[16,512]{1,0:T(8,128)S(1)}, u32[]{:S(2)}, u32[]{:S(2)}) collective-permute-start(f32[16,512]{1,0:T(8,128)S(1)} %get-tuple-element.16), channel_id=1, source_target_pairs={{0,8},{8,0},{16,24},{24,16},{1,9},{9,1},{17,25},{25,17},{2,10},{10... | collective-permute-start | bytes 98312 | tf_op jit(solution)/shard_map/ppermute | solution.py:404
  38.5 2.8 %collective-permute-start.6 = (f32[16,512]{1,0:T(8,128)S(1)}, f32[16,512]{1,0:T(8,128)S(1)}, u32[]{:S(2)}, u32[]{:S(2)}) collective-permute-start(f32[16,512]{1,0:T(8,128)S(1)} %get-tuple-element.16), channel_id=1, source_target_pairs={{0,16},{8,24},{16,0},{24,8},{1,17},{9,25},{17,1},{25,9},{2,18},{10... | collective-permute-start | bytes 98312 | tf_op jit(solution)/shard_map/ppermute | solution.py:404
  39.8 3.3 %collective-permute-start.7 = (f32[16,512]{1,0:T(8,128)S(1)}, f32[16,512]{1,0:T(8,128)S(1)}, u32[]{:S(2)}, u32[]{:S(2)}) collective-permute-start(f32[16,512]{1,0:T(8,128)S(1)} %get-tuple-element.16), channel_id=1, source_target_pairs={{0,24},{8,16},{16,8},{24,0},{1,25},{9,17},{17,9},{25,1},{2,26},{10... | collective-permute-start | bytes 98312 | tf_op jit(solution)/shard_map/ppermute | solution.py:404

commit v2 on v1

v2 whole, which is shorter than its diff:
```python
import functools

import jax
import jax.numpy as jnp
from jax import lax
from jax.experimental import pallas as pl
from jax.experimental.pallas import tpu as pltpu
from jax.sharding import PartitionSpec as P

NZ = 64
STEPS = 5
NMAT = 3
LANES = 2 * NZ
ROWS = 16
LINES = 8
CHUNKS = LINES // 2
PAD = 8
EXT_LINES = LINES + 2 * STEPS
FIELDS = 13

time_step = 0.5
contrast = 2.0

LINE_DEPTH = (5, 5, 5, 5, 4, 5, 3, 3, 3, 4, 4, 4, 4)
ROW_DEPTH = (5, 5, 5, 4, 5, 5, 3, 3, 3, 4, 4, 4, 4)
SAME_DEPTH = (4, 4, 4, 4, 4, 4, 2, 2, 2, 3, 3, 3, 3)
MIXED_DEPTH = (5, 5, 4, 4, 4, 4, 3, 3, 2, 4, 4, 3, 4)

Y_ENTRIES = [(f, k) for f in range(FIELDS) for k in range(LINE_DEPTH[f])]


def listed(entries):
    start, out = 0, []
    for f, k, depth in entries:
        out.append((f, k, depth, start))
        start += depth
    return out, (start + 7) // 8 * 8


X_ENTRIES, X_ROWS = listed([(f, line, ROW_DEPTH[f]) for f in range(FIELDS) for line in range(LINES)])
CORNERS = [
    listed([(f, k, depth[f] - k) for f in range(FIELDS) for k in range(depth[f])])
    for depth in (SAME_DEPTH, MIXED_DEPTH)
]


def low_lanes(shape):
    return lax.broadcasted_iota(jnp.int32, shape, len(shape) - 1) < NZ


def half_turn(v):
    return pltpu.roll(v, NZ, v.ndim - 1)


def choose(material, column):
    values = [column(m) for m in range(NMAT)]
    return jnp.where(material < 0.5, values[0], jnp.where(material < 1.5, values[1], values[2]))


def pole(table):
    out = []
    for m in range(NMAT):
        d, w, g = table[m, 1], table[m, 2], table[m, 3]
        denom = 1.0 + 0.25 * g
        drive = w * w * time_step / denom
        out.append(((1.0 - 0.25 * g) / denom, drive, drive * d))
    return [lambda m, i=i: out[m][i] for i in range(3)]


def pack_kernel(table_hbm, fields_hbm, material_hbm, density_hbm, tile, y_a, y_b, table, fields, material, density, sems):
    copies = [
        pltpu.make_async_copy(table_hbm, table, sems.at[CHUNKS]),
        pltpu.make_async_copy(material_hbm, material, sems.at[CHUNKS + 1]),
        pltpu.make_async_copy(density_hbm, density, sems.at[CHUNKS + 2]),
    ]
    chunks = [
        pltpu.make_async_copy(
            fields_hbm.at[0, :, :, :, pl.ds(k * LANES, LANES)], fields.at[k], sems.at[k]
        )
        for k in range(CHUNKS)
    ]
    for copy in copies + chunks:
        copy.start()
    for copy in copies:
        copy.wait()
    decay, drive, coupled = pole(table)
    low = low_lanes((ROWS, LANES))
    for k in range(CHUNKS):
        at = slice(k * LANES, (k + 1) * LANES)
        chunks[k].wait()

        def split(one, two):
            return jnp.where(low, one, half_turn(two)), jnp.where(low, half_turn(one), two)

        pairs = [split(fields[k, 0, f], fields[k, 1, f]) for f in range(12)]
        mat, dens = material[:, at].astype(jnp.float32), density[:, at]
        turned = half_turn(mat)
        mats = (jnp.where(low, mat, turned), jnp.where(low, turned, mat))
        mixed = split(mat, dens)
        for half in range(2):
            line = 2 * k + half
            dec, dri, cou = [choose(mats[half], column) for column in (decay, drive, coupled)]
            for c in range(3):
                e, p, j = pairs[c][half], pairs[6 + c][half], pairs[9 + c][half]
                j = dec * j + cou * e - dri * p
                tile[c, line] = e
                tile[3 + c, line] = pairs[3 + c][half]
                tile[6 + c, line] = p + time_step * j
                tile[9 + c, line] = j
            tile[12, line] = mixed[half]
    odd = lax.rem(lax.axis_index("ty"), 2) == 1
    for i, (f, k) in enumerate(Y_ENTRIES):
        first, last = k, LINES - 1 - k
        y_a[i] = tile[f, jnp.where(odd, first, last)]
        y_b[i] = tile[f, jnp.where(odd, last, first)]


def edge_kernel(tile, *messages):
    odd = lax.rem(lax.axis_index("tx"), 2)
    for kind in range(len(messages) // 3):
        along, same, mixed = messages[3 * kind : 3 * kind + 3]
        for is_lower in (True, False):

            @pl.when((odd == kind) == is_lower)
            def _(is_lower=is_lower, along=along, same=same, mixed=mixed):
                def pack(message, entries, line_of):
                    for f, k, depth, start in entries:
                        rows = slice(ROWS - depth, ROWS) if is_lower else slice(0, depth)
                        message[start : start + depth, :] = tile[f, line_of(k), rows, :]

                pack(along, X_ENTRIES, lambda k: k)
                pack(same, CORNERS[0][0], lambda k: LINES - 1 - k if is_lower else k)
                pack(mixed, CORNERS[1][0], lambda k: k if is_lower else LINES - 1 - k)


def window_kernel(
    tx_count,
    ty_count,
    waveforms_hbm,
    table_hbm,
    plane_hbm,
    box_hbm,
    profiles,
    tile,
    y_a,
    y_b,
    *rest,
):
    kinds = 1 if tx_count == 2 else 2
    messages, rest = rest[: 3 * kinds], rest[3 * kinds :]
    electric_out, gradient_out, E, H, Pol, J, C, coef, source, waveforms, table, plane, box, sems = rest
    wide = tx_count != 2
    ext_rows = E[0].shape[2]
    copies = [
        pltpu.make_async_copy(src, dst, sems.at[i])
        for i, (src, dst) in enumerate(
            [(waveforms_hbm, waveforms), (table_hbm, table), (plane_hbm, plane), (box_hbm, box)]
        )
    ]
    for copy in copies:
        copy.start()
    tx, ty = lax.axis_index("tx"), lax.axis_index("ty")
    odd_x, odd_y = lax.rem(tx, 2), lax.rem(ty, 2)
    offset = PAD if wide else pl.multiple_of(tx * PAD, PAD)
    rows_base, lines_base = tx * ROWS - offset, ty * LINES - STEPS
    rows_all, lines_all = tx_count * ROWS, ty_count * LINES
    middle = pl.ds(offset, ROWS)

    def put(f, line, rows, value):
        if f < 12:
            (E[0], H[0], Pol[0], J[0])[f // 3][f % 3, line, rows, :] = value
        else:
            C[line, rows, :] = value

    for ref in (E[0], H[0], Pol[0], J[0], C):
        ref[...] = jnp.zeros(ref.shape, jnp.float32)
    for f in range(FIELDS):
        for line in range(LINES):
            put(f, STEPS + line, middle, tile[f, line])

    def line_at(ahead, k):
        return jnp.where(ahead, STEPS + LINES + k, STEPS - 1 - k)

    for i, (f, k) in enumerate(Y_ENTRIES):
        put(f, line_at(odd_y == 0, k), middle, y_a[i])
        put(f, line_at(odd_y == 1, k), middle, y_b[i])
    for kind in range(kinds):
        along, same, mixed = messages[3 * kind : 3 * kind + 3]
        for is_lower in (True, False):

            @pl.when((odd_x == kind) == is_lower)
            def _(is_lower=is_lower, along=along, same=same, mixed=mixed):
                def unpack(message, entries, line_of):
                    for f, k, depth, start in entries:
                        if wide:
                            first = PAD + ROWS if is_lower else PAD - depth
                        else:
                            first = ROWS if is_lower else PAD - depth
                        put(f, line_of(k), slice(first, first + depth), message[start : start + depth, :])

                unpack(along, X_ENTRIES, lambda k: STEPS + k)
                unpack(same, CORNERS[0][0], lambda k: STEPS + LINES + k if is_lower else STEPS - 1 - k)
                unpack(mixed, CORNERS[1][0], lambda k: STEPS - 1 - k if is_lower else STEPS + LINES + k)
    for copy in copies:
        copy.wait()
    decay, drive, coupled = pole(table)
    shape = (ext_rows, LANES)
    low = low_lanes(shape)
    lane = lax.broadcasted_iota(jnp.int32, shape, 1)
    depth_id = jnp.where(low, lane, lane - NZ)
    row = lax.broadcasted_iota(jnp.int32, shape, 0) + rows_base
    first_z, last_z = depth_id == 0, depth_id == NZ - 1
    row_mask = ((row >= 0) & (row < rows_all)).astype(jnp.float32)
    in_z = (depth_id >= box[4]) & (depth_id < box[5])
    design_rows = ((row >= box[0]) & (row < box[1]) & in_z).astype(jnp.float32)
    source_rows = (row == jnp.where(low, plane[0], plane[1])).astype(jnp.float32)

    def line_design(line):
        where = lines_base + line
        return ((where >= box[2]) & (where < box[3])).astype(jnp.float32)

    def line_inside(line):
        where = lines_base + line
        return ((where >= 0) & (where < lines_all)).astype(jnp.float32)

    def is_own(line):
        return STEPS <= line < STEPS + LINES

    for line in range(1, EXT_LINES - 1):
        mixed = C[line]
        turned = half_turn(mixed)
        mat = jnp.where(low, mixed, turned)
        dens = jnp.where(low, turned, mixed)
        design = design_rows * line_design(line)
        permittivity = choose(mat, lambda m: table[m, 0]) + (design * dens) * contrast
        reach = time_step / permittivity
        if wide:
            reach = reach * row_mask
        if not is_own(line):
            reach = reach * line_inside(line)
        coef[0, line] = reach
        for i, column in enumerate((decay, drive, coupled)):
            coef[1 + i, line] = choose(mat, column)

    low_row = low[:1]
    for i in range(EXT_LINES // 2):
        chunk = jnp.clip(ty * CHUNKS + (i - STEPS // 2 - 1) + 1, 0, ty_count * CHUNKS - 1)
        for c in range(3):
            both = profiles[c, :, pl.ds(pl.multiple_of(chunk * LANES, LANES), LANES)]
            one, two = both[0:1], both[1:2]
            source[c, pl.ds(2 * i + 1, 1), :] = jnp.where(low_row, one, half_turn(two))
            source[c, pl.ds(2 * i + 2, 1), :] = jnp.where(low_row, half_turn(one), two)

    edge = jnp.zeros((1, LANES), jnp.float32)

    def ahead_row(v):
        return jnp.concatenate([v[1:], edge], axis=0)

    def behind_row(v):
        return jnp.concatenate([edge, v[:-1]], axis=0)

    def ahead_depth(v):
        return jnp.where(last_z, 0.0, pltpu.roll(v, LANES - 1, 1))

    def behind_depth(v):
        return jnp.where(first_z, 0.0, pltpu.roll(v, 1, 1))

    def magnetic_line(n, line):
        old, new = H[n % 2], H[(n + 1) % 2]
        ex, ey, ez = E[n][0, line], E[n][1, line], E[n][2, line]
        ex_next, ez_next = E[n][0, line + 1], E[n][2, line + 1]
        half = time_step
        if line < STEPS:
            half = half * line_inside(line)
        if wide:
            half = half * row_mask
        new[0, line] = old[0, line] - half * ((ez_next - ez) - (ahead_depth(ey) - ey))
        new[1, line] = old[1, line] - half * ((ahead_depth(ex) - ex) - (ahead_row(ez) - ez))
        new[2, line] = old[2, line] - half * ((ahead_row(ey) - ey) - (ex_next - ex))

    def electric_line(n, line, weight):
        field = H[(n + 1) % 2]
        hx, hy, hz = field[0, line], field[1, line], field[2, line]
        hx_last, hz_last = field[0, line - 1], field[2, line - 1]
        curls = (
            (hz - hz_last) - (hy - behind_depth(hy)),
            (hx - behind_depth(hx)) - (hz - behind_row(hz)),
            (hy - behind_row(hy)) - (hx - hx_last),
        )
        reach = coef[0, line]
        for c in range(3):
            e = E[n][c, line]
            if n == 0:
                j = J[0][c, line]
            else:
                p = Pol[(n + 1) % 2][c, line]
                j = coef[1, line] * J[(n + 1) % 2][c, line] + coef[3, line] * e - coef[2, line] * p
                if n < STEPS - 1:
                    J[n % 2][c, line] = j
                    Pol[n % 2][c, line] = p + time_step * j
            drawn = source_rows * (weight * source[c, line : line + 1, :])
            E[n + 1][c, line] = e + reach * ((curls[c] - j) - drawn)

    for n in range(STEPS):
        weight = jnp.where(low_row, waveforms[0, n], waveforms[1, n])
        for line in range(n, EXT_LINES - 1 - n):
            magnetic_line(n, line)
        for line in range(n + 1, EXT_LINES - 1 - n):
            electric_line(n, line, weight)

    low_tile = low[:ROWS]
    row_tile = lax.broadcasted_iota(jnp.int32, (ROWS, LANES), 0) + tx * ROWS
    design_tile = (
        (row_tile >= box[0]) & (row_tile < box[1]) & in_z[:ROWS]
    ).astype(jnp.float32) * contrast
    for k in range(CHUNKS):
        sums = []
        for half in range(2):
            line = STEPS + 2 * k + half
            total = jnp.zeros((ROWS, LANES), jnp.float32)
            for c in range(3):
                history = [E[n][c, line, middle, :] for n in range(STEPS + 1)]
                for n in range(1, STEPS + 1):
                    total = total + half_turn(history[STEPS + 1 - n]) * (history[n] - history[n - 1])
                electric_out[c, 2 * k + half] = history[STEPS]
            sums.append(total * (design_tile * line_design(line)))
        gradient_out[:, k * LANES : (k + 1) * LANES] = jnp.where(low_tile, sums[0], half_turn(sums[1]))


def emit_kernel(electric, out):
    low = low_lanes((ROWS, LANES))
    for k in range(CHUNKS):
        at = slice(k * LANES, (k + 1) * LANES)
        for c in range(3):
            one, two = electric[c, 2 * k], electric[c, 2 * k + 1]
            out[0, 0, c, :, at] = jnp.where(low, one, half_turn(two))
            out[0, 1, c, :, at] = jnp.where(low, half_turn(one), two)


def pair_of(index, kind, count):
    other = index + 1 if index % 2 == kind else index - 1
    return other if 0 <= other < count else None


def f32(*shape):
    return jax.ShapeDtypeStruct(shape, jnp.float32)


def in_hbm(value):
    return pltpu.with_memory_space_constraint(value, pltpu.HBM)


def on_device(
    tx_count,
    ty_count,
    initial_fields,
    source_profiles,
    source_waveforms,
    material_map,
    design_density,
    material_table,
    plane_indices,
    design_box,
):
    hbm = pl.BlockSpec(memory_space=pltpu.HBM)
    vmem = pl.BlockSpec(memory_space=pltpu.VMEM)
    kinds = (0,) if tx_count == 2 else (0, 1)

    def swap(value, partner):
        pairs = []
        for x in range(tx_count):
            for y in range(ty_count):
                other = partner(x, y)
                if None not in other and 0 <= other[1] < ty_count:
                    pairs.append((x * ty_count + y, other[0] * ty_count + other[1]))
        return lax.ppermute(value, ("tx", "ty"), pairs)

    def corner(kind, mixed):
        def partner(x, y):
            lower = x % 2 == kind
            return pair_of(x, kind, tx_count), y + (1 if lower != mixed else -1)

        return partner

    tile, y_a, y_b = pl.pallas_call(
        pack_kernel,
        out_shape=(
            f32(FIELDS, LINES, ROWS, LANES),
            f32(len(Y_ENTRIES), ROWS, LANES),
            f32(len(Y_ENTRIES), ROWS, LANES),
        ),
        in_specs=[hbm] * 4,
        out_specs=(vmem, vmem, vmem),
        scratch_shapes=[
            pltpu.SMEM((NMAT, 4), jnp.float32),
            pltpu.VMEM((CHUNKS, 2, 12, ROWS, LANES), jnp.float32),
            pltpu.VMEM((ROWS, LINES * NZ), jnp.int32),
            pltpu.VMEM((ROWS, LINES * NZ), jnp.float32),
            pltpu.SemaphoreType.DMA((CHUNKS + 3,)),
        ],
        compiler_params=pltpu.CompilerParams(vmem_limit_bytes=32 * 1024 * 1024),
        name="pack",
    )(*[in_hbm(v) for v in (material_table, initial_fields, material_map, design_density)])
    y_a = swap(y_a, lambda x, y: (x, pair_of(y, 0, ty_count)))
    y_b = swap(y_b, lambda x, y: (x, pair_of(y, 1, ty_count)))

    sizes = (X_ROWS, CORNERS[0][1], CORNERS[1][1]) * len(kinds)
    messages = pl.pallas_call(
        edge_kernel,
        out_shape=[f32(size, LANES) for size in sizes],
        in_specs=[vmem],
        out_specs=[vmem] * len(sizes),
        compiler_params=pltpu.CompilerParams(vmem_limit_bytes=32 * 1024 * 1024),
        name="edges",
    )(tile)
    arrived = []
    for i, message in enumerate(messages):
        kind = i // 3
        if i % 3 == 0:
            arrived.append(swap(message, lambda x, y, kind=kind: (pair_of(x, kind, tx_count), y)))
        else:
            arrived.append(swap(message, corner(kind, i % 3 == 2)))

    ext = (EXT_LINES, ROWS + (PAD if tx_count == 2 else 2 * PAD), LANES)
    electric, partial = pl.pallas_call(
        functools.partial(window_kernel, tx_count, ty_count),
        out_shape=(f32(3, LINES, ROWS, LANES), f32(ROWS, LINES * NZ)),
        in_specs=[hbm] * 4 + [vmem] * (4 + len(arrived)),
        out_specs=(vmem, vmem),
        scratch_shapes=[
            [pltpu.VMEM((3,) + ext, jnp.float32) for _ in range(STEPS + 1)],
            [pltpu.VMEM((3,) + ext, jnp.float32) for _ in range(2)],
            [pltpu.VMEM((3,) + ext, jnp.float32) for _ in range(2)],
            [pltpu.VMEM((3,) + ext, jnp.float32) for _ in range(2)],
            pltpu.VMEM(ext, jnp.float32),
            pltpu.VMEM((4,) + ext, jnp.float32),
            pltpu.VMEM((3, EXT_LINES + 6, LANES), jnp.float32),
            pltpu.SMEM((2, STEPS), jnp.float32),
            pltpu.SMEM((NMAT, 4), jnp.float32),
            pltpu.SMEM((2,), jnp.int32),
            pltpu.SMEM((6,), jnp.int32),
            pltpu.SemaphoreType.DMA((4,)),
        ],
        compiler_params=pltpu.CompilerParams(vmem_limit_bytes=48 * 1024 * 1024),
        name="window",
    )(
        *[in_hbm(v) for v in (source_waveforms[0], material_table, plane_indices, design_box)],
        source_profiles[0].transpose(1, 0, 2),
        tile,
        y_a,
        y_b,
        *arrived,
    )
    final = pl.pallas_call(
        emit_kernel,
        out_shape=f32(1, 2, 3, ROWS, LINES * NZ),
        in_specs=[vmem],
        out_specs=vmem,
        name="emit",
    )(electric)

    if lax.axis_size("wave") == 4:
        one, two, three = [
            lax.ppermute(partial, "wave", [(i, i ^ k) for i in range(4)]) for k in (1, 2, 3)
        ]
        gradient = (partial + one) + (two + three)
    else:
        gradient = lax.psum(partial, "wave")
    return gradient, final


def solution(mesh):
    placed = (
        P("wave", None, None, "tx", "ty"),
        P("wave", None, None, None),
        P("wave", None, None),
        P("tx", "ty"),
        P("tx", "ty"),
        P(),
        P(),
        P(),
    )
    return jax.shard_map(
        functools.partial(on_device, mesh.shape["tx"], mesh.shape["ty"]),
        mesh=mesh,
        in_specs=placed,
        out_specs=(P("tx", "ty"), P("wave", None, None, "tx", "ty")),
        check_vma=False,
    )
```

time: 44.2 us -> 29.4 us (0.67)
  the two profiles are of different devices: /device:TPU:17 before, /device:TPU:16 now
where the time goes in v2:
time: 29.4 us; the launch traced here: 29.1 us
  starting transfers between devices  13 us (44%)
  waiting for transfers between devices  7.45 us (25%)
  Pallas kernels  6.6 us (22%)
  between operations  0.71 us (2%)
  local copies, waits for them, and re-layouts  0.68 us (2%)
  other arithmetic  0.63 us (2%)
    ppermute x5, starting transfers between devices, swap(): return lax.ppermute(value, ('tx', 'ty'), pairs)  10.9 us
    ppermute x5, waiting for transfers between devices, swap(): return lax.ppermute(value, ('tx', 'ty'), pairs)  6.45 us
    pallas_call x1, Pallas kernels, on_device(): pl.pallas_call(functools.partial(window_kernel, tx_count, ty_count), out_...  3.21 us
    ppermute x3, starting transfers between devices, on_device(): lax.ppermute(partial, 'wave', [(i, i ^ k) for i in range(4)])  2.14 us
    pallas_call x1, Pallas kernels, on_device(): pl.pallas_call(emit_kernel, out_shape=f32(1, 2, 3, ROWS, LINES * NZ), in_...  1.72 us
    pallas_call x1, Pallas kernels, on_device(): pl.pallas_call(pack_kernel, out_shape=(f32(FIELDS, LINES, ROWS, LANES), f...  1.58 us
    ppermute x3, waiting for transfers between devices, on_device(): lax.ppermute(partial, 'wave', [(i, i ^ k) for i in range(4)])  1 us
    unnamed x4, local copies, waits for them, and re-layouts  0.68 us
  transfers between devices with their start and end apart: 8, of which 4 were waited for; matrix products, arithmetic and copies ran while one was open for 0% of the time, Pallas kernels for 6%

profile of v2, /device:TPU:16, one launch (start us, length us, event | category | flops | bytes accessed | tf_op | source)
XLA Modules:
  0.0 29.1 jit_solution(5105891319367431755)
XLA Ops:
  0.6 1.6 %pack.1 = (f32[13,8,16,128]{3,2,1,0:T(8,128)S(1)}, f32[54,16,128]{2,1,0:T(8,128)S(1)}, f32[54,16,128]{2,1,0:T(8,128)S(1)}) custom-call(f32[3,4]{1,0:T(4,128)} %table_hbm.3, f32[1,2,12,16,512]{4,3,2,1,0:T(8,128)} %fields_hbm.1, s32[16,512]{1,0:T(8,128)} %material_hbm.1, f32[16,512]{1,0:T(8,128)} %density_hbm.1), custom_call_target="tpu_custom_call" | custom-call | tf_op jit(solution)/shard_map/pack/pallas_call | solution.py:385
  2.2 1.6 %collective-permute-start = (f32[54,16,128]{2,1,0:T(8,128)S(1)}, f32[54,16,128]{2,1,0:T(8,128)S(1)}, u32[]{:S(2)}, u32[]{:S(2)}) collective-permute-start(f32[54,16,128]{2,1,0:T(8,128)S(1)} %get-tuple-element.11), channel_id=1, source_target_pairs={{0,1},{1,0},{2,3},{3,2},{4,5},{5,4},{6,7},{7,6},{8,9},{9,8},{10,11... | collective-permute-start | bytes 1327112 | tf_op jit(solution)/shard_map/ppermute | solution.py:376
  3.9 1.9 %collective-permute-start.1 = (f32[54,16,128]{2,1,0:T(8,128)S(1)}, f32[54,16,128]{2,1,0:T(8,128)S(1)}, u32[]{:S(2)}, u32[]{:S(2)}) collective-permute-start(f32[54,16,128]{2,1,0:T(8,128)S(1)} %get-tuple-element.12), channel_id=1, source_target_pairs={{1,2},{2,1},{5,6},{6,5},{9,10},{10,9},{13,14},{14,13},{17,18},{18,... | collective-permute-start | bytes 1327112 | tf_op jit(solution)/shard_map/ppermute | solution.py:376
  5.8 0.0 copy-start.1
  5.8 0.1 edges.1
  5.9 1.6 %collective-permute-start.2 = (f32[432,128]{1,0:T(8,128)S(1)}, f32[432,128]{1,0:T(8,128)S(1)}, u32[]{:S(2)}, u32[]{:S(2)}) collective-permute-start(f32[432,128]{1,0:T(8,128)S(1)} %get-tuple-element.13), channel_id=1, source_target_pairs={{0,4},{1,5},{2,6},{3,7},{4,0},{5,1},{6,2},{7,3},{8,12},{9,13},{10,... | collective-permute-start | bytes 663560 | tf_op jit(solution)/shard_map/ppermute | solution.py:376
  7.4 3.9 %collective-permute-start.4 = (f32[128,128]{1,0:T(8,128)S(1)}, f32[128,128]{1,0:T(8,128)S(1)}, u32[]{:S(2)}, u32[]{:S(2)}) collective-permute-start(f32[128,128]{1,0:T(8,128)S(1)} %get-tuple-element.15), channel_id=1, source_target_pairs={{1,4},{2,5},{3,6},{4,1},{5,2},{6,3},{9,12},{10,13},{11,14},{12,9},... | collective-permute-start | bytes 196616 | tf_op jit(solution)/shard_map/ppermute | solution.py:376
  11.3 1.9 %collective-permute-start.3 = (f32[96,128]{1,0:T(8,128)S(1)}, f32[96,128]{1,0:T(8,128)S(1)}, u32[]{:S(2)}, u32[]{:S(2)}) collective-permute-start(f32[96,128]{1,0:T(8,128)S(1)} %get-tuple-element.14), channel_id=1, source_target_pairs={{0,5},{1,6},{2,7},{5,0},{6,1},{7,2},{8,13},{9,14},{10,15},{13,8},{... | collective-permute-start | bytes 147464 | tf_op jit(solution)/shard_map/ppermute | solution.py:376
  13.3 5.2 %collective-permute-done.3.rest_1_ = f32[96,128]{1,0:T(8,128)S(1)} collective-permute-done((f32[96,128]{1,0:T(8,128)S(1)}, f32[96,128]{1,0:T(8,128)S(1)}, u32[]{:S(2)}, u32[]{:S(2)}) %collective-permute-start.3) | collective-permute-done | bytes 49184 | tf_op jit(solution)/shard_map/ppermute | solution.py:376
  18.5 1.2 %collective-permute-done.4.rest_2_ = f32[128,128]{1,0:T(8,128)S(1)} collective-permute-done((f32[128,128]{1,0:T(8,128)S(1)}, f32[128,128]{1,0:T(8,128)S(1)}, u32[]{:S(2)}, u32[]{:S(2)}) %collective-permute-start.4) | collective-permute-done | bytes 65568 | tf_op jit(solution)/shard_map/ppermute | solution.py:376
  19.7 0.0 collective-permute-done.2.rest_0_
  19.7 0.0 collective-permute-done.y_a
  19.7 0.0 collective-permute-done.1.y_b
  19.7 0.0 copy-done.1
  19.7 3.2 %window.1 = (f32[3,8,16,128]{3,2,1,0:T(8,128)S(1)}, f32[16,512]{1,0:T(8,128)S(1)}) custom-call(f32[2,5]{1,0:T(2,128)} %bitcast.5, f32[3,4]{1,0:T(4,128)} %table_hbm.3, s32[2]{0:T(128)} %plane_hbm.1, s32[6]{0:T(128)} %box_hbm.1, f32[3,2,2048]{2,1,0:T(2,128)S(1)} %bitcast.4, f32[13,8,16,128]{3,2,1,0:T(8,128)S(1)} %get-tuple-element.10.tile, ...), custom_call_target="tpu_custom_call" | custom-call | tf_op jit(solution)/shard_map/window/pallas_call | solution.py:425
  22.9 0.0 copy-start
  23.0 0.7 %copy-done = f32[3,8,16,128]{3,2,1,0:T(8,128)} copy-done((f32[3,8,16,128]{3,2,1,0:T(8,128)}, f32[3,8,16,128]{3,2,1,0:T(8,128)S(1)}, u32[]{:S(2)}) %copy-start) | copy-done | bytes 196632
  23.6 1.5 %collective-permute-start.6 = (f32[16,512]{1,0:T(8,128)S(1)}, f32[16,512]{1,0:T(8,128)S(1)}, u32[]{:S(2)}, u32[]{:S(2)}) collective-permute-start(f32[16,512]{1,0:T(8,128)S(1)} %get-tuple-element.16), channel_id=1, source_target_pairs={{0,16},{8,24},{16,0},{24,8},{1,17},{9,25},{17,1},{25,9},{2,18},{10... | collective-permute-start | bytes 98312 | tf_op jit(solution)/shard_map/ppermute | solution.py:464
  25.1 0.0 collective-permute-start.7
  25.1 0.6 %collective-permute-start.5 = (f32[16,512]{1,0:T(8,128)S(1)}, f32[16,512]{1,0:T(8,128)S(1)}, u32[]{:S(2)}, u32[]{:S(2)}) collective-permute-start(f32[16,512]{1,0:T(8,128)S(1)} %get-tuple-element.16), channel_id=1, source_target_pairs={{0,8},{8,0},{16,24},{24,16},{1,9},{9,1},{17,25},{25,17},{2,10},{10... | collective-permute-start | bytes 98312 | tf_op jit(solution)/shard_map/ppermute | solution.py:464
  25.8 1.7 %emit.1 = f32[1,2,3,16,512]{4,3,2,1,0:T(8,128)} custom-call(f32[3,8,16,128]{3,2,1,0:T(8,128)} %copy-done), custom_call_target="tpu_custom_call" | custom-call | tf_op jit(solution)/shard_map/emit/pallas_call | solution.py:454
  27.5 0.1 collective-permute-done.6
  27.5 0.9 %collective-permute-done.7 = f32[16,512]{1,0:T(8,128)S(1)} collective-permute-done((f32[16,512]{1,0:T(8,128)S(1)}, f32[16,512]{1,0:T(8,128)S(1)}, u32[]{:S(2)}, u32[]{:S(2)}) %collective-permute-start.7) | collective-permute-done | bytes 32800 | tf_op jit(solution)/shard_map/ppermute | solution.py:464
  28.5 0.0 collective-permute-done.5
  28.5 0.6 %add_add_fusion = f32[16,512]{1,0:T(8,128)} fusion(f32[16,512]{1,0:T(8,128)S(1)} %collective-permute-done.6, f32[16,512]{1,0:T(8,128)S(1)} %collective-permute-done.7, f32[16,512]{1,0:T(8,128)S(1)} %get-tuple-element.16, f32[16,512]{1,0:T(8,128)S(1)} %collective-permute-done.5), kind=kLoop, calls=%fused_computation | loop fusion | flops 24576 | bytes 163840 | tf_op jit(solution)/shard_map/add | solution.py:466
Async XLA Ops:
  2.2 17.5 %collective-permute-start = (f32[54,16,128]{2,1,0:T(8,128)S(1)}, f32[54,16,128]{2,1,0:T(8,128)S(1)}, u32[]{:S(2)}, u32[]{:S(2)}) collective-permute-start(f32[54,16,128]{2,1,0:T(8,128)S(1)} %get-tuple-element.11), channel_id=1, source_target_pairs={{0,1},{1,0},{2,3},{3,2},{4,5},{5,4},{6,7},{7,6},{8,9},{9,8},{10,11... | collective-permute-start | bytes 1327112 | tf_op jit(solution)/shard_map/ppermute | solution.py:376
  3.9 15.9 %collective-permute-start.1 = (f32[54,16,128]{2,1,0:T(8,128)S(1)}, f32[54,16,128]{2,1,0:T(8,128)S(1)}, u32[]{:S(2)}, u32[]{:S(2)}) collective-permute-start(f32[54,16,128]{2,1,0:T(8,128)S(1)} %get-tuple-element.12), channel_id=1, source_target_pairs={{1,2},{2,1},{5,6},{6,5},{9,10},{10,9},{13,14},{14,13},{17,18},{18,... | collective-permute-start | bytes 1327112 | tf_op jit(solution)/shard_map/ppermute | solution.py:376
  5.8 13.9 %copy-start.1 = (f32[1,2,3,2048]{3,1,2,0:T(2,128)S(1)}, f32[1,2,3,2048]{3,1,2,0:T(2,128)}, u32[]{:S(2)}) copy-start(f32[1,2,3,2048]{3,1,2,0:T(2,128)} %param.9) | copy-start | bytes 147460
  5.9 13.8 %collective-permute-start.2 = (f32[432,128]{1,0:T(8,128)S(1)}, f32[432,128]{1,0:T(8,128)S(1)}, u32[]{:S(2)}, u32[]{:S(2)}) collective-permute-start(f32[432,128]{1,0:T(8,128)S(1)} %get-tuple-element.13), channel_id=1, source_target_pairs={{0,4},{1,5},{2,6},{3,7},{4,0},{5,1},{6,2},{7,3},{8,12},{9,13},{10,... | collective-permute-start | bytes 663560 | tf_op jit(solution)/shard_map/ppermute | solution.py:376
  7.4 12.3 %collective-permute-start.4 = (f32[128,128]{1,0:T(8,128)S(1)}, f32[128,128]{1,0:T(8,128)S(1)}, u32[]{:S(2)}, u32[]{:S(2)}) collective-permute-start(f32[128,128]{1,0:T(8,128)S(1)} %get-tuple-element.15), channel_id=1, source_target_pairs={{1,4},{2,5},{3,6},{4,1},{5,2},{6,3},{9,12},{10,13},{11,14},{12,9},... | collective-permute-start | bytes 196616 | tf_op jit(solution)/shard_map/ppermute | solution.py:376
  11.3 7.1 %collective-permute-start.3 = (f32[96,128]{1,0:T(8,128)S(1)}, f32[96,128]{1,0:T(8,128)S(1)}, u32[]{:S(2)}, u32[]{:S(2)}) collective-permute-start(f32[96,128]{1,0:T(8,128)S(1)} %get-tuple-element.14), channel_id=1, source_target_pairs={{0,5},{1,6},{2,7},{5,0},{6,1},{7,2},{8,13},{9,14},{10,15},{13,8},{... | collective-permute-start | bytes 147464 | tf_op jit(solution)/shard_map/ppermute | solution.py:376
  22.9 0.7 %copy-start = (f32[3,8,16,128]{3,2,1,0:T(8,128)}, f32[3,8,16,128]{3,2,1,0:T(8,128)S(1)}, u32[]{:S(2)}) copy-start(f32[3,8,16,128]{3,2,1,0:T(8,128)S(1)} %get-tuple-element.17.electric) | copy-start | bytes 589828
  23.6 3.9 %collective-permute-start.6 = (f32[16,512]{1,0:T(8,128)S(1)}, f32[16,512]{1,0:T(8,128)S(1)}, u32[]{:S(2)}, u32[]{:S(2)}) collective-permute-start(f32[16,512]{1,0:T(8,128)S(1)} %get-tuple-element.16), channel_id=1, source_target_pairs={{0,16},{8,24},{16,0},{24,8},{1,17},{9,25},{17,1},{25,9},{2,18},{10... | collective-permute-start | bytes 98312 | tf_op jit(solution)/shard_map/ppermute | solution.py:464
  25.1 3.3 %collective-permute-start.7 = (f32[16,512]{1,0:T(8,128)S(1)}, f32[16,512]{1,0:T(8,128)S(1)}, u32[]{:S(2)}, u32[]{:S(2)}) collective-permute-start(f32[16,512]{1,0:T(8,128)S(1)} %get-tuple-element.16), channel_id=1, source_target_pairs={{0,24},{8,16},{16,8},{24,0},{1,25},{9,17},{17,9},{25,1},{2,26},{10... | collective-permute-start | bytes 98312 | tf_op jit(solution)/shard_map/ppermute | solution.py:464
  25.1 3.3 %collective-permute-start.5 = (f32[16,512]{1,0:T(8,128)S(1)}, f32[16,512]{1,0:T(8,128)S(1)}, u32[]{:S(2)}, u32[]{:S(2)}) collective-permute-start(f32[16,512]{1,0:T(8,128)S(1)} %get-tuple-element.16), channel_id=1, source_target_pairs={{0,8},{8,0},{16,24},{24,16},{1,9},{9,1},{17,25},{25,17},{2,10},{10... | collective-permute-start | bytes 98312 | tf_op jit(solution)/shard_map/ppermute | solution.py:464

commit v3 on v2

--- a/solution.py
+++ b/solution.py
@@ -65,6 +65,10 @@
         drive = w * w * time_step / denom
         out.append(((1.0 - 0.25 * g) / denom, drive, drive * d))
     return [lambda m, i=i: out[m][i] for i in range(3)]
+
+
+def is_lower_in_a():
+    return lax.rem(lax.axis_index("ty") + lax.axis_index("wave"), 2) == 0
 
 
 def pack_kernel(table_hbm, fields_hbm, material_hbm, density_hbm, tile, y_a, y_b, table, fields, material, density, sems):
@@ -108,11 +112,11 @@
                 tile[6 + c, line] = p + time_step * j
                 tile[9 + c, line] = j
             tile[12, line] = mixed[half]
-    odd = lax.rem(lax.axis_index("ty"), 2) == 1
+    lower = is_lower_in_a()
     for i, (f, k) in enumerate(Y_ENTRIES):
         first, last = k, LINES - 1 - k
-        y_a[i] = tile[f, jnp.where(odd, first, last)]
-        y_b[i] = tile[f, jnp.where(odd, last, first)]
+        y_a[i] = tile[f, jnp.where(lower, last, first)]
+        y_b[i] = tile[f, jnp.where(lower, first, last)]
 
 
 def edge_kernel(tile, *messages):
@@ -160,7 +164,7 @@
     for copy in copies:
         copy.start()
     tx, ty = lax.axis_index("tx"), lax.axis_index("ty")
-    odd_x, odd_y = lax.rem(tx, 2), lax.rem(ty, 2)
+    odd_x = lax.rem(tx, 2)
     offset = PAD if wide else pl.multiple_of(tx * PAD, PAD)
     rows_base, lines_base = tx * ROWS - offset, ty * LINES - STEPS
     rows_all, lines_all = tx_count * ROWS, ty_count * LINES
@@ -181,15 +185,23 @@
     def line_at(ahead, k):
         return jnp.where(ahead, STEPS + LINES + k, STEPS - 1 - k)
 
-    for i, (f, k) in enumerate(Y_ENTRIES):
-        put(f, line_at(odd_y == 0, k), middle, y_a[i])
-        put(f, line_at(odd_y == 1, k), middle, y_b[i])
+    lower = is_lower_in_a()
+    for message, is_lower in ((y_a, lower), (y_b, jnp.logical_not(lower))):
+
+        @pl.when(jnp.where(is_lower, ty + 1 < ty_count, ty > 0))
+        def _(message=message, is_lower=is_lower):
+            for i, (f, k) in enumerate(Y_ENTRIES):
+                put(f, line_at(is_lower, k), middle, message[i])
+
     for kind in range(kinds):
         along, same, mixed = messages[3 * kind : 3 * kind + 3]
         for is_lower in (True, False):
 
-            @pl.when((odd_x == kind) == is_lower)
-            def _(is_lower=is_lower, along=along, same=same, mixed=mixed):
+            in_x = tx + 1 < tx_count if is_lower else tx > 0
+            behind, ahead = ty > 0, ty + 1 < ty_count
+
+            @pl.when(jnp.logical_and((odd_x == kind) == is_lower, in_x))
+            def _(is_lower=is_lower, along=along, same=same, mixed=mixed, behind=behind, ahead=ahead):
                 def unpack(message, entries, line_of):
                     for f, k, depth, start in entries:
                         if wide:
@@ -199,8 +211,15 @@
                         put(f, line_of(k), slice(first, first + depth), message[start : start + depth, :])
 
                 unpack(along, X_ENTRIES, lambda k: STEPS + k)
-                unpack(same, CORNERS[0][0], lambda k: STEPS + LINES + k if is_lower else STEPS - 1 - k)
-                unpack(mixed, CORNERS[1][0], lambda k: STEPS - 1 - k if is_lower else STEPS + LINES + k)
+
+                @pl.when(ahead if is_lower else behind)
+                def _():
+                    unpack(same, CORNERS[0][0], lambda k: STEPS + LINES + k if is_lower else STEPS - 1 - k)
+
+                @pl.when(behind if is_lower else ahead)
+                def _():
+                    unpack(mixed, CORNERS[1][0], lambda k: STEPS - 1 - k if is_lower else STEPS + LINES + k)
+
     for copy in copies:
         copy.wait()
     decay, drive, coupled = pole(table)
@@ -366,21 +385,31 @@
     vmem = pl.BlockSpec(memory_space=pltpu.VMEM)
     kinds = (0,) if tx_count == 2 else (0, 1)
 
+    waves = lax.axis_size("wave")
+
     def swap(value, partner):
+        def index(w, x, y):
+            return (w * tx_count + x) * ty_count + y
+
         pairs = []
-        for x in range(tx_count):
-            for y in range(ty_count):
-                other = partner(x, y)
-                if None not in other and 0 <= other[1] < ty_count:
-                    pairs.append((x * ty_count + y, other[0] * ty_count + other[1]))
-        return lax.ppermute(value, ("tx", "ty"), pairs)
+        for w in range(waves):
+            for x in range(tx_count):
+                for y in range(ty_count):
+                    ox, oy = partner(w, x, y)
+                    if ox is not None and oy is not None and 0 <= oy < ty_count:
+                        pairs.append((index(w, x, y), index(w, ox, oy)))
+                    elif waves % 2 == 0:
+                        pairs.append((index(w, x, y), index((w + waves // 2) % waves, x, y)))
+        return lax.ppermute(value, ("wave", "tx", "ty"), pairs)
+
+    def along_y(b):
+        return lambda w, x, y: (x, pair_of(y, (w + b) % 2, ty_count))
+
+    def along_x(kind):
+        return lambda w, x, y: (pair_of(x, kind, tx_count), y)
 
     def corner(kind, mixed):
-        def partner(x, y):
-            lower = x % 2 == kind
-            return pair_of(x, kind, tx_count), y + (1 if lower != mixed else -1)
-
-        return partner
+        return lambda w, x, y: (pair_of(x, kind, tx_count), y + (1 if (x % 2 == kind) != mixed else -1))
 
     tile, y_a, y_b = pl.pallas_call(
         pack_kernel,
@@ -401,8 +430,7 @@
         compiler_params=pltpu.CompilerParams(vmem_limit_bytes=32 * 1024 * 1024),
         name="pack",
     )(*[in_hbm(v) for v in (material_table, initial_fields, material_map, design_density)])
-    y_a = swap(y_a, lambda x, y: (x, pair_of(y, 0, ty_count)))
-    y_b = swap(y_b, lambda x, y: (x, pair_of(y, 1, ty_count)))
+    y_a, y_b = swap(y_a, along_y(0)), swap(y_b, along_y(1))
 
     sizes = (X_ROWS, CORNERS[0][1], CORNERS[1][1]) * len(kinds)
     messages = pl.pallas_call(
@@ -416,10 +444,7 @@
     arrived = []
     for i, message in enumerate(messages):
         kind = i // 3
-        if i % 3 == 0:
-            arrived.append(swap(message, lambda x, y, kind=kind: (pair_of(x, kind, tx_count), y)))
-        else:
-            arrived.append(swap(message, corner(kind, i % 3 == 2)))
+        arrived.append(swap(message, along_x(kind) if i % 3 == 0 else corner(kind, i % 3 == 2)))
 
     ext = (EXT_LINES, ROWS + (PAD if tx_count == 2 else 2 * PAD), LANES)
     electric, partial = pl.pallas_call(
@@ -456,6 +481,7 @@
         out_shape=f32(1, 2, 3, ROWS, LINES * NZ),
         in_specs=[vmem],
         out_specs=vmem,
+        compiler_params=pltpu.CompilerParams(vmem_limit_bytes=8 * 1024 * 1024),
         name="emit",
     )(electric)
 

time: 29.4 us -> 28.1 us (0.956)
  the two profiles are of different devices: /device:TPU:16 before, /device:TPU:0 now
where the time goes in v3:
time: 28.1 us; the launch traced here: 27.9 us
  starting transfers between devices  10.9 us (39%)
  waiting for transfers between devices  10 us (36%)
  Pallas kernels  5.66 us (20%)
  between operations  0.68 us (2%)
  other arithmetic  0.63 us (2%)
    ppermute x5, starting transfers between devices, swap(): return lax.ppermute(value, ('wave', 'tx', 'ty'), pairs)  8.69 us
    ppermute x5, waiting for transfers between devices, swap(): return lax.ppermute(value, ('wave', 'tx', 'ty'), pairs)  7.67 us
    pallas_call x1, Pallas kernels, on_device(): pl.pallas_call(functools.partial(window_kernel, tx_count, ty_count), out_...  3.22 us
    ppermute x3, waiting for transfers between devices, on_device(): lax.ppermute(partial, 'wave', [(i, i ^ k) for i in range(4)])  2.37 us
    ppermute x3, starting transfers between devices, on_device(): lax.ppermute(partial, 'wave', [(i, i ^ k) for i in range(4)])  2.21 us
    pallas_call x1, Pallas kernels, on_device(): pl.pallas_call(pack_kernel, out_shape=(f32(FIELDS, LINES, ROWS, LANES), f...  1.58 us
    pallas_call x1, Pallas kernels, on_device(): pl.pallas_call(emit_kernel, out_shape=f32(1, 2, 3, ROWS, LINES * NZ), in_...  0.79 us
    add x1, other arithmetic, on_device(): gradient = partial + one + (two + three)  0.63 us
  transfers between devices with their start and end apart: 8, of which 3 were waited for; matrix products, arithmetic and copies ran while one was open for 0% of the time, Pallas kernels for 3%

profile of v3, /device:TPU:0, one launch (start us, length us, event | category | flops | bytes accessed | tf_op | source)
XLA Modules:
  0.0 27.9 jit_solution(1534821958765784966)
XLA Ops:
  0.6 1.6 %pack.1 = (f32[13,8,16,128]{3,2,1,0:T(8,128)S(1)}, f32[54,16,128]{2,1,0:T(8,128)S(1)}, f32[54,16,128]{2,1,0:T(8,128)S(1)}) custom-call(f32[3,4]{1,0:T(4,128)} %table_hbm.3, f32[1,2,12,16,512]{4,3,2,1,0:T(8,128)} %fields_hbm.1, s32[16,512]{1,0:T(8,128)} %material_hbm.1, f32[16,512]{1,0:T(8,128)} %density_hbm.1), custom_call_target="tpu_custom_call" | custom-call | tf_op jit(solution)/shard_map/pack/pallas_call | solution.py:414
  2.2 3.1 %collective-permute-start = (f32[54,16,128]{2,1,0:T(8,128)S(1)}, f32[54,16,128]{2,1,0:T(8,128)S(1)}, u32[]{:S(2)}, u32[]{:S(2)}) collective-permute-start(f32[54,16,128]{2,1,0:T(8,128)S(1)} %get-tuple-element.11), channel_id=1, source_target_pairs={{0,1},{1,0},{2,3},{3,2},{4,5},{5,4},{6,7},{7,6},{8,24},{9,10},{10,... | collective-permute-start | bytes 1327112 | tf_op jit(solution)/shard_map/ppermute | solution.py:403
  5.3 1.5 %collective-permute-start.1 = (f32[54,16,128]{2,1,0:T(8,128)S(1)}, f32[54,16,128]{2,1,0:T(8,128)S(1)}, u32[]{:S(2)}, u32[]{:S(2)}) collective-permute-start(f32[54,16,128]{2,1,0:T(8,128)S(1)} %get-tuple-element.12), channel_id=1, source_target_pairs={{0,16},{1,2},{2,1},{3,19},{4,20},{5,6},{6,5},{7,23},{8,9},{9,8},{1... | collective-permute-start | bytes 1327112 | tf_op jit(solution)/shard_map/ppermute | solution.py:403
  6.8 0.0 copy-start
  6.8 0.1 edges.1
  6.9 1.6 %collective-permute-start.2 = (f32[432,128]{1,0:T(8,128)S(1)}, f32[432,128]{1,0:T(8,128)S(1)}, u32[]{:S(2)}, u32[]{:S(2)}) collective-permute-start(f32[432,128]{1,0:T(8,128)S(1)} %get-tuple-element.13), channel_id=1, source_target_pairs={{0,4},{1,5},{2,6},{3,7},{4,0},{5,1},{6,2},{7,3},{8,12},{9,13},{10,... | collective-permute-start | bytes 663560 | tf_op jit(solution)/shard_map/ppermute | solution.py:403
  8.5 0.5 %collective-permute-start.4 = (f32[128,128]{1,0:T(8,128)S(1)}, f32[128,128]{1,0:T(8,128)S(1)}, u32[]{:S(2)}, u32[]{:S(2)}) collective-permute-start(f32[128,128]{1,0:T(8,128)S(1)} %get-tuple-element.15), channel_id=1, source_target_pairs={{0,16},{1,4},{2,5},{3,6},{4,1},{5,2},{6,3},{7,23},{8,24},{9,12},{1... | collective-permute-start | bytes 196616 | tf_op jit(solution)/shard_map/ppermute | solution.py:403
  9.0 2.0 %collective-permute-start.3 = (f32[96,128]{1,0:T(8,128)S(1)}, f32[96,128]{1,0:T(8,128)S(1)}, u32[]{:S(2)}, u32[]{:S(2)}) collective-permute-start(f32[96,128]{1,0:T(8,128)S(1)} %get-tuple-element.14), channel_id=1, source_target_pairs={{0,5},{1,6},{2,7},{3,19},{4,20},{5,0},{6,1},{7,2},{8,13},{9,14},{1... | collective-permute-start | bytes 147464 | tf_op jit(solution)/shard_map/ppermute | solution.py:403
  11.0 7.7 %collective-permute-done.3.rest_1_ = f32[96,128]{1,0:T(8,128)S(1)} collective-permute-done((f32[96,128]{1,0:T(8,128)S(1)}, f32[96,128]{1,0:T(8,128)S(1)}, u32[]{:S(2)}, u32[]{:S(2)}) %collective-permute-start.3) | collective-permute-done | bytes 49184 | tf_op jit(solution)/shard_map/ppermute | solution.py:403
  18.7 0.0 collective-permute-done.4.rest_2_
  18.7 0.0 collective-permute-done.2.rest_0_
  18.7 0.0 collective-permute-done.y_a
  18.7 0.0 collective-permute-done.1.y_b
  18.7 0.0 copy-done
  18.7 3.2 %window.1 = (f32[3,8,16,128]{3,2,1,0:T(8,128)S(1)}, f32[16,512]{1,0:T(8,128)S(1)}) custom-call(f32[2,5]{1,0:T(2,128)} %bitcast.5, f32[3,4]{1,0:T(4,128)} %table_hbm.3, s32[2]{0:T(128)} %plane_hbm.1, s32[6]{0:T(128)} %box_hbm.1, f32[3,2,2048]{2,1,0:T(2,128)S(1)} %bitcast.4, f32[13,8,16,128]{3,2,1,0:T(8,128)S(1)} %get-tuple-element.10.tile, ...), custom_call_target="tpu_custom_call" | custom-call | tf_op jit(solution)/shard_map/window/pallas_call | solution.py:450
  21.9 1.7 %collective-permute-start.6 = (f32[16,512]{1,0:T(8,128)S(1)}, f32[16,512]{1,0:T(8,128)S(1)}, u32[]{:S(2)}, u32[]{:S(2)}) collective-permute-start(f32[16,512]{1,0:T(8,128)S(1)} %get-tuple-element.16), channel_id=1, source_target_pairs={{0,16},{8,24},{16,0},{24,8},{1,17},{9,25},{17,1},{25,9},{2,18},{10... | collective-permute-start | bytes 98312 | tf_op jit(solution)/shard_map/ppermute | solution.py:490
  23.6 0.0 collective-permute-start.7
  23.6 0.5 %collective-permute-start.5 = (f32[16,512]{1,0:T(8,128)S(1)}, f32[16,512]{1,0:T(8,128)S(1)}, u32[]{:S(2)}, u32[]{:S(2)}) collective-permute-start(f32[16,512]{1,0:T(8,128)S(1)} %get-tuple-element.16), channel_id=1, source_target_pairs={{0,8},{8,0},{16,24},{24,16},{1,9},{9,1},{17,25},{25,17},{2,10},{10... | collective-permute-start | bytes 98312 | tf_op jit(solution)/shard_map/ppermute | solution.py:490
  24.1 0.8 %emit.1 = f32[1,2,3,16,512]{4,3,2,1,0:T(8,128)} custom-call(f32[3,8,16,128]{3,2,1,0:T(8,128)S(1)} %get-tuple-element.17.electric), custom_call_target="tpu_custom_call" | custom-call | tf_op jit(solution)/shard_map/emit/pallas_call | solution.py:479
  24.9 1.0 %collective-permute-done.6 = f32[16,512]{1,0:T(8,128)S(1)} collective-permute-done((f32[16,512]{1,0:T(8,128)S(1)}, f32[16,512]{1,0:T(8,128)S(1)}, u32[]{:S(2)}, u32[]{:S(2)}) %collective-permute-start.6) | collective-permute-done | bytes 32800 | tf_op jit(solution)/shard_map/ppermute | solution.py:490
  25.9 1.4 %collective-permute-done.7 = f32[16,512]{1,0:T(8,128)S(1)} collective-permute-done((f32[16,512]{1,0:T(8,128)S(1)}, f32[16,512]{1,0:T(8,128)S(1)}, u32[]{:S(2)}, u32[]{:S(2)}) %collective-permute-start.7) | collective-permute-done | bytes 32800 | tf_op jit(solution)/shard_map/ppermute | solution.py:490
  27.3 0.0 collective-permute-done.5
  27.3 0.6 %add_add_fusion = f32[16,512]{1,0:T(8,128)} fusion(f32[16,512]{1,0:T(8,128)S(1)} %collective-permute-done.6, f32[16,512]{1,0:T(8,128)S(1)} %collective-permute-done.7, f32[16,512]{1,0:T(8,128)S(1)} %get-tuple-element.16, f32[16,512]{1,0:T(8,128)S(1)} %collective-permute-done.5), kind=kLoop, calls=%fused_computation | loop fusion | flops 24576 | bytes 163840 | tf_op jit(solution)/shard_map/add | solution.py:492
Async XLA Ops:
  2.2 16.4 %collective-permute-start = (f32[54,16,128]{2,1,0:T(8,128)S(1)}, f32[54,16,128]{2,1,0:T(8,128)S(1)}, u32[]{:S(2)}, u32[]{:S(2)}) collective-permute-start(f32[54,16,128]{2,1,0:T(8,128)S(1)} %get-tuple-element.11), channel_id=1, source_target_pairs={{0,1},{1,0},{2,3},{3,2},{4,5},{5,4},{6,7},{7,6},{8,24},{9,10},{10,... | collective-permute-start | bytes 1327112 | tf_op jit(solution)/shard_map/ppermute | solution.py:403
  5.3 13.4 %collective-permute-start.1 = (f32[54,16,128]{2,1,0:T(8,128)S(1)}, f32[54,16,128]{2,1,0:T(8,128)S(1)}, u32[]{:S(2)}, u32[]{:S(2)}) collective-permute-start(f32[54,16,128]{2,1,0:T(8,128)S(1)} %get-tuple-element.12), channel_id=1, source_target_pairs={{0,16},{1,2},{2,1},{3,19},{4,20},{5,6},{6,5},{7,23},{8,9},{9,8},{1... | collective-permute-start | bytes 1327112 | tf_op jit(solution)/shard_map/ppermute | solution.py:403
  6.8 11.8 %copy-start = (f32[1,2,3,2048]{3,1,2,0:T(2,128)S(1)}, f32[1,2,3,2048]{3,1,2,0:T(2,128)}, u32[]{:S(2)}) copy-start(f32[1,2,3,2048]{3,1,2,0:T(2,128)} %param.9) | copy-start | bytes 147460
  6.9 11.8 %collective-permute-start.2 = (f32[432,128]{1,0:T(8,128)S(1)}, f32[432,128]{1,0:T(8,128)S(1)}, u32[]{:S(2)}, u32[]{:S(2)}) collective-permute-start(f32[432,128]{1,0:T(8,128)S(1)} %get-tuple-element.13), channel_id=1, source_target_pairs={{0,4},{1,5},{2,6},{3,7},{4,0},{5,1},{6,2},{7,3},{8,12},{9,13},{10,... | collective-permute-start | bytes 663560 | tf_op jit(solution)/shard_map/ppermute | solution.py:403
  8.5 10.2 %collective-permute-start.4 = (f32[128,128]{1,0:T(8,128)S(1)}, f32[128,128]{1,0:T(8,128)S(1)}, u32[]{:S(2)}, u32[]{:S(2)}) collective-permute-start(f32[128,128]{1,0:T(8,128)S(1)} %get-tuple-element.15), channel_id=1, source_target_pairs={{0,16},{1,4},{2,5},{3,6},{4,1},{5,2},{6,3},{7,23},{8,24},{9,12},{1... | collective-permute-start | bytes 196616 | tf_op jit(solution)/shard_map/ppermute | solution.py:403
  9.0 9.7 %collective-permute-start.3 = (f32[96,128]{1,0:T(8,128)S(1)}, f32[96,128]{1,0:T(8,128)S(1)}, u32[]{:S(2)}, u32[]{:S(2)}) collective-permute-start(f32[96,128]{1,0:T(8,128)S(1)} %get-tuple-element.14), channel_id=1, source_target_pairs={{0,5},{1,6},{2,7},{3,19},{4,20},{5,0},{6,1},{7,2},{8,13},{9,14},{1... | collective-permute-start | bytes 147464 | tf_op jit(solution)/shard_map/ppermute | solution.py:403
  21.9 4.0 %collective-permute-start.6 = (f32[16,512]{1,0:T(8,128)S(1)}, f32[16,512]{1,0:T(8,128)S(1)}, u32[]{:S(2)}, u32[]{:S(2)}) collective-permute-start(f32[16,512]{1,0:T(8,128)S(1)} %get-tuple-element.16), channel_id=1, source_target_pairs={{0,16},{8,24},{16,0},{24,8},{1,17},{9,25},{17,1},{25,9},{2,18},{10... | collective-permute-start | bytes 98312 | tf_op jit(solution)/shard_map/ppermute | solution.py:490
  23.6 3.7 %collective-permute-start.7 = (f32[16,512]{1,0:T(8,128)S(1)}, f32[16,512]{1,0:T(8,128)S(1)}, u32[]{:S(2)}, u32[]{:S(2)}) collective-permute-start(f32[16,512]{1,0:T(8,128)S(1)} %get-tuple-element.16), channel_id=1, source_target_pairs={{0,24},{8,16},{16,8},{24,0},{1,25},{9,17},{17,9},{25,1},{2,26},{10... | collective-permute-start | bytes 98312 | tf_op jit(solution)/shard_map/ppermute | solution.py:490
  23.6 3.7 %collective-permute-start.5 = (f32[16,512]{1,0:T(8,128)S(1)}, f32[16,512]{1,0:T(8,128)S(1)}, u32[]{:S(2)}, u32[]{:S(2)}) collective-permute-start(f32[16,512]{1,0:T(8,128)S(1)} %get-tuple-element.16), channel_id=1, source_target_pairs={{0,8},{8,0},{16,24},{24,16},{1,9},{9,1},{17,25},{25,17},{2,10},{10... | collective-permute-start | bytes 98312 | tf_op jit(solution)/shard_map/ppermute | solution.py:490

commit v4 on v3

--- a/solution.py
+++ b/solution.py
@@ -21,27 +21,50 @@
 time_step = 0.5
 contrast = 2.0
 
-LINE_DEPTH = (5, 5, 5, 5, 4, 5, 3, 3, 3, 4, 4, 4, 4)
-ROW_DEPTH = (5, 5, 5, 4, 5, 5, 3, 3, 3, 4, 4, 4, 4)
-SAME_DEPTH = (4, 4, 4, 4, 4, 4, 2, 2, 2, 3, 3, 3, 3)
-MIXED_DEPTH = (5, 5, 4, 4, 4, 4, 3, 3, 2, 4, 4, 3, 4)
-
-Y_ENTRIES = [(f, k) for f in range(FIELDS) for k in range(LINE_DEPTH[f])]
-
-
-def listed(entries):
+BEHIND_LINES = (4, 4, 4, 5, 4, 5, 2, 2, 2, 3, 3, 3, 4)
+AHEAD_LINES = (4, 3, 4, 4, 4, 4, 2, 1, 2, 3, 2, 3, 4)
+BEHIND_ROWS = (4, 4, 4, 4, 5, 5, 2, 2, 2, 3, 3, 3, 4)
+AHEAD_ROWS = (3, 4, 4, 4, 4, 4, 1, 2, 2, 2, 3, 3, 4)
+BEHIND_BOTH = (3, 3, 3, 4, 4, 4, 1, 1, 1, 2, 2, 2, 3)
+AHEAD_BOTH = (3, 3, 3, 3, 3, 3, 1, 1, 1, 2, 2, 2, 3)
+AHEAD_ROW_BEHIND_LINE = (3, 4, 3, 4, 3, 4, 1, 2, 1, 2, 3, 2, 4)
+BEHIND_ROW_AHEAD_LINE = (4, 3, 3, 3, 4, 4, 2, 1, 1, 3, 2, 2, 4)
+BORDER = 5
+
+
+def line_entries(depth):
+    return [(f, k) for f in range(FIELDS) for k in range(depth[f])]
+
+
+def row_entries(entries):
     start, out = 0, []
     for f, k, depth in entries:
         out.append((f, k, depth, start))
         start += depth
-    return out, (start + 7) // 8 * 8
-
-
-X_ENTRIES, X_ROWS = listed([(f, line, ROW_DEPTH[f]) for f in range(FIELDS) for line in range(LINES)])
-CORNERS = [
-    listed([(f, k, depth[f] - k) for f in range(FIELDS) for k in range(depth[f])])
-    for depth in (SAME_DEPTH, MIXED_DEPTH)
-]
+    return out, start
+
+
+def corner_entries(depth):
+    return row_entries([(f, k, depth[f] - k) for f in range(FIELDS) for k in range(depth[f])])
+
+
+Y_ENTRIES = {False: line_entries(BEHIND_LINES), True: line_entries(AHEAD_LINES)}
+Y_SIZE = max(len(Y_ENTRIES[False]) + 1, len(Y_ENTRIES[True]) + 3)
+X_ENTRIES = {
+    ahead: row_entries([(f, line, depth[f]) for f in range(FIELDS) for line in range(LINES)])
+    for ahead, depth in ((False, BEHIND_ROWS), (True, AHEAD_ROWS))
+}
+SAME_ENTRIES = {False: corner_entries(BEHIND_BOTH), True: corner_entries(AHEAD_BOTH)}
+MIXED_ENTRIES = {False: corner_entries(BEHIND_ROW_AHEAD_LINE), True: corner_entries(AHEAD_ROW_BEHIND_LINE)}
+
+
+def round_up(n):
+    return (n + 7) // 8 * 8
+
+
+X_SIZE = round_up(max(X_ENTRIES[False][1] + 2 * BORDER, X_ENTRIES[True][1] + 2 * BORDER + 2 * LINES))
+SAME_SIZE = round_up(max(SAME_ENTRIES[False][1], SAME_ENTRIES[True][1] + 16))
+MIXED_SIZE = round_up(max(MIXED_ENTRIES[ahead][1] + 2 * BORDER for ahead in (False, True)))
 
 
 def low_lanes(shape):
@@ -71,11 +94,28 @@
     return lax.rem(lax.axis_index("ty") + lax.axis_index("wave"), 2) == 0
 
 
-def pack_kernel(table_hbm, fields_hbm, material_hbm, density_hbm, tile, y_a, y_b, table, fields, material, density, sems):
+def pack_kernel(
+    table_hbm,
+    box_hbm,
+    fields_hbm,
+    material_hbm,
+    density_hbm,
+    tile,
+    start,
+    y_a,
+    y_b,
+    table,
+    box,
+    fields,
+    material,
+    density,
+    sems,
+):
     copies = [
-        pltpu.make_async_copy(table_hbm, table, sems.at[CHUNKS]),
-        pltpu.make_async_copy(material_hbm, material, sems.at[CHUNKS + 1]),
-        pltpu.make_async_copy(density_hbm, density, sems.at[CHUNKS + 2]),
+        pltpu.make_async_copy(src, dst, sems.at[CHUNKS + i])
+        for i, (src, dst) in enumerate(
+            [(table_hbm, table), (box_hbm, box), (material_hbm, material), (density_hbm, density)]
+        )
     ]
     chunks = [
         pltpu.make_async_copy(
@@ -88,7 +128,15 @@
     for copy in copies:
         copy.wait()
     decay, drive, coupled = pole(table)
-    low = low_lanes((ROWS, LANES))
+    shape = (ROWS, LANES)
+    low = low_lanes(shape)
+    lane = lax.broadcasted_iota(jnp.int32, shape, 1)
+    depth_id = jnp.where(low, lane, lane - NZ)
+    last_z = depth_id == NZ - 1
+    row = lax.broadcasted_iota(jnp.int32, shape, 0) + lax.axis_index("tx") * ROWS
+    in_z = (depth_id >= box[4]) & (depth_id < box[5])
+    design_rows = ((row >= box[0]) & (row < box[1]) & in_z).astype(jnp.float32)
+    first_line = lax.axis_index("ty") * LINES
     for k in range(CHUNKS):
         at = slice(k * LANES, (k + 1) * LANES)
         chunks[k].wait()
@@ -100,41 +148,107 @@
         mat, dens = material[:, at].astype(jnp.float32), density[:, at]
         turned = half_turn(mat)
         mats = (jnp.where(low, mat, turned), jnp.where(low, turned, mat))
-        mixed = split(mat, dens)
+        turned = half_turn(dens)
+        denses = (jnp.where(low, dens, turned), jnp.where(low, turned, dens))
         for half in range(2):
             line = 2 * k + half
-            dec, dri, cou = [choose(mats[half], column) for column in (decay, drive, coupled)]
+            mat, dens = mats[half], denses[half]
+            where = first_line + line
+            design = design_rows * ((where >= box[2]) & (where < box[3])).astype(jnp.float32)
+            permittivity = choose(mat, lambda m: table[m, 0]) + design * dens * contrast
+            reach = time_step / permittivity
+            dec, dri, cou = [choose(mat, column) for column in (decay, drive, coupled)]
             for c in range(3):
                 e, p, j = pairs[c][half], pairs[6 + c][half], pairs[9 + c][half]
                 j = dec * j + cou * e - dri * p
-                tile[c, line] = e
+                p = p + time_step * j
+                start[c, line] = e
+                tile[c, line] = e - reach * j
                 tile[3 + c, line] = pairs[3 + c][half]
-                tile[6 + c, line] = p + time_step * j
-                tile[9 + c, line] = j
-            tile[12, line] = mixed[half]
+                tile[6 + c, line] = p
+                tile[9 + c, line] = dec * j - dri * p
+            tile[12, line] = jnp.where(low, mat, dens)
+
+    edge = jnp.zeros((1, LANES), jnp.float32)
+
+    def ahead_row(v):
+        return jnp.concatenate([v[1:], edge], axis=0)
+
+    def ahead_depth(v):
+        return jnp.where(last_z, 0.0, pltpu.roll(v, LANES - 1, 1))
+
+    for line in range(LINES):
+        ex, ey, ez = [start[c, line] for c in range(3)]
+        if line + 1 < LINES:
+            ex_next, ez_next = start[0, line + 1], start[2, line + 1]
+        else:
+            ex_next = ez_next = jnp.zeros(shape, jnp.float32)
+        tile[3, line] = tile[3, line] - time_step * ((ez_next - ez) - (ahead_depth(ey) - ey))
+        tile[4, line] = tile[4, line] - time_step * ((ahead_depth(ex) - ex) - (ahead_row(ez) - ez))
+        tile[5, line] = tile[5, line] - time_step * ((ahead_row(ey) - ey) - (ex_next - ex))
+
     lower = is_lower_in_a()
-    for i, (f, k) in enumerate(Y_ENTRIES):
-        first, last = k, LINES - 1 - k
-        y_a[i] = tile[f, jnp.where(lower, last, first)]
-        y_b[i] = tile[f, jnp.where(lower, first, last)]
-
-
-def edge_kernel(tile, *messages):
+    for message, is_lower in ((y_a, lower), (y_b, jnp.logical_not(lower))):
+        for ahead in (False, True):
+
+            @pl.when(is_lower != ahead)
+            def _(message=message, ahead=ahead):
+                def line_of(k):
+                    return k if ahead else LINES - 1 - k
+
+                entries = Y_ENTRIES[ahead]
+                for i, (f, k) in enumerate(entries):
+                    message[i] = tile[f, line_of(k)]
+                last = len(entries)
+                for k in range(4 if ahead else 5):
+                    message[last, k : k + 1, :] = start[1, line_of(k), 0:1, :]
+                    message[last, 5 + k : 6 + k, :] = start[2, line_of(k), 0:1, :]
+                if ahead:
+                    message[last + 1] = start[0, 0]
+                    message[last + 2] = start[2, 0]
+
+
+def edge_kernel(tile, start, *messages):
     odd = lax.rem(lax.axis_index("tx"), 2)
     for kind in range(len(messages) // 3):
         along, same, mixed = messages[3 * kind : 3 * kind + 3]
-        for is_lower in (True, False):
-
-            @pl.when((odd == kind) == is_lower)
-            def _(is_lower=is_lower, along=along, same=same, mixed=mixed):
+        for ahead in (False, True):
+
+            @pl.when((odd == kind) != ahead)
+            def _(ahead=ahead, along=along, same=same, mixed=mixed):
+                def rows(depth):
+                    return slice(0, depth) if ahead else slice(ROWS - depth, ROWS)
+
                 def pack(message, entries, line_of):
-                    for f, k, depth, start in entries:
-                        rows = slice(ROWS - depth, ROWS) if is_lower else slice(0, depth)
-                        message[start : start + depth, :] = tile[f, line_of(k), rows, :]
-
-                pack(along, X_ENTRIES, lambda k: k)
-                pack(same, CORNERS[0][0], lambda k: LINES - 1 - k if is_lower else k)
-                pack(mixed, CORNERS[1][0], lambda k: k if is_lower else LINES - 1 - k)
+                    for f, k, depth, at in entries[0]:
+                        message[at : at + depth, :] = tile[f, line_of(k), rows(depth), :]
+                    return entries[1]
+
+                def pack_first_line(message, at, depth):
+                    for c in (0, 2):
+                        message[at : at + depth, :] = start[c, 0, rows(depth), :]
+                        at += depth
+                    return at
+
+                def pack_first_row(message, at, lines):
+                    for c in (1, 2):
+                        for line in lines:
+                            message[at : at + 1, :] = start[c, line, 0:1, :]
+                            at += 1
+
+                at = pack(along, X_ENTRIES[ahead], lambda k: k)
+                at = pack_first_line(along, at, BORDER)
+                if ahead:
+                    pack_first_row(along, at, range(LINES))
+                at = pack(same, SAME_ENTRIES[ahead], lambda k: k if ahead else LINES - 1 - k)
+                if ahead:
+                    at = pack_first_line(same, at, 4)
+                    pack_first_row(same, at, range(4))
+                at = pack(mixed, MIXED_ENTRIES[ahead], lambda k: LINES - 1 - k if ahead else k)
+                if ahead:
+                    pack_first_row(mixed, at, [LINES - 1 - k for k in range(BORDER)])
+                else:
+                    pack_first_line(mixed, at, BORDER)
 
 
 def window_kernel(
@@ -146,13 +260,14 @@
     box_hbm,
     profiles,
     tile,
+    start,
     y_a,
     y_b,
     *rest,
 ):
     kinds = 1 if tx_count == 2 else 2
     messages, rest = rest[: 3 * kinds], rest[3 * kinds :]
-    electric_out, gradient_out, E, H, Pol, J, C, coef, source, waveforms, table, plane, box, sems = rest
+    electric_out, gradient_out, E, H, Pol, J, C, coef, source, first_row, waveforms, table, plane, box, sems = rest
     wide = tx_count != 2
     ext_rows = E[0].shape[2]
     copies = [
@@ -172,53 +287,131 @@
 
     def put(f, line, rows, value):
         if f < 12:
-            (E[0], H[0], Pol[0], J[0])[f // 3][f % 3, line, rows, :] = value
+            (E[0], H[1], Pol[0], J[0])[f // 3][f % 3, line, rows, :] = value
         else:
             C[line, rows, :] = value
 
-    for ref in (E[0], H[0], Pol[0], J[0], C):
-        ref[...] = jnp.zeros(ref.shape, jnp.float32)
+    def clear(lines, rows, count):
+        for f in range(FIELDS):
+            for line in lines:
+                put(f, line, rows, jnp.zeros((count, LANES), jnp.float32))
+
+    every_row, behind_lines, ahead_lines = slice(0, ext_rows), range(STEPS), range(STEPS + LINES, EXT_LINES)
+    no_behind, no_ahead = ty == 0, ty + 1 == ty_count
+    if wide:
+
+        @pl.when(tx == 0)
+        def _():
+            clear(range(EXT_LINES), slice(0, PAD), PAD)
+
+        @pl.when(tx + 1 == tx_count)
+        def _():
+            clear(range(EXT_LINES), slice(PAD + ROWS, ext_rows), PAD)
+
+    @pl.when(no_behind)
+    def _():
+        clear(behind_lines, every_row, ext_rows)
+
+    @pl.when(no_ahead)
+    def _():
+        clear(ahead_lines, every_row, ext_rows)
+
     for f in range(FIELDS):
         for line in range(LINES):
             put(f, STEPS + line, middle, tile[f, line])
 
-    def line_at(ahead, k):
-        return jnp.where(ahead, STEPS + LINES + k, STEPS - 1 - k)
+    def near(ahead, k):
+        return STEPS + LINES + k if ahead else STEPS - 1 - k
+
+    def correct_line(line, rows, ex, ez):
+        H[1][0, line, rows, :] = H[1][0, line, rows, :] - time_step * ez
+        H[1][2, line, rows, :] = H[1][2, line, rows, :] + time_step * ex
+
+    def correct_row(line, row, ey, ez):
+        at = slice(row, row + 1)
+        H[1][1, line, at, :] = H[1][1, line, at, :] + time_step * ez
+        H[1][2, line, at, :] = H[1][2, line, at, :] - time_step * ey
 
     lower = is_lower_in_a()
     for message, is_lower in ((y_a, lower), (y_b, jnp.logical_not(lower))):
-
-        @pl.when(jnp.where(is_lower, ty + 1 < ty_count, ty > 0))
-        def _(message=message, is_lower=is_lower):
-            for i, (f, k) in enumerate(Y_ENTRIES):
-                put(f, line_at(is_lower, k), middle, message[i])
+        for ahead in (False, True):
+
+            @pl.when(jnp.logical_and(is_lower == ahead, jnp.logical_not(no_ahead if ahead else no_behind)))
+            def _(message=message, ahead=ahead):
+                entries = Y_ENTRIES[ahead]
+                for i, (f, k) in enumerate(entries):
+                    put(f, near(ahead, k), middle, message[i])
+                last = len(entries)
+                for k in range(4 if ahead else 5):
+                    first_row[0, near(ahead, k) : near(ahead, k) + 1, :] = message[last, k : k + 1, :]
+                    first_row[1, near(ahead, k) : near(ahead, k) + 1, :] = message[last, 5 + k : 6 + k, :]
+                if ahead:
+                    correct_line(STEPS + LINES - 1, middle, message[last + 1], message[last + 2])
+                else:
+                    correct_line(STEPS - 1, middle, start[0, 0], start[2, 0])
 
     for kind in range(kinds):
         along, same, mixed = messages[3 * kind : 3 * kind + 3]
-        for is_lower in (True, False):
-
-            in_x = tx + 1 < tx_count if is_lower else tx > 0
-            behind, ahead = ty > 0, ty + 1 < ty_count
-
-            @pl.when(jnp.logical_and((odd_x == kind) == is_lower, in_x))
-            def _(is_lower=is_lower, along=along, same=same, mixed=mixed, behind=behind, ahead=ahead):
+        for ahead in (False, True):
+            in_x = tx + 1 < tx_count if ahead else tx > 0
+            halo = ROWS + (PAD if wide else 0) if ahead else PAD
+            last_row = halo - 1
+
+            @pl.when(jnp.logical_and((odd_x == kind) == ahead, in_x))
+            def _(ahead=ahead, along=along, same=same, mixed=mixed, halo=halo, last_row=last_row):
+                def rows(depth):
+                    return slice(halo, halo + depth) if ahead else slice(halo - depth, halo)
+
                 def unpack(message, entries, line_of):
-                    for f, k, depth, start in entries:
-                        if wide:
-                            first = PAD + ROWS if is_lower else PAD - depth
-                        else:
-                            first = ROWS if is_lower else PAD - depth
-                        put(f, line_of(k), slice(first, first + depth), message[start : start + depth, :])
-
-                unpack(along, X_ENTRIES, lambda k: STEPS + k)
-
-                @pl.when(ahead if is_lower else behind)
+                    for f, k, depth, at in entries[0]:
+                        put(f, line_of(k), rows(depth), message[at : at + depth, :])
+                    return entries[1]
+
+                def first_line(message, at, depth, line):
+                    ex, ez = message[at : at + depth, :], message[at + depth : at + 2 * depth, :]
+                    correct_line(line, rows(depth), ex, ez)
+                    return at + 2 * depth
+
+                def rows_ahead(message, at, lines):
+                    for i, line in enumerate(lines):
+                        one, two = at + i, at + len(lines) + i
+                        correct_row(line, last_row, message[one : one + 1, :], message[two : two + 1, :])
+
+                def rows_own(lines):
+                    for line in lines:
+                        correct_row(
+                            line,
+                            last_row,
+                            first_row[0, line : line + 1, :],
+                            first_row[1, line : line + 1, :],
+                        )
+
+                along_end = unpack(along, X_ENTRIES[ahead], lambda k: STEPS + k)
+                if ahead:
+                    rows_ahead(along, along_end + 2 * BORDER, range(STEPS, STEPS + LINES))
+                else:
+                    for line in range(LINES):
+                        correct_row(STEPS + line, last_row, start[1, line, 0:1, :], start[2, line, 0:1, :])
+
+                @pl.when(jnp.logical_not(no_behind))
                 def _():
-                    unpack(same, CORNERS[0][0], lambda k: STEPS + LINES + k if is_lower else STEPS - 1 - k)
-
-                @pl.when(behind if is_lower else ahead)
+                    message, entries = (mixed, MIXED_ENTRIES[True]) if ahead else (same, SAME_ENTRIES[False])
+                    at = unpack(message, entries, lambda k: near(False, k))
+                    first_line(along, along_end, BORDER, STEPS - 1)
+                    if ahead:
+                        rows_ahead(message, at, [near(False, k) for k in range(BORDER)])
+                    else:
+                        rows_own(behind_lines)
+
+                @pl.when(jnp.logical_not(no_ahead))
                 def _():
-                    unpack(mixed, CORNERS[1][0], lambda k: STEPS - 1 - k if is_lower else STEPS + LINES + k)
+                    message, entries = (same, SAME_ENTRIES[True]) if ahead else (mixed, MIXED_ENTRIES[False])
+                    at = unpack(message, entries, lambda k: near(True, k))
+                    at = first_line(message, at, 4 if ahead else BORDER, STEPS + LINES - 1)
+                    if ahead:
+                        rows_ahead(message, at, [near(True, k) for k in range(4)])
+                    else:
+                        rows_own([near(True, k) for k in range(4)])
 
     for copy in copies:
         copy.wait()
@@ -309,20 +502,23 @@
         reach = coef[0, line]
         for c in range(3):
             e = E[n][c, line]
-            if n == 0:
-                j = J[0][c, line]
-            else:
-                p = Pol[(n + 1) % 2][c, line]
-                j = coef[1, line] * J[(n + 1) % 2][c, line] + coef[3, line] * e - coef[2, line] * p
+            curl = curls[c]
+            if n > 0:
+                p, j = Pol[(n + 1) % 2][c, line], J[(n + 1) % 2][c, line]
+                if n == 1:
+                    j = j + coef[3, line] * e
+                else:
+                    j = coef[1, line] * j + coef[3, line] * e - coef[2, line] * p
                 if n < STEPS - 1:
                     J[n % 2][c, line] = j
                     Pol[n % 2][c, line] = p + time_step * j
+                curl = curl - j
             drawn = source_rows * (weight * source[c, line : line + 1, :])
-            E[n + 1][c, line] = e + reach * ((curls[c] - j) - drawn)
+            E[n + 1][c, line] = e + reach * (curl - drawn)
 
     for n in range(STEPS):
         weight = jnp.where(low_row, waveforms[0, n], waveforms[1, n])
-        for line in range(n, EXT_LINES - 1 - n):
+        for line in range(n, EXT_LINES - 1 - n) if n > 0 else ():
             magnetic_line(n, line)
         for line in range(n + 1, EXT_LINES - 1 - n):
             electric_line(n, line, weight)
@@ -338,7 +534,8 @@
             line = STEPS + 2 * k + half
             total = jnp.zeros((ROWS, LANES), jnp.float32)
             for c in range(3):
-                history = [E[n][c, line, middle, :] for n in range(STEPS + 1)]
+                history = [start[c, 2 * k + half]]
+                history += [E[n][c, line, middle, :] for n in range(1, STEPS + 1)]
                 for n in range(1, STEPS + 1):
                     total = total + half_turn(history[STEPS + 1 - n]) * (history[n] - history[n - 1])
                 electric_out[c, 2 * k + half] = history[STEPS]
@@ -411,36 +608,38 @@
     def corner(kind, mixed):
         return lambda w, x, y: (pair_of(x, kind, tx_count), y + (1 if (x % 2 == kind) != mixed else -1))
 
-    tile, y_a, y_b = pl.pallas_call(
+    tile, start, y_a, y_b = pl.pallas_call(
         pack_kernel,
         out_shape=(
             f32(FIELDS, LINES, ROWS, LANES),
-            f32(len(Y_ENTRIES), ROWS, LANES),
-            f32(len(Y_ENTRIES), ROWS, LANES),
+            f32(3, LINES, ROWS, LANES),
+            f32(Y_SIZE, ROWS, LANES),
+            f32(Y_SIZE, ROWS, LANES),
         ),
-        in_specs=[hbm] * 4,
-        out_specs=(vmem, vmem, vmem),
+        in_specs=[hbm] * 5,
+        out_specs=(vmem,) * 4,
         scratch_shapes=[
             pltpu.SMEM((NMAT, 4), jnp.float32),
+            pltpu.SMEM((6,), jnp.int32),
             pltpu.VMEM((CHUNKS, 2, 12, ROWS, LANES), jnp.float32),
             pltpu.VMEM((ROWS, LINES * NZ), jnp.int32),
             pltpu.VMEM((ROWS, LINES * NZ), jnp.float32),
-            pltpu.SemaphoreType.DMA((CHUNKS + 3,)),
+            pltpu.SemaphoreType.DMA((CHUNKS + 4,)),
         ],
         compiler_params=pltpu.CompilerParams(vmem_limit_bytes=32 * 1024 * 1024),
         name="pack",
-    )(*[in_hbm(v) for v in (material_table, initial_fields, material_map, design_density)])
+    )(*[in_hbm(v) for v in (material_table, design_box, initial_fields, material_map, design_density)])
     y_a, y_b = swap(y_a, along_y(0)), swap(y_b, along_y(1))
 
-    sizes = (X_ROWS, CORNERS[0][1], CORNERS[1][1]) * len(kinds)
+    sizes = (X_SIZE, SAME_SIZE, MIXED_SIZE) * len(kinds)
     messages = pl.pallas_call(
         edge_kernel,
         out_shape=[f32(size, LANES) for size in sizes],
-        in_specs=[vmem],
+        in_specs=[vmem, vmem],
         out_specs=[vmem] * len(sizes),
         compiler_params=pltpu.CompilerParams(vmem_limit_bytes=32 * 1024 * 1024),
         name="edges",
-    )(tile)
+    )(tile, start)
     arrived = []
     for i, message in enumerate(messages):
         kind = i // 3
@@ -450,7 +649,7 @@
     electric, partial = pl.pallas_call(
         functools.partial(window_kernel, tx_count, ty_count),
         out_shape=(f32(3, LINES, ROWS, LANES), f32(ROWS, LINES * NZ)),
-        in_specs=[hbm] * 4 + [vmem] * (4 + len(arrived)),
+        in_specs=[hbm] * 4 + [vmem] * (5 + len(arrived)),
         out_specs=(vmem, vmem),
         scratch_shapes=[
             [pltpu.VMEM((3,) + ext, jnp.float32) for _ in range(STEPS + 1)],
@@ -460,6 +659,7 @@
             pltpu.VMEM(ext, jnp.float32),
             pltpu.VMEM((4,) + ext, jnp.float32),
             pltpu.VMEM((3, EXT_LINES + 6, LANES), jnp.float32),
+            pltpu.VMEM((2, EXT_LINES + 6, LANES), jnp.float32),
             pltpu.SMEM((2, STEPS), jnp.float32),
             pltpu.SMEM((NMAT, 4), jnp.float32),
             pltpu.SMEM((2,), jnp.int32),
@@ -472,6 +672,7 @@
         *[in_hbm(v) for v in (source_waveforms[0], material_table, plane_indices, design_box)],
         source_profiles[0].transpose(1, 0, 2),
         tile,
+        start,
         y_a,
         y_b,
         *arrived,

time: 28.1 us -> 26.2 us (0.932)
  waiting for transfers between devices: 10 us -> 8.37 us
    ppermute x5, waiting for transfers between devices: 7.67 us -> 6 us  [swap(): return lax.ppermute(value, ('wave', 'tx', 'ty'), pairs)]
where the time goes in v4:
time: 26.2 us; the launch traced here: 26.1 us
  starting transfers between devices  10.9 us (42%)
  waiting for transfers between devices  8.37 us (32%)
  Pallas kernels  5.47 us (21%)
  between operations  0.68 us (3%)
  other arithmetic  0.63 us (2%)
    ppermute x5, starting transfers between devices, swap(): return lax.ppermute(value, ('wave', 'tx', 'ty'), pairs)  8.7 us
    ppermute x5, waiting for transfers between devices, swap(): return lax.ppermute(value, ('wave', 'tx', 'ty'), pairs)  6 us
    pallas_call x1, Pallas kernels, on_device(): pl.pallas_call(functools.partial(window_kernel, tx_count, ty_count), out_...  2.98 us
    ppermute x3, waiting for transfers between devices, on_device(): lax.ppermute(partial, 'wave', [(i, i ^ k) for i in range(4)])  2.37 us
    ppermute x3, starting transfers between devices, on_device(): lax.ppermute(partial, 'wave', [(i, i ^ k) for i in range(4)])  2.21 us
    pallas_call x1, Pallas kernels, on_device(): pl.pallas_call(pack_kernel, out_shape=(f32(FIELDS, LINES, ROWS, LANES), f...  1.64 us
    pallas_call x1, Pallas kernels, on_device(): pl.pallas_call(emit_kernel, out_shape=f32(1, 2, 3, ROWS, LINES * NZ), in_...  0.79 us
    add x1, other arithmetic, on_device(): gradient = partial + one + (two + three)  0.63 us
  transfers between devices with their start and end apart: 8, of which 3 were waited for; matrix products, arithmetic and copies ran while one was open for 0% of the time, Pallas kernels for 3%

profile of v4, /device:TPU:0, one launch (start us, length us, event | category | flops | bytes accessed | tf_op | source)
XLA Modules:
  0.0 26.1 jit_solution(2549642564215767165)
XLA Ops:
  0.6 1.6 %pack.1 = (f32[13,8,16,128]{3,2,1,0:T(8,128)S(1)}, f32[3,8,16,128]{3,2,1,0:T(8,128)S(1)}, f32[46,16,128]{2,1,0:T(8,128)S(1)}, f32[46,16,128]{2,1,0:T(8,128)S(1)}) custom-call(f32[3,4]{1,0:T(4,128)} %table_hbm.3, s32[6]{0:T(128)} %box_hbm.3, f32[1,2,12,16,512]{4,3,2,1,0:T(8,128)} %fields_hbm.1, s32[16,512]{1,0:T(8,128)} %material_hbm.1, f32[16,512]{1,0:T(8,128)} %density_hbm.1), custom_call_target="tpu_custom_call" | custom-call | tf_op jit(solution)/shard_map/pack/pallas_call | solution.py:611
  2.3 3.1 %collective-permute-start = (f32[46,16,128]{2,1,0:T(8,128)S(1)}, f32[46,16,128]{2,1,0:T(8,128)S(1)}, u32[]{:S(2)}, u32[]{:S(2)}) collective-permute-start(f32[46,16,128]{2,1,0:T(8,128)S(1)} %get-tuple-element.13), channel_id=1, source_target_pairs={{0,1},{1,0},{2,3},{3,2},{4,5},{5,4},{6,7},{7,6},{8,24},{9,10},{10,... | collective-permute-start | bytes 1130504 | tf_op jit(solution)/shard_map/ppermute | solution.py:600
  5.4 1.5 %collective-permute-start.1 = (f32[46,16,128]{2,1,0:T(8,128)S(1)}, f32[46,16,128]{2,1,0:T(8,128)S(1)}, u32[]{:S(2)}, u32[]{:S(2)}) collective-permute-start(f32[46,16,128]{2,1,0:T(8,128)S(1)} %get-tuple-element.14), channel_id=1, source_target_pairs={{0,16},{1,2},{2,1},{3,19},{4,20},{5,6},{6,5},{7,23},{8,9},{9,8},{1... | collective-permute-start | bytes 1130504 | tf_op jit(solution)/shard_map/ppermute | solution.py:600
  6.9 0.0 copy-start
  6.9 0.1 edges.1
  7.0 1.6 %collective-permute-start.2 = (f32[376,128]{1,0:T(8,128)S(1)}, f32[376,128]{1,0:T(8,128)S(1)}, u32[]{:S(2)}, u32[]{:S(2)}) collective-permute-start(f32[376,128]{1,0:T(8,128)S(1)} %get-tuple-element.15), channel_id=1, source_target_pairs={{0,4},{1,5},{2,6},{3,7},{4,0},{5,1},{6,2},{7,3},{8,12},{9,13},{10,... | collective-permute-start | bytes 577544 | tf_op jit(solution)/shard_map/ppermute | solution.py:600
  8.5 0.5 %collective-permute-start.4 = (f32[88,128]{1,0:T(8,128)S(1)}, f32[88,128]{1,0:T(8,128)S(1)}, u32[]{:S(2)}, u32[]{:S(2)}) collective-permute-start(f32[88,128]{1,0:T(8,128)S(1)} %get-tuple-element.17), channel_id=1, source_target_pairs={{0,16},{1,4},{2,5},{3,6},{4,1},{5,2},{6,3},{7,23},{8,24},{9,12},{1... | collective-permute-start | bytes 135176 | tf_op jit(solution)/shard_map/ppermute | solution.py:600
  9.0 2.0 %collective-permute-start.3 = (f32[72,128]{1,0:T(8,128)S(1)}, f32[72,128]{1,0:T(8,128)S(1)}, u32[]{:S(2)}, u32[]{:S(2)}) collective-permute-start(f32[72,128]{1,0:T(8,128)S(1)} %get-tuple-element.16), channel_id=1, source_target_pairs={{0,5},{1,6},{2,7},{3,19},{4,20},{5,0},{6,1},{7,2},{8,13},{9,14},{1... | collective-permute-start | bytes 110600 | tf_op jit(solution)/shard_map/ppermute | solution.py:600
  11.1 6.0 %collective-permute-done.3.rest_1_ = f32[72,128]{1,0:T(8,128)S(1)} collective-permute-done((f32[72,128]{1,0:T(8,128)S(1)}, f32[72,128]{1,0:T(8,128)S(1)}, u32[]{:S(2)}, u32[]{:S(2)}) %collective-permute-start.3) | collective-permute-done | bytes 36896 | tf_op jit(solution)/shard_map/ppermute | solution.py:600
  17.0 0.0 collective-permute-done.4.rest_2_
  17.0 0.0 collective-permute-done.2.rest_0_
  17.1 0.0 collective-permute-done.y_a
  17.1 0.0 collective-permute-done.1.y_b
  17.1 0.0 copy-done
  17.1 3.0 %window.1 = (f32[3,8,16,128]{3,2,1,0:T(8,128)S(1)}, f32[16,512]{1,0:T(8,128)S(1)}) custom-call(f32[2,5]{1,0:T(2,128)} %bitcast.5, f32[3,4]{1,0:T(4,128)} %table_hbm.3, s32[2]{0:T(128)} %plane_hbm.1, s32[6]{0:T(128)} %box_hbm.3, f32[3,2,2048]{2,1,0:T(2,128)S(1)} %bitcast.4, f32[13,8,16,128]{3,2,1,0:T(8,128)S(1)} %get-tuple-element.11.tile, ...), custom_call_target="tpu_custom_call" | custom-call | tf_op jit(solution)/shard_map/window/pallas_call | solution.py:649
  20.1 1.7 %collective-permute-start.6 = (f32[16,512]{1,0:T(8,128)S(1)}, f32[16,512]{1,0:T(8,128)S(1)}, u32[]{:S(2)}, u32[]{:S(2)}) collective-permute-start(f32[16,512]{1,0:T(8,128)S(1)} %get-tuple-element.18), channel_id=1, source_target_pairs={{0,16},{8,24},{16,0},{24,8},{1,17},{9,25},{17,1},{25,9},{2,18},{10... | collective-permute-start | bytes 98312 | tf_op jit(solution)/shard_map/ppermute | solution.py:691
  21.7 0.0 collective-permute-start.7
  21.7 0.5 %collective-permute-start.5 = (f32[16,512]{1,0:T(8,128)S(1)}, f32[16,512]{1,0:T(8,128)S(1)}, u32[]{:S(2)}, u32[]{:S(2)}) collective-permute-start(f32[16,512]{1,0:T(8,128)S(1)} %get-tuple-element.18), channel_id=1, source_target_pairs={{0,8},{8,0},{16,24},{24,16},{1,9},{9,1},{17,25},{25,17},{2,10},{10... | collective-permute-start | bytes 98312 | tf_op jit(solution)/shard_map/ppermute | solution.py:691
  22.3 0.8 %emit.1 = f32[1,2,3,16,512]{4,3,2,1,0:T(8,128)} custom-call(f32[3,8,16,128]{3,2,1,0:T(8,128)S(1)} %get-tuple-element.19.electric), custom_call_target="tpu_custom_call" | custom-call | tf_op jit(solution)/shard_map/emit/pallas_call | solution.py:680
  23.1 1.0 %collective-permute-done.6 = f32[16,512]{1,0:T(8,128)S(1)} collective-permute-done((f32[16,512]{1,0:T(8,128)S(1)}, f32[16,512]{1,0:T(8,128)S(1)}, u32[]{:S(2)}, u32[]{:S(2)}) %collective-permute-start.6) | collective-permute-done | bytes 32800 | tf_op jit(solution)/shard_map/ppermute | solution.py:691
  24.0 1.4 %collective-permute-done.7 = f32[16,512]{1,0:T(8,128)S(1)} collective-permute-done((f32[16,512]{1,0:T(8,128)S(1)}, f32[16,512]{1,0:T(8,128)S(1)}, u32[]{:S(2)}, u32[]{:S(2)}) %collective-permute-start.7) | collective-permute-done | bytes 32800 | tf_op jit(solution)/shard_map/ppermute | solution.py:691
  25.4 0.0 collective-permute-done.5
  25.4 0.6 %add_add_fusion = f32[16,512]{1,0:T(8,128)} fusion(f32[16,512]{1,0:T(8,128)S(1)} %collective-permute-done.6, f32[16,512]{1,0:T(8,128)S(1)} %collective-permute-done.7, f32[16,512]{1,0:T(8,128)S(1)} %get-tuple-element.18, f32[16,512]{1,0:T(8,128)S(1)} %collective-permute-done.5), kind=kLoop, calls=%fused_computation | loop fusion | flops 24576 | bytes 163840 | tf_op jit(solution)/shard_map/add | solution.py:693
Async XLA Ops:
  2.3 14.8 %collective-permute-start = (f32[46,16,128]{2,1,0:T(8,128)S(1)}, f32[46,16,128]{2,1,0:T(8,128)S(1)}, u32[]{:S(2)}, u32[]{:S(2)}) collective-permute-start(f32[46,16,128]{2,1,0:T(8,128)S(1)} %get-tuple-element.13), channel_id=1, source_target_pairs={{0,1},{1,0},{2,3},{3,2},{4,5},{5,4},{6,7},{7,6},{8,24},{9,10},{10,... | collective-permute-start | bytes 1130504 | tf_op jit(solution)/shard_map/ppermute | solution.py:600
  5.4 11.7 %collective-permute-start.1 = (f32[46,16,128]{2,1,0:T(8,128)S(1)}, f32[46,16,128]{2,1,0:T(8,128)S(1)}, u32[]{:S(2)}, u32[]{:S(2)}) collective-permute-start(f32[46,16,128]{2,1,0:T(8,128)S(1)} %get-tuple-element.14), channel_id=1, source_target_pairs={{0,16},{1,2},{2,1},{3,19},{4,20},{5,6},{6,5},{7,23},{8,9},{9,8},{1... | collective-permute-start | bytes 1130504 | tf_op jit(solution)/shard_map/ppermute | solution.py:600
  6.9 10.2 %copy-start = (f32[1,2,3,2048]{3,1,2,0:T(2,128)S(1)}, f32[1,2,3,2048]{3,1,2,0:T(2,128)}, u32[]{:S(2)}) copy-start(f32[1,2,3,2048]{3,1,2,0:T(2,128)} %param.9) | copy-start | bytes 147460
  7.0 10.1 %collective-permute-start.2 = (f32[376,128]{1,0:T(8,128)S(1)}, f32[376,128]{1,0:T(8,128)S(1)}, u32[]{:S(2)}, u32[]{:S(2)}) collective-permute-start(f32[376,128]{1,0:T(8,128)S(1)} %get-tuple-element.15), channel_id=1, source_target_pairs={{0,4},{1,5},{2,6},{3,7},{4,0},{5,1},{6,2},{7,3},{8,12},{9,13},{10,... | collective-permute-start | bytes 577544 | tf_op jit(solution)/shard_map/ppermute | solution.py:600
  8.5 8.5 %collective-permute-start.4 = (f32[88,128]{1,0:T(8,128)S(1)}, f32[88,128]{1,0:T(8,128)S(1)}, u32[]{:S(2)}, u32[]{:S(2)}) collective-permute-start(f32[88,128]{1,0:T(8,128)S(1)} %get-tuple-element.17), channel_id=1, source_target_pairs={{0,16},{1,4},{2,5},{3,6},{4,1},{5,2},{6,3},{7,23},{8,24},{9,12},{1... | collective-permute-start | bytes 135176 | tf_op jit(solution)/shard_map/ppermute | solution.py:600
  9.0 8.0 %collective-permute-start.3 = (f32[72,128]{1,0:T(8,128)S(1)}, f32[72,128]{1,0:T(8,128)S(1)}, u32[]{:S(2)}, u32[]{:S(2)}) collective-permute-start(f32[72,128]{1,0:T(8,128)S(1)} %get-tuple-element.16), channel_id=1, source_target_pairs={{0,5},{1,6},{2,7},{3,19},{4,20},{5,0},{6,1},{7,2},{8,13},{9,14},{1... | collective-permute-start | bytes 110600 | tf_op jit(solution)/shard_map/ppermute | solution.py:600
  20.1 4.0 %collective-permute-start.6 = (f32[16,512]{1,0:T(8,128)S(1)}, f32[16,512]{1,0:T(8,128)S(1)}, u32[]{:S(2)}, u32[]{:S(2)}) collective-permute-start(f32[16,512]{1,0:T(8,128)S(1)} %get-tuple-element.18), channel_id=1, source_target_pairs={{0,16},{8,24},{16,0},{24,8},{1,17},{9,25},{17,1},{25,9},{2,18},{10... | collective-permute-start | bytes 98312 | tf_op jit(solution)/shard_map/ppermute | solution.py:691
  21.7 3.7 %collective-permute-start.7 = (f32[16,512]{1,0:T(8,128)S(1)}, f32[16,512]{1,0:T(8,128)S(1)}, u32[]{:S(2)}, u32[]{:S(2)}) collective-permute-start(f32[16,512]{1,0:T(8,128)S(1)} %get-tuple-element.18), channel_id=1, source_target_pairs={{0,24},{8,16},{16,8},{24,0},{1,25},{9,17},{17,9},{25,1},{2,26},{10... | collective-permute-start | bytes 98312 | tf_op jit(solution)/shard_map/ppermute | solution.py:691
  21.7 3.7 %collective-permute-start.5 = (f32[16,512]{1,0:T(8,128)S(1)}, f32[16,512]{1,0:T(8,128)S(1)}, u32[]{:S(2)}, u32[]{:S(2)}) collective-permute-start(f32[16,512]{1,0:T(8,128)S(1)} %get-tuple-element.18), channel_id=1, source_target_pairs={{0,8},{8,0},{16,24},{24,16},{1,9},{9,1},{17,25},{25,17},{2,10},{10... | collective-permute-start | bytes 98312 | tf_op jit(solution)/shard_map/ppermute | solution.py:691

commit v5 on v4

--- a/solution.py
+++ b/solution.py
@@ -91,7 +91,7 @@
 
 
 def is_lower_in_a():
-    return lax.rem(lax.axis_index("ty") + lax.axis_index("wave"), 2) == 0
+    return lax.rem(lax.axis_index("ty"), 2) == 0
 
 
 def pack_kernel(
@@ -596,11 +596,11 @@
                     if ox is not None and oy is not None and 0 <= oy < ty_count:
                         pairs.append((index(w, x, y), index(w, ox, oy)))
                     elif waves % 2 == 0:
-                        pairs.append((index(w, x, y), index((w + waves // 2) % waves, x, y)))
+                        pairs.append((index(w, x, y), index(w ^ 1, x, y)))
         return lax.ppermute(value, ("wave", "tx", "ty"), pairs)
 
     def along_y(b):
-        return lambda w, x, y: (x, pair_of(y, (w + b) % 2, ty_count))
+        return lambda w, x, y: (x, pair_of(y, b, ty_count))
 
     def along_x(kind):
         return lambda w, x, y: (pair_of(x, kind, tx_count), y)

time: 26.2 us -> 24.8 us (0.947)
  the two profiles are of different devices: /device:TPU:0 before, /device:TPU:16 now
where the time goes in v5:
time: 24.8 us; the launch traced here: 24.6 us
  waiting for transfers between devices  10.4 us (42%)
  starting transfers between devices  7.4 us (30%)
  Pallas kernels  5.48 us (22%)
  between operations  0.67 us (3%)
  other arithmetic  0.63 us (3%)
    ppermute x5, waiting for transfers between devices, swap(): return lax.ppermute(value, ('wave', 'tx', 'ty'), pairs)  8.49 us
    ppermute x5, starting transfers between devices, swap(): return lax.ppermute(value, ('wave', 'tx', 'ty'), pairs)  5.2 us
    pallas_call x1, Pallas kernels, on_device(): pl.pallas_call(functools.partial(window_kernel, tx_count, ty_count), out_...  2.97 us
    ppermute x3, starting transfers between devices, on_device(): lax.ppermute(partial, 'wave', [(i, i ^ k) for i in range(4)])  2.21 us
    ppermute x3, waiting for transfers between devices, on_device(): lax.ppermute(partial, 'wave', [(i, i ^ k) for i in range(4)])  1.93 us
    pallas_call x1, Pallas kernels, on_device(): pl.pallas_call(pack_kernel, out_shape=(f32(FIELDS, LINES, ROWS, LANES), f...  1.65 us
    pallas_call x1, Pallas kernels, on_device(): pl.pallas_call(emit_kernel, out_shape=f32(1, 2, 3, ROWS, LINES * NZ), in_...  0.79 us
    add x1, other arithmetic, on_device(): gradient = partial + one + (two + three)  0.63 us
  transfers between devices with their start and end apart: 8, of which 4 were waited for; matrix products, arithmetic and copies ran while one was open for 0% of the time, Pallas kernels for 3%

profile of v5, /device:TPU:16, one launch (start us, length us, event | category | flops | bytes accessed | tf_op | source)
XLA Modules:
  0.0 24.6 jit_solution(2625549826479577820)
XLA Ops:
  0.6 1.6 %pack.1 = (f32[13,8,16,128]{3,2,1,0:T(8,128)S(1)}, f32[3,8,16,128]{3,2,1,0:T(8,128)S(1)}, f32[46,16,128]{2,1,0:T(8,128)S(1)}, f32[46,16,128]{2,1,0:T(8,128)S(1)}) custom-call(f32[3,4]{1,0:T(4,128)} %table_hbm.3, s32[6]{0:T(128)} %box_hbm.3, f32[1,2,12,16,512]{4,3,2,1,0:T(8,128)} %fields_hbm.1, s32[16,512]{1,0:T(8,128)} %material_hbm.1, f32[16,512]{1,0:T(8,128)} %density_hbm.1), custom_call_target="tpu_custom_call" | custom-call | tf_op jit(solution)/shard_map/pack/pallas_call | solution.py:611
  2.3 1.6 %collective-permute-start = (f32[46,16,128]{2,1,0:T(8,128)S(1)}, f32[46,16,128]{2,1,0:T(8,128)S(1)}, u32[]{:S(2)}, u32[]{:S(2)}) collective-permute-start(f32[46,16,128]{2,1,0:T(8,128)S(1)} %get-tuple-element.13), channel_id=1, source_target_pairs={{0,1},{1,0},{2,3},{3,2},{4,5},{5,4},{6,7},{7,6},{8,9},{9,8},{10,11... | collective-permute-start | bytes 1130504 | tf_op jit(solution)/shard_map/ppermute | solution.py:600
  3.9 0.0 collective-permute-start.1
  3.9 0.0 copy-start
  3.9 0.1 edges.1
  4.0 1.6 %collective-permute-start.2 = (f32[376,128]{1,0:T(8,128)S(1)}, f32[376,128]{1,0:T(8,128)S(1)}, u32[]{:S(2)}, u32[]{:S(2)}) collective-permute-start(f32[376,128]{1,0:T(8,128)S(1)} %get-tuple-element.15), channel_id=1, source_target_pairs={{0,4},{1,5},{2,6},{3,7},{4,0},{5,1},{6,2},{7,3},{8,12},{9,13},{10,... | collective-permute-start | bytes 577544 | tf_op jit(solution)/shard_map/ppermute | solution.py:600
  5.6 2.0 %collective-permute-start.4 = (f32[88,128]{1,0:T(8,128)S(1)}, f32[88,128]{1,0:T(8,128)S(1)}, u32[]{:S(2)}, u32[]{:S(2)}) collective-permute-start(f32[88,128]{1,0:T(8,128)S(1)} %get-tuple-element.17), channel_id=1, source_target_pairs={{0,8},{1,4},{2,5},{3,6},{4,1},{5,2},{6,3},{7,15},{8,0},{9,12},{10,... | collective-permute-start | bytes 135176 | tf_op jit(solution)/shard_map/ppermute | solution.py:600
  7.6 0.0 collective-permute-start.3
  7.6 7.2 %collective-permute-done.3.rest_1_ = f32[72,128]{1,0:T(8,128)S(1)} collective-permute-done((f32[72,128]{1,0:T(8,128)S(1)}, f32[72,128]{1,0:T(8,128)S(1)}, u32[]{:S(2)}, u32[]{:S(2)}) %collective-permute-start.3) | collective-permute-done | bytes 36896 | tf_op jit(solution)/shard_map/ppermute | solution.py:600
  14.8 1.3 %collective-permute-done.4.rest_2_ = f32[88,128]{1,0:T(8,128)S(1)} collective-permute-done((f32[88,128]{1,0:T(8,128)S(1)}, f32[88,128]{1,0:T(8,128)S(1)}, u32[]{:S(2)}, u32[]{:S(2)}) %collective-permute-start.4) | collective-permute-done | bytes 45088 | tf_op jit(solution)/shard_map/ppermute | solution.py:600
  16.0 0.0 collective-permute-done.2.rest_0_
  16.0 0.0 collective-permute-done.y_a
  16.0 0.0 collective-permute-done.1.y_b
  16.1 0.0 copy-done
  16.1 3.0 %window.1 = (f32[3,8,16,128]{3,2,1,0:T(8,128)S(1)}, f32[16,512]{1,0:T(8,128)S(1)}) custom-call(f32[2,5]{1,0:T(2,128)} %bitcast.5, f32[3,4]{1,0:T(4,128)} %table_hbm.3, s32[2]{0:T(128)} %plane_hbm.1, s32[6]{0:T(128)} %box_hbm.3, f32[3,2,2048]{2,1,0:T(2,128)S(1)} %bitcast.4, f32[13,8,16,128]{3,2,1,0:T(8,128)S(1)} %get-tuple-element.11.tile, ...), custom_call_target="tpu_custom_call" | custom-call | tf_op jit(solution)/shard_map/window/pallas_call | solution.py:649
  19.0 1.6 %collective-permute-start.6 = (f32[16,512]{1,0:T(8,128)S(1)}, f32[16,512]{1,0:T(8,128)S(1)}, u32[]{:S(2)}, u32[]{:S(2)}) collective-permute-start(f32[16,512]{1,0:T(8,128)S(1)} %get-tuple-element.18), channel_id=1, source_target_pairs={{0,16},{8,24},{16,0},{24,8},{1,17},{9,25},{17,1},{25,9},{2,18},{10... | collective-permute-start | bytes 98312 | tf_op jit(solution)/shard_map/ppermute | solution.py:691
  20.6 0.0 collective-permute-start.7
  20.6 0.6 %collective-permute-start.5 = (f32[16,512]{1,0:T(8,128)S(1)}, f32[16,512]{1,0:T(8,128)S(1)}, u32[]{:S(2)}, u32[]{:S(2)}) collective-permute-start(f32[16,512]{1,0:T(8,128)S(1)} %get-tuple-element.18), channel_id=1, source_target_pairs={{0,8},{8,0},{16,24},{24,16},{1,9},{9,1},{17,25},{25,17},{2,10},{10... | collective-permute-start | bytes 98312 | tf_op jit(solution)/shard_map/ppermute | solution.py:691
  21.3 0.8 %emit.1 = f32[1,2,3,16,512]{4,3,2,1,0:T(8,128)} custom-call(f32[3,8,16,128]{3,2,1,0:T(8,128)S(1)} %get-tuple-element.19.electric), custom_call_target="tpu_custom_call" | custom-call | tf_op jit(solution)/shard_map/emit/pallas_call | solution.py:680
  22.0 1.0 %collective-permute-done.6 = f32[16,512]{1,0:T(8,128)S(1)} collective-permute-done((f32[16,512]{1,0:T(8,128)S(1)}, f32[16,512]{1,0:T(8,128)S(1)}, u32[]{:S(2)}, u32[]{:S(2)}) %collective-permute-start.6) | collective-permute-done | bytes 32800 | tf_op jit(solution)/shard_map/ppermute | solution.py:691
  23.0 0.9 %collective-permute-done.7 = f32[16,512]{1,0:T(8,128)S(1)} collective-permute-done((f32[16,512]{1,0:T(8,128)S(1)}, f32[16,512]{1,0:T(8,128)S(1)}, u32[]{:S(2)}, u32[]{:S(2)}) %collective-permute-start.7) | collective-permute-done | bytes 32800 | tf_op jit(solution)/shard_map/ppermute | solution.py:691
  24.0 0.0 collective-permute-done.5
  24.0 0.6 %add_add_fusion = f32[16,512]{1,0:T(8,128)} fusion(f32[16,512]{1,0:T(8,128)S(1)} %collective-permute-done.6, f32[16,512]{1,0:T(8,128)S(1)} %collective-permute-done.7, f32[16,512]{1,0:T(8,128)S(1)} %get-tuple-element.18, f32[16,512]{1,0:T(8,128)S(1)} %collective-permute-done.5), kind=kLoop, calls=%fused_computation | loop fusion | flops 24576 | bytes 163840 | tf_op jit(solution)/shard_map/add | solution.py:693
Async XLA Ops:
  2.3 13.8 %collective-permute-start = (f32[46,16,128]{2,1,0:T(8,128)S(1)}, f32[46,16,128]{2,1,0:T(8,128)S(1)}, u32[]{:S(2)}, u32[]{:S(2)}) collective-permute-start(f32[46,16,128]{2,1,0:T(8,128)S(1)} %get-tuple-element.13), channel_id=1, source_target_pairs={{0,1},{1,0},{2,3},{3,2},{4,5},{5,4},{6,7},{7,6},{8,9},{9,8},{10,11... | collective-permute-start | bytes 1130504 | tf_op jit(solution)/shard_map/ppermute | solution.py:600
  3.9 12.1 %collective-permute-start.1 = (f32[46,16,128]{2,1,0:T(8,128)S(1)}, f32[46,16,128]{2,1,0:T(8,128)S(1)}, u32[]{:S(2)}, u32[]{:S(2)}) collective-permute-start(f32[46,16,128]{2,1,0:T(8,128)S(1)} %get-tuple-element.14), channel_id=1, source_target_pairs={{0,8},{1,2},{2,1},{3,11},{4,12},{5,6},{6,5},{7,15},{8,0},{9,10},{1... | collective-permute-start | bytes 1130504 | tf_op jit(solution)/shard_map/ppermute | solution.py:600
  3.9 12.1 %copy-start = (f32[1,2,3,2048]{3,1,2,0:T(2,128)S(1)}, f32[1,2,3,2048]{3,1,2,0:T(2,128)}, u32[]{:S(2)}) copy-start(f32[1,2,3,2048]{3,1,2,0:T(2,128)} %param.9) | copy-start | bytes 147460
  4.0 12.0 %collective-permute-start.2 = (f32[376,128]{1,0:T(8,128)S(1)}, f32[376,128]{1,0:T(8,128)S(1)}, u32[]{:S(2)}, u32[]{:S(2)}) collective-permute-start(f32[376,128]{1,0:T(8,128)S(1)} %get-tuple-element.15), channel_id=1, source_target_pairs={{0,4},{1,5},{2,6},{3,7},{4,0},{5,1},{6,2},{7,3},{8,12},{9,13},{10,... | collective-permute-start | bytes 577544 | tf_op jit(solution)/shard_map/ppermute | solution.py:600
  5.6 10.5 %collective-permute-start.4 = (f32[88,128]{1,0:T(8,128)S(1)}, f32[88,128]{1,0:T(8,128)S(1)}, u32[]{:S(2)}, u32[]{:S(2)}) collective-permute-start(f32[88,128]{1,0:T(8,128)S(1)} %get-tuple-element.17), channel_id=1, source_target_pairs={{0,8},{1,4},{2,5},{3,6},{4,1},{5,2},{6,3},{7,15},{8,0},{9,12},{10,... | collective-permute-start | bytes 135176 | tf_op jit(solution)/shard_map/ppermute | solution.py:600
  7.6 7.2 %collective-permute-start.3 = (f32[72,128]{1,0:T(8,128)S(1)}, f32[72,128]{1,0:T(8,128)S(1)}, u32[]{:S(2)}, u32[]{:S(2)}) collective-permute-start(f32[72,128]{1,0:T(8,128)S(1)} %get-tuple-element.16), channel_id=1, source_target_pairs={{0,5},{1,6},{2,7},{3,11},{4,12},{5,0},{6,1},{7,2},{8,13},{9,14},{1... | collective-permute-start | bytes 110600 | tf_op jit(solution)/shard_map/ppermute | solution.py:600
  19.0 4.0 %collective-permute-start.6 = (f32[16,512]{1,0:T(8,128)S(1)}, f32[16,512]{1,0:T(8,128)S(1)}, u32[]{:S(2)}, u32[]{:S(2)}) collective-permute-start(f32[16,512]{1,0:T(8,128)S(1)} %get-tuple-element.18), channel_id=1, source_target_pairs={{0,16},{8,24},{16,0},{24,8},{1,17},{9,25},{17,1},{25,9},{2,18},{10... | collective-permute-start | bytes 98312 | tf_op jit(solution)/shard_map/ppermute | solution.py:691
  20.6 3.3 %collective-permute-start.7 = (f32[16,512]{1,0:T(8,128)S(1)}, f32[16,512]{1,0:T(8,128)S(1)}, u32[]{:S(2)}, u32[]{:S(2)}) collective-permute-start(f32[16,512]{1,0:T(8,128)S(1)} %get-tuple-element.18), channel_id=1, source_target_pairs={{0,24},{8,16},{16,8},{24,0},{1,25},{9,17},{17,9},{25,1},{2,26},{10... | collective-permute-start | bytes 98312 | tf_op jit(solution)/shard_map/ppermute | solution.py:691
  20.6 3.3 %collective-permute-start.5 = (f32[16,512]{1,0:T(8,128)S(1)}, f32[16,512]{1,0:T(8,128)S(1)}, u32[]{:S(2)}, u32[]{:S(2)}) collective-permute-start(f32[16,512]{1,0:T(8,128)S(1)} %get-tuple-element.18), channel_id=1, source_target_pairs={{0,8},{8,0},{16,24},{24,16},{1,9},{9,1},{17,25},{25,17},{2,10},{10... | collective-permute-start | bytes 98312 | tf_op jit(solution)/shard_map/ppermute | solution.py:691

commit v6 on v5

--- a/solution.py
+++ b/solution.py
@@ -86,7 +86,7 @@
         d, w, g = table[m, 1], table[m, 2], table[m, 3]
         denom = 1.0 + 0.25 * g
         drive = w * w * time_step / denom
-        out.append(((1.0 - 0.25 * g) / denom, drive, drive * d))
+        out.append(((1.0 - 0.25 * g) / denom, drive * 0.5, drive * d * 2.0))
     return [lambda m, i=i: out[m][i] for i in range(3)]
 
 
@@ -156,15 +156,15 @@
             where = first_line + line
             design = design_rows * ((where >= box[2]) & (where < box[3])).astype(jnp.float32)
             permittivity = choose(mat, lambda m: table[m, 0]) + design * dens * contrast
-            reach = time_step / permittivity
+            reach = time_step * 0.5 / permittivity
             dec, dri, cou = [choose(mat, column) for column in (decay, drive, coupled)]
             for c in range(3):
-                e, p, j = pairs[c][half], pairs[6 + c][half], pairs[9 + c][half]
+                e, p, j = pairs[c][half], 4.0 * pairs[6 + c][half], 2.0 * pairs[9 + c][half]
                 j = dec * j + cou * e - dri * p
-                p = p + time_step * j
+                p = p + j
                 start[c, line] = e
                 tile[c, line] = e - reach * j
-                tile[3 + c, line] = pairs[3 + c][half]
+                tile[3 + c, line] = 2.0 * pairs[3 + c][half]
                 tile[6 + c, line] = p
                 tile[9 + c, line] = dec * j - dri * p
             tile[12, line] = jnp.where(low, mat, dens)
@@ -183,9 +183,9 @@
             ex_next, ez_next = start[0, line + 1], start[2, line + 1]
         else:
             ex_next = ez_next = jnp.zeros(shape, jnp.float32)
-        tile[3, line] = tile[3, line] - time_step * ((ez_next - ez) - (ahead_depth(ey) - ey))
-        tile[4, line] = tile[4, line] - time_step * ((ahead_depth(ex) - ex) - (ahead_row(ez) - ez))
-        tile[5, line] = tile[5, line] - time_step * ((ahead_row(ey) - ey) - (ex_next - ex))
+        tile[3, line] = tile[3, line] - ((ez_next - ez) - (ahead_depth(ey) - ey))
+        tile[4, line] = tile[4, line] - ((ahead_depth(ex) - ex) - (ahead_row(ez) - ez))
+        tile[5, line] = tile[5, line] - ((ahead_row(ey) - ey) - (ex_next - ex))
 
     lower = is_lower_in_a()
     for message, is_lower in ((y_a, lower), (y_b, jnp.logical_not(lower))):
@@ -251,7 +251,7 @@
                     pack_first_line(mixed, at, BORDER)
 
 
-def window_kernel(
+def prepare_kernel(
     tx_count,
     ty_count,
     waveforms_hbm,
@@ -259,6 +259,71 @@
     plane_hbm,
     box_hbm,
     profiles,
+    sources,
+    source_rows,
+    design,
+    poles,
+    waveforms,
+    table,
+    plane,
+    box,
+    sems,
+):
+    copies = [
+        pltpu.make_async_copy(src, dst, sems.at[i])
+        for i, (src, dst) in enumerate(
+            [(waveforms_hbm, waveforms), (table_hbm, table), (plane_hbm, plane), (box_hbm, box)]
+        )
+    ]
+    for copy in copies:
+        copy.start()
+    for copy in copies:
+        copy.wait()
+    tx, ty = lax.axis_index("tx"), lax.axis_index("ty")
+    shape = source_rows.shape
+    low = low_lanes(shape)
+    lane = lax.broadcasted_iota(jnp.int32, shape, 1)
+    depth_id = jnp.where(low, lane, lane - NZ)
+    row = window_rows(tx_count, shape)
+    source_rows[...] = (row == jnp.where(low, plane[0], plane[1])).astype(jnp.float32)
+    in_z = (depth_id >= box[4]) & (depth_id < box[5])
+    design_rows = ((row >= box[0]) & (row < box[1]) & in_z).astype(jnp.float32) * contrast
+    for line in range(1, EXT_LINES - 1):
+        where = ty * LINES - STEPS + line
+        design[line] = design_rows * ((where >= box[2]) & (where < box[3])).astype(jnp.float32)
+    for i, column in enumerate((lambda m: table[m, 0], *pole(table))):
+        for m in range(NMAT):
+            at = NMAT * i + m
+            poles[at : at + 1, :] = jnp.full((1, LANES), column(m), jnp.float32)
+    low_row = low[:1]
+    weights = [2.0 * jnp.where(low_row, waveforms[0, n], waveforms[1, n]) for n in range(STEPS)]
+    for i in range(EXT_LINES // 2 - 1):
+        chunk = jnp.clip(ty * CHUNKS + i - STEPS // 2, 0, ty_count * CHUNKS - 1)
+        for c in range(3):
+            both = profiles[c, :, pl.ds(pl.multiple_of(chunk * LANES, LANES), LANES)]
+            one, two = both[0:1], both[1:2]
+            first = jnp.where(low_row, one, half_turn(two))
+            second = jnp.where(low_row, half_turn(one), two)
+            for n in range(STEPS):
+                sources[n, c, 2 * i + 1 : 2 * i + 2, :] = weights[n] * first
+                sources[n, c, 2 * i + 2 : 2 * i + 3, :] = weights[n] * second
+
+
+def window_rows(tx_count, shape):
+    tx = lax.axis_index("tx")
+    at = lax.broadcasted_iota(jnp.int32, shape, 0)
+    if tx_count == 2:
+        return at + tx * ROWS - jnp.where(at >= ROWS, tx * (ROWS + PAD), 0)
+    return at + tx * ROWS - PAD
+
+
+def window_kernel(
+    tx_count,
+    ty_count,
+    sources,
+    source_rows,
+    design,
+    poles,
     tile,
     start,
     y_a,
@@ -267,23 +332,15 @@
 ):
     kinds = 1 if tx_count == 2 else 2
     messages, rest = rest[: 3 * kinds], rest[3 * kinds :]
-    electric_out, gradient_out, E, H, Pol, J, C, coef, source, first_row, waveforms, table, plane, box, sems = rest
+    electric_out, gradient_out, E, H, Pol, J, C, coef, first_row = rest
     wide = tx_count != 2
     ext_rows = E[0].shape[2]
-    copies = [
-        pltpu.make_async_copy(src, dst, sems.at[i])
-        for i, (src, dst) in enumerate(
-            [(waveforms_hbm, waveforms), (table_hbm, table), (plane_hbm, plane), (box_hbm, box)]
-        )
-    ]
-    for copy in copies:
-        copy.start()
     tx, ty = lax.axis_index("tx"), lax.axis_index("ty")
     odd_x = lax.rem(tx, 2)
-    offset = PAD if wide else pl.multiple_of(tx * PAD, PAD)
-    rows_base, lines_base = tx * ROWS - offset, ty * LINES - STEPS
+    tile_row = PAD if wide else 0
+    lines_base = ty * LINES - STEPS
     rows_all, lines_all = tx_count * ROWS, ty_count * LINES
-    middle = pl.ds(offset, ROWS)
+    middle = slice(tile_row, tile_row + ROWS)
 
     def put(f, line, rows, value):
         if f < 12:
@@ -319,18 +376,20 @@
     for f in range(FIELDS):
         for line in range(LINES):
             put(f, STEPS + line, middle, tile[f, line])
+    if not wide:
+        H[1][1:3, :, ROWS:ext_rows, :] = jnp.zeros((2, EXT_LINES, PAD, LANES), jnp.float32)
 
     def near(ahead, k):
         return STEPS + LINES + k if ahead else STEPS - 1 - k
 
     def correct_line(line, rows, ex, ez):
-        H[1][0, line, rows, :] = H[1][0, line, rows, :] - time_step * ez
-        H[1][2, line, rows, :] = H[1][2, line, rows, :] + time_step * ex
+        H[1][0, line, rows, :] = H[1][0, line, rows, :] - ez
+        H[1][2, line, rows, :] = H[1][2, line, rows, :] + ex
 
     def correct_row(line, row, ey, ez):
         at = slice(row, row + 1)
-        H[1][1, line, at, :] = H[1][1, line, at, :] + time_step * ez
-        H[1][2, line, at, :] = H[1][2, line, at, :] - time_step * ey
+        H[1][1, line, at, :] = H[1][1, line, at, :] + ez
+        H[1][2, line, at, :] = H[1][2, line, at, :] - ey
 
     lower = is_lower_in_a()
     for message, is_lower in ((y_a, lower), (y_b, jnp.logical_not(lower))):
@@ -354,7 +413,7 @@
         along, same, mixed = messages[3 * kind : 3 * kind + 3]
         for ahead in (False, True):
             in_x = tx + 1 < tx_count if ahead else tx > 0
-            halo = ROWS + (PAD if wide else 0) if ahead else PAD
+            halo = tile_row + ROWS if ahead else (PAD if wide else ext_rows)
             last_row = halo - 1
 
             @pl.when(jnp.logical_and((odd_x == kind) == ahead, in_x))
@@ -413,23 +472,10 @@
                     else:
                         rows_own([near(True, k) for k in range(4)])
 
-    for copy in copies:
-        copy.wait()
-    decay, drive, coupled = pole(table)
     shape = (ext_rows, LANES)
     low = low_lanes(shape)
-    lane = lax.broadcasted_iota(jnp.int32, shape, 1)
-    depth_id = jnp.where(low, lane, lane - NZ)
-    row = lax.broadcasted_iota(jnp.int32, shape, 0) + rows_base
-    first_z, last_z = depth_id == 0, depth_id == NZ - 1
+    row = window_rows(tx_count, shape)
     row_mask = ((row >= 0) & (row < rows_all)).astype(jnp.float32)
-    in_z = (depth_id >= box[4]) & (depth_id < box[5])
-    design_rows = ((row >= box[0]) & (row < box[1]) & in_z).astype(jnp.float32)
-    source_rows = (row == jnp.where(low, plane[0], plane[1])).astype(jnp.float32)
-
-    def line_design(line):
-        where = lines_base + line
-        return ((where >= box[2]) & (where < box[3])).astype(jnp.float32)
 
     def line_inside(line):
         where = lines_base + line
@@ -443,33 +489,38 @@
         turned = half_turn(mixed)
         mat = jnp.where(low, mixed, turned)
         dens = jnp.where(low, turned, mixed)
-        design = design_rows * line_design(line)
-        permittivity = choose(mat, lambda m: table[m, 0]) + (design * dens) * contrast
-        reach = time_step / permittivity
+        eps, *others = [
+            choose(mat, lambda m, i=i: poles[NMAT * i + m : NMAT * i + m + 1, :]) for i in range(4)
+        ]
+        reach = time_step * 0.5 / (eps + design[line] * dens)
         if wide:
             reach = reach * row_mask
         if not is_own(line):
             reach = reach * line_inside(line)
         coef[0, line] = reach
-        for i, column in enumerate((decay, drive, coupled)):
-            coef[1 + i, line] = choose(mat, column)
-
-    low_row = low[:1]
-    for i in range(EXT_LINES // 2):
-        chunk = jnp.clip(ty * CHUNKS + (i - STEPS // 2 - 1) + 1, 0, ty_count * CHUNKS - 1)
-        for c in range(3):
-            both = profiles[c, :, pl.ds(pl.multiple_of(chunk * LANES, LANES), LANES)]
-            one, two = both[0:1], both[1:2]
-            source[c, pl.ds(2 * i + 1, 1), :] = jnp.where(low_row, one, half_turn(two))
-            source[c, pl.ds(2 * i + 2, 1), :] = jnp.where(low_row, half_turn(one), two)
-
-    edge = jnp.zeros((1, LANES), jnp.float32)
+        for i, value in enumerate(others):
+            coef[1 + i, line] = value
+
+    count = ext_rows // 8
+    block = (8, LANES)
+    lane = lax.broadcasted_iota(jnp.int32, block, 1)
+    depth_id = jnp.where(low[:8], lane, lane - NZ)
+    first_z, last_z = depth_id == 0, depth_id == NZ - 1
+    sub = lax.broadcasted_iota(jnp.int32, block, 0)
+    first_sub, last_sub = sub == 0, sub == 7
+    sent = sub + tx * (7 - 2 * sub) < STEPS
+    every, own = range(count), range(tile_row // 8, (tile_row + ROWS) // 8)
+
+    def blocks(ref, c, line):
+        return [ref[c, line, 8 * b : 8 * b + 8, :] for b in every]
 
     def ahead_row(v):
-        return jnp.concatenate([v[1:], edge], axis=0)
+        turned = [pltpu.roll(x, 7, 0) for x in v]
+        return [jnp.where(last_sub, turned[(b + 1) % count], turned[b]) for b in every]
 
     def behind_row(v):
-        return jnp.concatenate([edge, v[:-1]], axis=0)
+        turned = [pltpu.roll(x, 1, 0) for x in v]
+        return [jnp.where(first_sub, turned[b - 1], turned[b]) for b in every]
 
     def ahead_depth(v):
         return jnp.where(last_z, 0.0, pltpu.roll(v, LANES - 1, 1))
@@ -477,70 +528,86 @@
     def behind_depth(v):
         return jnp.where(first_z, 0.0, pltpu.roll(v, 1, 1))
 
+    def settle(ref, c, line, b, value):
+        if not wide and b not in own:
+            value = jnp.where(sent, value, 0.0)
+        ref[c, line, 8 * b : 8 * b + 8, :] = value
+
     def magnetic_line(n, line):
         old, new = H[n % 2], H[(n + 1) % 2]
-        ex, ey, ez = E[n][0, line], E[n][1, line], E[n][2, line]
-        ex_next, ez_next = E[n][0, line + 1], E[n][2, line + 1]
-        half = time_step
-        if line < STEPS:
-            half = half * line_inside(line)
-        if wide:
-            half = half * row_mask
-        new[0, line] = old[0, line] - half * ((ez_next - ez) - (ahead_depth(ey) - ey))
-        new[1, line] = old[1, line] - half * ((ahead_depth(ex) - ex) - (ahead_row(ez) - ez))
-        new[2, line] = old[2, line] - half * ((ahead_row(ey) - ey) - (ex_next - ex))
-
-    def electric_line(n, line, weight):
+        ex, ey, ez = [blocks(E[n], c, line) for c in range(3)]
+        ex_next, ez_next = blocks(E[n], 0, line + 1), blocks(E[n], 2, line + 1)
+        hx, hy, hz = [blocks(old, c, line) for c in range(3)]
+        ey_ahead, ez_ahead = ahead_row(ey), ahead_row(ez)
+        for b in every:
+            curls = (
+                (ez_next[b] - ez[b]) - (ahead_depth(ey[b]) - ey[b]),
+                (ahead_depth(ex[b]) - ex[b]) - (ez_ahead[b] - ez[b]),
+                (ey_ahead[b] - ey[b]) - (ex_next[b] - ex[b]),
+            )
+            if line < STEPS:
+                curls = [curl * line_inside(line) for curl in curls]
+            if wide:
+                curls = [curl * row_mask[8 * b : 8 * b + 8] for curl in curls]
+            for c, h in enumerate((hx, hy, hz)):
+                settle(new, c, line, b, h[b] - curls[c])
+
+    def electric_line(n, line):
         field = H[(n + 1) % 2]
-        hx, hy, hz = field[0, line], field[1, line], field[2, line]
-        hx_last, hz_last = field[0, line - 1], field[2, line - 1]
-        curls = (
-            (hz - hz_last) - (hy - behind_depth(hy)),
-            (hx - behind_depth(hx)) - (hz - behind_row(hz)),
-            (hy - behind_row(hy)) - (hx - hx_last),
-        )
-        reach = coef[0, line]
-        for c in range(3):
-            e = E[n][c, line]
-            curl = curls[c]
-            if n > 0:
-                p, j = Pol[(n + 1) % 2][c, line], J[(n + 1) % 2][c, line]
-                if n == 1:
-                    j = j + coef[3, line] * e
-                else:
-                    j = coef[1, line] * j + coef[3, line] * e - coef[2, line] * p
-                if n < STEPS - 1:
-                    J[n % 2][c, line] = j
-                    Pol[n % 2][c, line] = p + time_step * j
-                curl = curl - j
-            drawn = source_rows * (weight * source[c, line : line + 1, :])
-            E[n + 1][c, line] = e + reach * (curl - drawn)
+        hx, hy, hz = [blocks(field, c, line) for c in range(3)]
+        hx_last, hz_last = blocks(field, 0, line - 1), blocks(field, 2, line - 1)
+        hy_behind, hz_behind = behind_row(hy), behind_row(hz)
+        for b in every if n + 1 < STEPS else own:
+            rows = slice(8 * b, 8 * b + 8)
+            curls = (
+                (hz[b] - hz_last[b]) - (hy[b] - behind_depth(hy[b])),
+                (hx[b] - behind_depth(hx[b])) - (hz[b] - hz_behind[b]),
+                (hy[b] - hy_behind[b]) - (hx[b] - hx_last[b]),
+            )
+            reach = coef[0, line, rows, :]
+            for c in range(3):
+                e = E[n][c, line, rows, :]
+                curl = curls[c]
+                if n > 0:
+                    p, j = Pol[(n + 1) % 2][c, line, rows, :], J[(n + 1) % 2][c, line, rows, :]
+                    if n == 1:
+                        j = j + coef[3, line, rows, :] * e
+                    else:
+                        j = coef[1, line, rows, :] * j + coef[3, line, rows, :] * e - coef[2, line, rows, :] * p
+                    if n < STEPS - 1:
+                        J[n % 2][c, line, rows, :] = j
+                        Pol[n % 2][c, line, rows, :] = p + j
+                    curl = curl - j
+                drawn = source_rows[rows, :] * sources[n, c, line : line + 1, :]
+                settle(E[n + 1], c, line, b, e + reach * (curl - drawn))
 
     for n in range(STEPS):
-        weight = jnp.where(low_row, waveforms[0, n], waveforms[1, n])
         for line in range(n, EXT_LINES - 1 - n) if n > 0 else ():
             magnetic_line(n, line)
         for line in range(n + 1, EXT_LINES - 1 - n):
-            electric_line(n, line, weight)
+            electric_line(n, line)
 
     low_tile = low[:ROWS]
-    row_tile = lax.broadcasted_iota(jnp.int32, (ROWS, LANES), 0) + tx * ROWS
-    design_tile = (
-        (row_tile >= box[0]) & (row_tile < box[1]) & in_z[:ROWS]
-    ).astype(jnp.float32) * contrast
+
+    def turned(line):
+        return [[half_turn(E[n][c, line, middle, :]) for n in (5, 4, 3)] for c in range(3)]
+
+    totals, following = [], turned(STEPS)
+    for own_line in range(LINES):
+        line, (x, y, z) = STEPS + own_line, following
+        if own_line + 1 < LINES:
+            following = turned(line + 1)
+        terms = []
+        for c, (five, four, three) in enumerate((x, y, z)):
+            one, two = E[1][c, line, middle, :], E[2][c, line, middle, :]
+            zero_low = jnp.where(low_tile, start[c, own_line], 0.0)
+            three_low = jnp.where(low_tile, E[3][c, line, middle, :], 0.0)
+            terms.append(five * (one - zero_low) + four * (two - one) + three * (three_low - two))
+            electric_out[c, own_line] = E[STEPS][c, line, middle, :]
+        totals.append((terms[0] + terms[1] + terms[2]) * design[line, middle, :])
+    folded = [total + half_turn(total) for total in totals]
     for k in range(CHUNKS):
-        sums = []
-        for half in range(2):
-            line = STEPS + 2 * k + half
-            total = jnp.zeros((ROWS, LANES), jnp.float32)
-            for c in range(3):
-                history = [start[c, 2 * k + half]]
-                history += [E[n][c, line, middle, :] for n in range(1, STEPS + 1)]
-                for n in range(1, STEPS + 1):
-                    total = total + half_turn(history[STEPS + 1 - n]) * (history[n] - history[n - 1])
-                electric_out[c, 2 * k + half] = history[STEPS]
-            sums.append(total * (design_tile * line_design(line)))
-        gradient_out[:, k * LANES : (k + 1) * LANES] = jnp.where(low_tile, sums[0], half_turn(sums[1]))
+        gradient_out[:, k * LANES : (k + 1) * LANES] = jnp.where(low_tile, folded[2 * k], folded[2 * k + 1])
 
 
 def emit_kernel(electric, out):
@@ -646,10 +713,28 @@
         arrived.append(swap(message, along_x(kind) if i % 3 == 0 else corner(kind, i % 3 == 2)))
 
     ext = (EXT_LINES, ROWS + (PAD if tx_count == 2 else 2 * PAD), LANES)
+    prepared = pl.pallas_call(
+        functools.partial(prepare_kernel, tx_count, ty_count),
+        out_shape=(f32(STEPS, 3, EXT_LINES + 6, LANES), f32(*ext[1:]), f32(*ext), f32(16, LANES)),
+        in_specs=[hbm] * 4 + [vmem],
+        out_specs=(vmem,) * 4,
+        scratch_shapes=[
+            pltpu.SMEM((2, STEPS), jnp.float32),
+            pltpu.SMEM((NMAT, 4), jnp.float32),
+            pltpu.SMEM((2,), jnp.int32),
+            pltpu.SMEM((6,), jnp.int32),
+            pltpu.SemaphoreType.DMA((4,)),
+        ],
+        compiler_params=pltpu.CompilerParams(vmem_limit_bytes=16 * 1024 * 1024),
+        name="prepare",
+    )(
+        *[in_hbm(v) for v in (source_waveforms[0], material_table, plane_indices, design_box)],
+        source_profiles[0].transpose(1, 0, 2),
+    )
     electric, partial = pl.pallas_call(
         functools.partial(window_kernel, tx_count, ty_count),
         out_shape=(f32(3, LINES, ROWS, LANES), f32(ROWS, LINES * NZ)),
-        in_specs=[hbm] * 4 + [vmem] * (5 + len(arrived)),
+        in_specs=[vmem] * (8 + len(arrived)),
         out_specs=(vmem, vmem),
         scratch_shapes=[
             [pltpu.VMEM((3,) + ext, jnp.float32) for _ in range(STEPS + 1)],
@@ -658,19 +743,12 @@
             [pltpu.VMEM((3,) + ext, jnp.float32) for _ in range(2)],
             pltpu.VMEM(ext, jnp.float32),
             pltpu.VMEM((4,) + ext, jnp.float32),
-            pltpu.VMEM((3, EXT_LINES + 6, LANES), jnp.float32),
             pltpu.VMEM((2, EXT_LINES + 6, LANES), jnp.float32),
-            pltpu.SMEM((2, STEPS), jnp.float32),
-            pltpu.SMEM((NMAT, 4), jnp.float32),
-            pltpu.SMEM((2,), jnp.int32),
-            pltpu.SMEM((6,), jnp.int32),
-            pltpu.SemaphoreType.DMA((4,)),
         ],
         compiler_params=pltpu.CompilerParams(vmem_limit_bytes=48 * 1024 * 1024),
         name="window",
     )(
-        *[in_hbm(v) for v in (source_waveforms[0], material_table, plane_indices, design_box)],
-        source_profiles[0].transpose(1, 0, 2),
+        *prepared,
         tile,
         start,
         y_a,

time: 24.8 us -> 24.2 us (0.976)
  the two profiles are of different devices: /device:TPU:16 before, /device:TPU:17 now
where the time goes in v6:
time: 24.2 us; the launch traced here: 24 us
  waiting for transfers between devices  9.57 us (40%)
  starting transfers between devices  7.72 us (32%)
  Pallas kernels  5.45 us (23%)
  between operations  0.67 us (3%)
  other arithmetic  0.63 us (3%)
    ppermute x5, waiting for transfers between devices, swap(): return lax.ppermute(value, ('wave', 'tx', 'ty'), pairs)  7.48 us
    ppermute x5, starting transfers between devices, swap(): return lax.ppermute(value, ('wave', 'tx', 'ty'), pairs)  4.08 us
    ppermute x3, starting transfers between devices, on_device(): lax.ppermute(partial, 'wave', [(i, i ^ k) for i in range(4)])  3.64 us
    ppermute x3, waiting for transfers between devices, on_device(): lax.ppermute(partial, 'wave', [(i, i ^ k) for i in range(4)])  2.09 us
    pallas_call x1, Pallas kernels, on_device(): pl.pallas_call(functools.partial(window_kernel, tx_count, ty_count), out_...  2.02 us
    pallas_call x1, Pallas kernels, on_device(): pl.pallas_call(pack_kernel, out_shape=(f32(FIELDS, LINES, ROWS, LANES), f...  1.64 us
    pallas_call x1, Pallas kernels, on_device(): pl.pallas_call(functools.partial(prepare_kernel, tx_count, ty_count), out...  0.94 us
    pallas_call x1, Pallas kernels, on_device(): pl.pallas_call(emit_kernel, out_shape=f32(1, 2, 3, ROWS, LINES * NZ), in_...  0.79 us
  transfers between devices with their start and end apart: 8, of which 4 were waited for; matrix products, arithmetic and copies ran while one was open for 0% of the time, Pallas kernels for 7%

profile of v6, /device:TPU:17, one launch (start us, length us, event | category | flops | bytes accessed | tf_op | source)
XLA Modules:
  0.0 24.0 jit_solution(13843772446888567529)
XLA Ops:
  0.6 1.6 %pack.1 = (f32[13,8,16,128]{3,2,1,0:T(8,128)S(1)}, f32[3,8,16,128]{3,2,1,0:T(8,128)S(1)}, f32[46,16,128]{2,1,0:T(8,128)S(1)}, f32[46,16,128]{2,1,0:T(8,128)S(1)}) custom-call(f32[3,4]{1,0:T(4,128)} %table_hbm.3, s32[6]{0:T(128)} %box_hbm.3, f32[1,2,12,16,512]{4,3,2,1,0:T(8,128)} %fields_hbm.1, s32[16,512]{1,0:T(8,128)} %material_hbm.1, f32[16,512]{1,0:T(8,128)} %density_hbm.1), custom_call_target="tpu_custom_call" | custom-call | tf_op jit(solution)/shard_map/pack/pallas_call | solution.py:678
  2.3 1.4 %collective-permute-start = (f32[46,16,128]{2,1,0:T(8,128)S(1)}, f32[46,16,128]{2,1,0:T(8,128)S(1)}, u32[]{:S(2)}, u32[]{:S(2)}) collective-permute-start(f32[46,16,128]{2,1,0:T(8,128)S(1)} %get-tuple-element.21), channel_id=1, source_target_pairs={{0,1},{1,0},{2,3},{3,2},{4,5},{5,4},{6,7},{7,6},{8,9},{9,8},{10,11... | collective-permute-start | bytes 1130504 | tf_op jit(solution)/shard_map/ppermute | solution.py:667
  3.6 0.0 collective-permute-start.1
  3.6 0.0 copy-start
  3.6 0.1 edges.1
  3.7 1.3 %collective-permute-start.2 = (f32[376,128]{1,0:T(8,128)S(1)}, f32[376,128]{1,0:T(8,128)S(1)}, u32[]{:S(2)}, u32[]{:S(2)}) collective-permute-start(f32[376,128]{1,0:T(8,128)S(1)} %get-tuple-element.23), channel_id=1, source_target_pairs={{0,4},{1,5},{2,6},{3,7},{4,0},{5,1},{6,2},{7,3},{8,12},{9,13},{10,... | collective-permute-start | bytes 577544 | tf_op jit(solution)/shard_map/ppermute | solution.py:667
  5.0 1.4 %collective-permute-start.4 = (f32[88,128]{1,0:T(8,128)S(1)}, f32[88,128]{1,0:T(8,128)S(1)}, u32[]{:S(2)}, u32[]{:S(2)}) collective-permute-start(f32[88,128]{1,0:T(8,128)S(1)} %get-tuple-element.25), channel_id=1, source_target_pairs={{0,8},{1,4},{2,5},{3,6},{4,1},{5,2},{6,3},{7,15},{8,0},{9,12},{10,... | collective-permute-start | bytes 135176 | tf_op jit(solution)/shard_map/ppermute | solution.py:667
  6.4 0.0 collective-permute-start.3
  6.4 0.0 copy-done
  6.4 0.9 %prepare.1 = (f32[5,3,24,128]{3,2,1,0:T(8,128)S(1)}, f32[24,128]{1,0:T(8,128)S(1)}, f32[18,24,128]{2,1,0:T(8,128)S(1)}, f32[16,128]{1,0:T(8,128)S(1)}) custom-call(f32[2,5]{1,0:T(2,128)} %bitcast.5, f32[3,4]{1,0:T(4,128)} %table_hbm.3, s32[2]{0:T(128)} %plane_hbm.1, s32[6]{0:T(128)} %box_hbm.3, f32[3,2,2048]{2,1,0:T(2,128)S(1)} %bitcast.4), custom_call_target="tpu_custom_call" | custom-call | tf_op jit(solution)/shard_map/prepare/pallas_call | solution.py:716
  7.4 6.0 %collective-permute-done.3.rest_1_ = f32[72,128]{1,0:T(8,128)S(1)} collective-permute-done((f32[72,128]{1,0:T(8,128)S(1)}, f32[72,128]{1,0:T(8,128)S(1)}, u32[]{:S(2)}, u32[]{:S(2)}) %collective-permute-start.3) | collective-permute-done | bytes 36896 | tf_op jit(solution)/shard_map/ppermute | solution.py:667
  13.4 1.4 %collective-permute-done.4.rest_2_ = f32[88,128]{1,0:T(8,128)S(1)} collective-permute-done((f32[88,128]{1,0:T(8,128)S(1)}, f32[88,128]{1,0:T(8,128)S(1)}, u32[]{:S(2)}, u32[]{:S(2)}) %collective-permute-start.4) | collective-permute-done | bytes 45088 | tf_op jit(solution)/shard_map/ppermute | solution.py:667
  14.8 0.0 collective-permute-done.2.rest_0_
  14.9 0.0 collective-permute-done.y_a
  14.9 0.0 collective-permute-done.1.y_b
  14.9 2.0 %window.1 = (f32[3,8,16,128]{3,2,1,0:T(8,128)S(1)}, f32[16,512]{1,0:T(8,128)S(1)}) custom-call(f32[5,3,24,128]{3,2,1,0:T(8,128)S(1)} %get-tuple-element.15.sources, f32[24,128]{1,0:T(8,128)S(1)} %get-tuple-element.16.source_rows, f32[18,24,128]{2,1,0:T(8,128)S(1)} %get-tuple-element.17.design, f32[16,128]{1,0:T(8,128)S(1)} %get-tuple-element.18.poles, ...), custom_call_target="tpu_custom_call" | custom-call | tf_op jit(solution)/shard_map/window/pallas_call | solution.py:734
  16.9 1.9 %collective-permute-start.5 = (f32[16,512]{1,0:T(8,128)S(1)}, f32[16,512]{1,0:T(8,128)S(1)}, u32[]{:S(2)}, u32[]{:S(2)}) collective-permute-start(f32[16,512]{1,0:T(8,128)S(1)} %get-tuple-element.26), channel_id=1, source_target_pairs={{0,8},{8,0},{16,24},{24,16},{1,9},{9,1},{17,25},{25,17},{2,10},{10... | collective-permute-start | bytes 98312 | tf_op jit(solution)/shard_map/ppermute | solution.py:769
  18.8 1.3 %collective-permute-start.6 = (f32[16,512]{1,0:T(8,128)S(1)}, f32[16,512]{1,0:T(8,128)S(1)}, u32[]{:S(2)}, u32[]{:S(2)}) collective-permute-start(f32[16,512]{1,0:T(8,128)S(1)} %get-tuple-element.26), channel_id=1, source_target_pairs={{0,16},{8,24},{16,0},{24,8},{1,17},{9,25},{17,1},{25,9},{2,18},{10... | collective-permute-start | bytes 98312 | tf_op jit(solution)/shard_map/ppermute | solution.py:769
  20.1 0.5 %collective-permute-start.7 = (f32[16,512]{1,0:T(8,128)S(1)}, f32[16,512]{1,0:T(8,128)S(1)}, u32[]{:S(2)}, u32[]{:S(2)}) collective-permute-start(f32[16,512]{1,0:T(8,128)S(1)} %get-tuple-element.26), channel_id=1, source_target_pairs={{0,24},{8,16},{16,8},{24,0},{1,25},{9,17},{17,9},{25,1},{2,26},{10... | collective-permute-start | bytes 98312 | tf_op jit(solution)/shard_map/ppermute | solution.py:769
  20.5 0.8 %emit.1 = f32[1,2,3,16,512]{4,3,2,1,0:T(8,128)} custom-call(f32[3,8,16,128]{3,2,1,0:T(8,128)S(1)} %get-tuple-element.27.electric), custom_call_target="tpu_custom_call" | custom-call | tf_op jit(solution)/shard_map/emit/pallas_call | solution.py:758
  21.3 0.0 collective-permute-done.5
  21.3 0.3 %collective-permute-done.6 = f32[16,512]{1,0:T(8,128)S(1)} collective-permute-done((f32[16,512]{1,0:T(8,128)S(1)}, f32[16,512]{1,0:T(8,128)S(1)}, u32[]{:S(2)}, u32[]{:S(2)}) %collective-permute-start.6) | collective-permute-done | bytes 32800 | tf_op jit(solution)/shard_map/ppermute | solution.py:769
  21.6 1.8 %collective-permute-done.7 = f32[16,512]{1,0:T(8,128)S(1)} collective-permute-done((f32[16,512]{1,0:T(8,128)S(1)}, f32[16,512]{1,0:T(8,128)S(1)}, u32[]{:S(2)}, u32[]{:S(2)}) %collective-permute-start.7) | collective-permute-done | bytes 32800 | tf_op jit(solution)/shard_map/ppermute | solution.py:769
  23.4 0.6 %add_add_fusion = f32[16,512]{1,0:T(8,128)} fusion(f32[16,512]{1,0:T(8,128)S(1)} %collective-permute-done.6, f32[16,512]{1,0:T(8,128)S(1)} %collective-permute-done.7, f32[16,512]{1,0:T(8,128)S(1)} %get-tuple-element.26, f32[16,512]{1,0:T(8,128)S(1)} %collective-permute-done.5), kind=kLoop, calls=%fused_computation | loop fusion | flops 24576 | bytes 163840 | tf_op jit(solution)/shard_map/add | solution.py:771
Async XLA Ops:
  2.3 12.6 %collective-permute-start = (f32[46,16,128]{2,1,0:T(8,128)S(1)}, f32[46,16,128]{2,1,0:T(8,128)S(1)}, u32[]{:S(2)}, u32[]{:S(2)}) collective-permute-start(f32[46,16,128]{2,1,0:T(8,128)S(1)} %get-tuple-element.21), channel_id=1, source_target_pairs={{0,1},{1,0},{2,3},{3,2},{4,5},{5,4},{6,7},{7,6},{8,9},{9,8},{10,11... | collective-permute-start | bytes 1130504 | tf_op jit(solution)/shard_map/ppermute | solution.py:667
  3.6 11.2 %collective-permute-start.1 = (f32[46,16,128]{2,1,0:T(8,128)S(1)}, f32[46,16,128]{2,1,0:T(8,128)S(1)}, u32[]{:S(2)}, u32[]{:S(2)}) collective-permute-start(f32[46,16,128]{2,1,0:T(8,128)S(1)} %get-tuple-element.22), channel_id=1, source_target_pairs={{0,8},{1,2},{2,1},{3,11},{4,12},{5,6},{6,5},{7,15},{8,0},{9,10},{1... | collective-permute-start | bytes 1130504 | tf_op jit(solution)/shard_map/ppermute | solution.py:667
  3.6 2.8 %copy-start = (f32[1,2,3,2048]{3,1,2,0:T(2,128)S(1)}, f32[1,2,3,2048]{3,1,2,0:T(2,128)}, u32[]{:S(2)}) copy-start(f32[1,2,3,2048]{3,1,2,0:T(2,128)} %param.9) | copy-start | bytes 147460
  3.7 11.1 %collective-permute-start.2 = (f32[376,128]{1,0:T(8,128)S(1)}, f32[376,128]{1,0:T(8,128)S(1)}, u32[]{:S(2)}, u32[]{:S(2)}) collective-permute-start(f32[376,128]{1,0:T(8,128)S(1)} %get-tuple-element.23), channel_id=1, source_target_pairs={{0,4},{1,5},{2,6},{3,7},{4,0},{5,1},{6,2},{7,3},{8,12},{9,13},{10,... | collective-permute-start | bytes 577544 | tf_op jit(solution)/shard_map/ppermute | solution.py:667
  5.0 9.9 %collective-permute-start.4 = (f32[88,128]{1,0:T(8,128)S(1)}, f32[88,128]{1,0:T(8,128)S(1)}, u32[]{:S(2)}, u32[]{:S(2)}) collective-permute-start(f32[88,128]{1,0:T(8,128)S(1)} %get-tuple-element.25), channel_id=1, source_target_pairs={{0,8},{1,4},{2,5},{3,6},{4,1},{5,2},{6,3},{7,15},{8,0},{9,12},{10,... | collective-permute-start | bytes 135176 | tf_op jit(solution)/shard_map/ppermute | solution.py:667
  6.4 7.0 %collective-permute-start.3 = (f32[72,128]{1,0:T(8,128)S(1)}, f32[72,128]{1,0:T(8,128)S(1)}, u32[]{:S(2)}, u32[]{:S(2)}) collective-permute-start(f32[72,128]{1,0:T(8,128)S(1)} %get-tuple-element.24), channel_id=1, source_target_pairs={{0,5},{1,6},{2,7},{3,11},{4,12},{5,0},{6,1},{7,2},{8,13},{9,14},{1... | collective-permute-start | bytes 110600 | tf_op jit(solution)/shard_map/ppermute | solution.py:667
  16.9 4.4 %collective-permute-start.5 = (f32[16,512]{1,0:T(8,128)S(1)}, f32[16,512]{1,0:T(8,128)S(1)}, u32[]{:S(2)}, u32[]{:S(2)}) collective-permute-start(f32[16,512]{1,0:T(8,128)S(1)} %get-tuple-element.26), channel_id=1, source_target_pairs={{0,8},{8,0},{16,24},{24,16},{1,9},{9,1},{17,25},{25,17},{2,10},{10... | collective-permute-start | bytes 98312 | tf_op jit(solution)/shard_map/ppermute | solution.py:769
  18.8 2.8 %collective-permute-start.6 = (f32[16,512]{1,0:T(8,128)S(1)}, f32[16,512]{1,0:T(8,128)S(1)}, u32[]{:S(2)}, u32[]{:S(2)}) collective-permute-start(f32[16,512]{1,0:T(8,128)S(1)} %get-tuple-element.26), channel_id=1, source_target_pairs={{0,16},{8,24},{16,0},{24,8},{1,17},{9,25},{17,1},{25,9},{2,18},{10... | collective-permute-start | bytes 98312 | tf_op jit(solution)/shard_map/ppermute | solution.py:769
  20.1 3.3 %collective-permute-start.7 = (f32[16,512]{1,0:T(8,128)S(1)}, f32[16,512]{1,0:T(8,128)S(1)}, u32[]{:S(2)}, u32[]{:S(2)}) collective-permute-start(f32[16,512]{1,0:T(8,128)S(1)} %get-tuple-element.26), channel_id=1, source_target_pairs={{0,24},{8,16},{16,8},{24,0},{1,25},{9,17},{17,9},{25,1},{2,26},{10... | collective-permute-start | bytes 98312 | tf_op jit(solution)/shard_map/ppermute | solution.py:769

commit v7 on v6

--- a/solution.py
+++ b/solution.py
@@ -118,56 +118,56 @@
         )
     ]
     chunks = [
-        pltpu.make_async_copy(
-            fields_hbm.at[0, :, :, :, pl.ds(k * LANES, LANES)], fields.at[k], sems.at[k]
-        )
-        for k in range(CHUNKS)
+        pltpu.make_async_copy(fields_hbm.at[0, :, :, pl.ds(8 * b, 8), :], fields.at[b], sems.at[b])
+        for b in range(ROWS // 8)
     ]
     for copy in copies + chunks:
         copy.start()
     for copy in copies:
         copy.wait()
     decay, drive, coupled = pole(table)
-    shape = (ROWS, LANES)
-    low = low_lanes(shape)
-    lane = lax.broadcasted_iota(jnp.int32, shape, 1)
+    block = (8, LANES)
+    low = low_lanes(block)
+    lane = lax.broadcasted_iota(jnp.int32, block, 1)
     depth_id = jnp.where(low, lane, lane - NZ)
-    last_z = depth_id == NZ - 1
-    row = lax.broadcasted_iota(jnp.int32, shape, 0) + lax.axis_index("tx") * ROWS
+    last_z = (jnp.concatenate([depth_id, depth_id], axis=0) == NZ - 1)
     in_z = (depth_id >= box[4]) & (depth_id < box[5])
-    design_rows = ((row >= box[0]) & (row < box[1]) & in_z).astype(jnp.float32)
     first_line = lax.axis_index("ty") * LINES
-    for k in range(CHUNKS):
-        at = slice(k * LANES, (k + 1) * LANES)
-        chunks[k].wait()
-
-        def split(one, two):
-            return jnp.where(low, one, half_turn(two)), jnp.where(low, half_turn(one), two)
-
-        pairs = [split(fields[k, 0, f], fields[k, 1, f]) for f in range(12)]
-        mat, dens = material[:, at].astype(jnp.float32), density[:, at]
-        turned = half_turn(mat)
-        mats = (jnp.where(low, mat, turned), jnp.where(low, turned, mat))
-        turned = half_turn(dens)
-        denses = (jnp.where(low, dens, turned), jnp.where(low, turned, dens))
-        for half in range(2):
-            line = 2 * k + half
-            mat, dens = mats[half], denses[half]
-            where = first_line + line
-            design = design_rows * ((where >= box[2]) & (where < box[3])).astype(jnp.float32)
-            permittivity = choose(mat, lambda m: table[m, 0]) + design * dens * contrast
-            reach = time_step * 0.5 / permittivity
-            dec, dri, cou = [choose(mat, column) for column in (decay, drive, coupled)]
-            for c in range(3):
-                e, p, j = pairs[c][half], 4.0 * pairs[6 + c][half], 2.0 * pairs[9 + c][half]
-                j = dec * j + cou * e - dri * p
-                p = p + j
-                start[c, line] = e
-                tile[c, line] = e - reach * j
-                tile[3 + c, line] = 2.0 * pairs[3 + c][half]
-                tile[6 + c, line] = p
-                tile[9 + c, line] = dec * j - dri * p
-            tile[12, line] = jnp.where(low, mat, dens)
+
+    def split(one, two):
+        return jnp.where(low, one, half_turn(two)), jnp.where(low, half_turn(one), two)
+
+    for b in range(ROWS // 8):
+        rows = slice(8 * b, 8 * b + 8)
+        row = lax.broadcasted_iota(jnp.int32, block, 0) + (lax.axis_index("tx") * ROWS + 8 * b)
+        design_rows = ((row >= box[0]) & (row < box[1]) & in_z).astype(jnp.float32)
+        chunks[b].wait()
+        for k in range(CHUNKS):
+            at = slice(k * LANES, (k + 1) * LANES)
+            pairs = [split(fields[b, 0, f, :, at], fields[b, 1, f, :, at]) for f in range(12)]
+            mat, dens = material[rows, at].astype(jnp.float32), density[rows, at]
+            turned = half_turn(mat)
+            mats = (jnp.where(low, mat, turned), jnp.where(low, turned, mat))
+            turned = half_turn(dens)
+            denses = (jnp.where(low, dens, turned), jnp.where(low, turned, dens))
+            for half in range(2):
+                line = 2 * k + half
+                mat, dens = mats[half], denses[half]
+                where = first_line + line
+                design = design_rows * ((where >= box[2]) & (where < box[3])).astype(jnp.float32)
+                permittivity = choose(mat, lambda m: table[m, 0]) + design * dens * contrast
+                reach = time_step * 0.5 / permittivity
+                dec, dri, cou = [choose(mat, column) for column in (decay, drive, coupled)]
+                for c in range(3):
+                    e, p, j = pairs[c][half], 4.0 * pairs[6 + c][half], 2.0 * pairs[9 + c][half]
+                    j = dec * j + cou * e - dri * p
+                    p = p + j
+                    start[c, line, rows, :] = e
+                    tile[c, line, rows, :] = e - reach * j
+                    tile[3 + c, line, rows, :] = 2.0 * pairs[3 + c][half]
+                    tile[6 + c, line, rows, :] = p
+                    tile[9 + c, line, rows, :] = dec * j - dri * p
+                tile[12, line, rows, :] = jnp.where(low, mat, dens)
 
     edge = jnp.zeros((1, LANES), jnp.float32)
 
@@ -182,7 +182,7 @@
         if line + 1 < LINES:
             ex_next, ez_next = start[0, line + 1], start[2, line + 1]
         else:
-            ex_next = ez_next = jnp.zeros(shape, jnp.float32)
+            ex_next = ez_next = jnp.zeros((ROWS, LANES), jnp.float32)
         tile[3, line] = tile[3, line] - ((ez_next - ez) - (ahead_depth(ey) - ey))
         tile[4, line] = tile[4, line] - ((ahead_depth(ex) - ex) - (ahead_row(ez) - ez))
         tile[5, line] = tile[5, line] - ((ahead_row(ey) - ey) - (ex_next - ex))
@@ -317,22 +317,23 @@
     return at + tx * ROWS - PAD
 
 
-def window_kernel(
-    tx_count,
-    ty_count,
-    sources,
-    source_rows,
-    design,
-    poles,
-    tile,
-    start,
-    y_a,
-    y_b,
-    *rest,
-):
+def window_part(early, late, tx_count, ty_count, *refs):
+    *most, one, two = refs
+    window_kernel(early, late, tx_count, ty_count, *most, (one, two))
+
+
+def window_kernel(early, late, tx_count, ty_count, *refs):
     kinds = 1 if tx_count == 2 else 2
-    messages, rest = rest[: 3 * kinds], rest[3 * kinds :]
-    electric_out, gradient_out, E, H, Pol, J, C, coef, first_row = rest
+    refs = list(refs)
+    sources, source_rows, design, poles, start = [refs.pop(0) for _ in range(5)]
+    tile, y_a, y_b = [refs.pop(0) for _ in range(3)] if early else (None,) * 3
+    messages = [refs.pop(0) for _ in range(3 * kinds)] if late else []
+    if late and not early:
+        refs.pop(0)
+    electric_out, gradient_out = [refs.pop(0) for _ in range(2)] if late else (None, None)
+    (E, H, Pol, J, C, coef, first_row), (Pol_next, J_next) = refs if len(refs) == 2 else (refs[:-1], refs[-1])
+    H = [None] + list(H)
+    Pol, J = (Pol, Pol_next), (J, J_next)
     wide = tx_count != 2
     ext_rows = E[0].shape[2]
     tx, ty = lax.axis_index("tx"), lax.axis_index("ty")
@@ -353,7 +354,9 @@
             for line in lines:
                 put(f, line, rows, jnp.zeros((count, LANES), jnp.float32))
 
-    every_row, behind_lines, ahead_lines = slice(0, ext_rows), range(STEPS), range(STEPS + LINES, EXT_LINES)
+    every_row = slice(0 if early else ROWS, ext_rows if late else ROWS)
+    row_count = every_row.stop - every_row.start
+    behind_lines, ahead_lines = range(STEPS), range(STEPS + LINES, EXT_LINES)
     no_behind, no_ahead = ty == 0, ty + 1 == ty_count
     if wide:
 
@@ -367,16 +370,17 @@
 
     @pl.when(no_behind)
     def _():
-        clear(behind_lines, every_row, ext_rows)
+        clear(behind_lines, every_row, row_count)
 
     @pl.when(no_ahead)
     def _():
-        clear(ahead_lines, every_row, ext_rows)
-
-    for f in range(FIELDS):
-        for line in range(LINES):
-            put(f, STEPS + line, middle, tile[f, line])
-    if not wide:
+        clear(ahead_lines, every_row, row_count)
+
+    if early:
+        for f in range(FIELDS):
+            for line in range(LINES):
+                put(f, STEPS + line, middle, tile[f, line])
+    if late and not wide:
         H[1][1:3, :, ROWS:ext_rows, :] = jnp.zeros((2, EXT_LINES, PAD, LANES), jnp.float32)
 
     def near(ahead, k):
@@ -392,7 +396,7 @@
         H[1][2, line, at, :] = H[1][2, line, at, :] - ey
 
     lower = is_lower_in_a()
-    for message, is_lower in ((y_a, lower), (y_b, jnp.logical_not(lower))):
+    for message, is_lower in ((y_a, lower), (y_b, jnp.logical_not(lower))) if early else ():
         for ahead in (False, True):
 
             @pl.when(jnp.logical_and(is_lower == ahead, jnp.logical_not(no_ahead if ahead else no_behind)))
@@ -409,7 +413,7 @@
                 else:
                     correct_line(STEPS - 1, middle, start[0, 0], start[2, 0])
 
-    for kind in range(kinds):
+    for kind in range(kinds if late else 0):
         along, same, mixed = messages[3 * kind : 3 * kind + 3]
         for ahead in (False, True):
             in_x = tx + 1 < tx_count if ahead else tx > 0
@@ -472,9 +476,9 @@
                     else:
                         rows_own([near(True, k) for k in range(4)])
 
-    shape = (ext_rows, LANES)
+    shape = (row_count, LANES)
     low = low_lanes(shape)
-    row = window_rows(tx_count, shape)
+    row = window_rows(tx_count, (ext_rows, LANES))
     row_mask = ((row >= 0) & (row < rows_all)).astype(jnp.float32)
 
     def line_inside(line):
@@ -485,42 +489,63 @@
         return STEPS <= line < STEPS + LINES
 
     for line in range(1, EXT_LINES - 1):
-        mixed = C[line]
+        mixed = C[line, every_row, :]
         turned = half_turn(mixed)
         mat = jnp.where(low, mixed, turned)
         dens = jnp.where(low, turned, mixed)
         eps, *others = [
             choose(mat, lambda m, i=i: poles[NMAT * i + m : NMAT * i + m + 1, :]) for i in range(4)
         ]
-        reach = time_step * 0.5 / (eps + design[line] * dens)
+        reach = time_step * 0.5 / (eps + design[line, every_row, :] * dens)
         if wide:
             reach = reach * row_mask
         if not is_own(line):
             reach = reach * line_inside(line)
-        coef[0, line] = reach
+        coef[0, line, every_row, :] = reach
         for i, value in enumerate(others):
-            coef[1 + i, line] = value
+            coef[1 + i, line, every_row, :] = value
 
     count = ext_rows // 8
     block = (8, LANES)
     lane = lax.broadcasted_iota(jnp.int32, block, 1)
-    depth_id = jnp.where(low[:8], lane, lane - NZ)
+    depth_id = jnp.where(low_lanes(block), lane, lane - NZ)
     first_z, last_z = depth_id == 0, depth_id == NZ - 1
     sub = lax.broadcasted_iota(jnp.int32, block, 0)
     first_sub, last_sub = sub == 0, sub == 7
     sent = sub + tx * (7 - 2 * sub) < STEPS
-    every, own = range(count), range(tile_row // 8, (tile_row + ROWS) // 8)
+    own = range(tile_row // 8, (tile_row + ROWS) // 8)
+    if early:
+        made = {b: ((b - 1) % count, (b + 1) % count) for b in (range(count) if late else own)}
+        own_made = list(own)
+    else:
+        beside = 1 - tx
+        made = {2: (1, 0), "beside": (lax.rem(beside + 2, 3), beside + 1)}
+        own_made = ["beside"]
+
+    def rows_of(b):
+        if isinstance(b, int):
+            return slice(8 * b, 8 * b + 8)
+        return pl.ds(pl.multiple_of(8 * (beside if isinstance(b, str) else b), 8), 8)
+
+    def block_of(ref, c, line, b):
+        if isinstance(b, int) and not late and b not in own:
+            return jnp.zeros(block, jnp.float32)
+        return ref[c, line, rows_of(b), :]
 
     def blocks(ref, c, line):
-        return [ref[c, line, 8 * b : 8 * b + 8, :] for b in every]
-
-    def ahead_row(v):
-        turned = [pltpu.roll(x, 7, 0) for x in v]
-        return [jnp.where(last_sub, turned[(b + 1) % count], turned[b]) for b in every]
-
-    def behind_row(v):
-        turned = [pltpu.roll(x, 1, 0) for x in v]
-        return [jnp.where(first_sub, turned[b - 1], turned[b]) for b in every]
+        return {b: block_of(ref, c, line, b) for b in made}
+
+    def ahead_row(ref, c, line, v):
+        return {
+            b: jnp.where(last_sub, pltpu.roll(block_of(ref, c, line, made[b][1]), 7, 0), pltpu.roll(v[b], 7, 0))
+            for b in made
+        }
+
+    def behind_row(ref, c, line, v):
+        return {
+            b: jnp.where(first_sub, pltpu.roll(block_of(ref, c, line, made[b][0]), 1, 0), pltpu.roll(v[b], 1, 0))
+            for b in made
+        }
 
     def ahead_depth(v):
         return jnp.where(last_z, 0.0, pltpu.roll(v, LANES - 1, 1))
@@ -529,17 +554,16 @@
         return jnp.where(first_z, 0.0, pltpu.roll(v, 1, 1))
 
     def settle(ref, c, line, b, value):
-        if not wide and b not in own:
+        if not wide and isinstance(b, int) and b not in own:
             value = jnp.where(sent, value, 0.0)
-        ref[c, line, 8 * b : 8 * b + 8, :] = value
+        ref[c, line, rows_of(b), :] = value
 
     def magnetic_line(n, line):
-        old, new = H[n % 2], H[(n + 1) % 2]
         ex, ey, ez = [blocks(E[n], c, line) for c in range(3)]
         ex_next, ez_next = blocks(E[n], 0, line + 1), blocks(E[n], 2, line + 1)
-        hx, hy, hz = [blocks(old, c, line) for c in range(3)]
-        ey_ahead, ez_ahead = ahead_row(ey), ahead_row(ez)
-        for b in every:
+        hx, hy, hz = [blocks(H[n], c, line) for c in range(3)]
+        ey_ahead, ez_ahead = ahead_row(E[n], 1, line, ey), ahead_row(E[n], 2, line, ez)
+        for b in made:
             curls = (
                 (ez_next[b] - ez[b]) - (ahead_depth(ey[b]) - ey[b]),
                 (ahead_depth(ex[b]) - ex[b]) - (ez_ahead[b] - ez[b]),
@@ -550,15 +574,15 @@
             if wide:
                 curls = [curl * row_mask[8 * b : 8 * b + 8] for curl in curls]
             for c, h in enumerate((hx, hy, hz)):
-                settle(new, c, line, b, h[b] - curls[c])
+                settle(H[n + 1], c, line, b, h[b] - curls[c])
 
     def electric_line(n, line):
-        field = H[(n + 1) % 2]
+        field = H[n + 1]
         hx, hy, hz = [blocks(field, c, line) for c in range(3)]
         hx_last, hz_last = blocks(field, 0, line - 1), blocks(field, 2, line - 1)
-        hy_behind, hz_behind = behind_row(hy), behind_row(hz)
-        for b in every if n + 1 < STEPS else own:
-            rows = slice(8 * b, 8 * b + 8)
+        hy_behind, hz_behind = behind_row(field, 1, line, hy), behind_row(field, 2, line, hz)
+        for b in made if n + 1 < STEPS else own_made:
+            rows = rows_of(b)
             curls = (
                 (hz[b] - hz_last[b]) - (hy[b] - behind_depth(hy[b])),
                 (hx[b] - behind_depth(hx[b])) - (hz[b] - hz_behind[b]),
@@ -569,14 +593,15 @@
                 e = E[n][c, line, rows, :]
                 curl = curls[c]
                 if n > 0:
-                    p, j = Pol[(n + 1) % 2][c, line, rows, :], J[(n + 1) % 2][c, line, rows, :]
+                    held = 0 if n == 1 else 1
+                    p, j = Pol[held][c, line, rows, :], J[held][c, line, rows, :]
                     if n == 1:
                         j = j + coef[3, line, rows, :] * e
                     else:
                         j = coef[1, line, rows, :] * j + coef[3, line, rows, :] * e - coef[2, line, rows, :] * p
                     if n < STEPS - 1:
-                        J[n % 2][c, line, rows, :] = j
-                        Pol[n % 2][c, line, rows, :] = p + j
+                        J[1][c, line, rows, :] = j
+                        Pol[1][c, line, rows, :] = p + j
                     curl = curl - j
                 drawn = source_rows[rows, :] * sources[n, c, line : line + 1, :]
                 settle(E[n + 1], c, line, b, e + reach * (curl - drawn))
@@ -587,7 +612,10 @@
         for line in range(n + 1, EXT_LINES - 1 - n):
             electric_line(n, line)
 
-    low_tile = low[:ROWS]
+    if not late:
+        return
+
+    low_tile = low_lanes((ROWS, LANES))
 
     def turned(line):
         return [[half_turn(E[n][c, line, middle, :]) for n in (5, 4, 3)] for c in range(3)]
@@ -688,7 +716,7 @@
         scratch_shapes=[
             pltpu.SMEM((NMAT, 4), jnp.float32),
             pltpu.SMEM((6,), jnp.int32),
-            pltpu.VMEM((CHUNKS, 2, 12, ROWS, LANES), jnp.float32),
+            pltpu.VMEM((ROWS // 8, 2, 12, 8, LINES * NZ), jnp.float32),
             pltpu.VMEM((ROWS, LINES * NZ), jnp.int32),
             pltpu.VMEM((ROWS, LINES * NZ), jnp.float32),
             pltpu.SemaphoreType.DMA((CHUNKS + 4,)),
@@ -731,30 +759,47 @@
         *[in_hbm(v) for v in (source_waveforms[0], material_table, plane_indices, design_box)],
         source_profiles[0].transpose(1, 0, 2),
     )
-    electric, partial = pl.pallas_call(
-        functools.partial(window_kernel, tx_count, ty_count),
-        out_shape=(f32(3, LINES, ROWS, LANES), f32(ROWS, LINES * NZ)),
-        in_specs=[vmem] * (8 + len(arrived)),
-        out_specs=(vmem, vmem),
-        scratch_shapes=[
-            [pltpu.VMEM((3,) + ext, jnp.float32) for _ in range(STEPS + 1)],
-            [pltpu.VMEM((3,) + ext, jnp.float32) for _ in range(2)],
-            [pltpu.VMEM((3,) + ext, jnp.float32) for _ in range(2)],
-            [pltpu.VMEM((3,) + ext, jnp.float32) for _ in range(2)],
-            pltpu.VMEM(ext, jnp.float32),
-            pltpu.VMEM((4,) + ext, jnp.float32),
-            pltpu.VMEM((2, EXT_LINES + 6, LANES), jnp.float32),
-        ],
-        compiler_params=pltpu.CompilerParams(vmem_limit_bytes=48 * 1024 * 1024),
-        name="window",
-    )(
-        *prepared,
-        tile,
-        start,
-        y_a,
-        y_b,
-        *arrived,
-    )
+    fields = f32(3, *ext)
+    state = ([fields] * (STEPS + 1), [fields] * STEPS, fields, fields, f32(*ext), f32(4, *ext), f32(2, EXT_LINES + 6, LANES))
+    scratch = [pltpu.VMEM(fields.shape, jnp.float32)] * 2
+    results = (f32(3, LINES, ROWS, LANES), f32(ROWS, LINES * NZ))
+    params = pltpu.CompilerParams(vmem_limit_bytes=24 * 1024 * 1024)
+    first, last = (*prepared, start), (tile, y_a, y_b)
+
+    def in_vmem(shapes):
+        return jax.tree.map(lambda _: vmem, shapes)
+
+    if tx_count == 2:
+        made = pl.pallas_call(
+            functools.partial(window_part, True, False, tx_count, ty_count),
+            out_shape=state,
+            in_specs=[vmem] * 8,
+            out_specs=in_vmem(state),
+            scratch_shapes=scratch,
+            compiler_params=params,
+            name="early",
+        )(*first, *last)
+        operands = (*first, *arrived)
+        electric, partial, *_ = pl.pallas_call(
+            functools.partial(window_part, False, True, tx_count, ty_count),
+            out_shape=(*results, state),
+            in_specs=[vmem] * len(operands) + [in_vmem(state)],
+            out_specs=(vmem, vmem, in_vmem(state)),
+            scratch_shapes=scratch,
+            input_output_aliases={len(operands) + i: 2 + i for i in range(len(jax.tree.leaves(state)))},
+            compiler_params=params,
+            name="late",
+        )(*operands, made)
+    else:
+        electric, partial = pl.pallas_call(
+            functools.partial(window_part, True, True, tx_count, ty_count),
+            out_shape=results,
+            in_specs=[vmem] * (8 + len(arrived)),
+            out_specs=(vmem, vmem),
+            scratch_shapes=[jax.tree.map(lambda v: pltpu.VMEM(v.shape, jnp.float32), state), *scratch],
+            compiler_params=params,
+            name="window",
+        )(*first, *last, *arrived)
     final = pl.pallas_call(
         emit_kernel,
         out_shape=f32(1, 2, 3, ROWS, LINES * NZ),

time: 24.2 us -> 23.3 us (0.963)
  waiting for transfers between devices: 9.57 us -> 7.71 us
  Pallas kernels: 5.45 us -> 6.51 us
    ppermute x5, waiting for transfers between devices: 7.48 us -> 6.21 us  [swap(): return lax.ppermute(value, ('wave', 'tx', 'ty'), pairs)]
    pallas_call x1 -> x2, Pallas kernels: 2.02 us -> 3.14 us  [the longest x1 1.9 us: on_device(): pl.pallas_call(functools.partial(window_part, False, True, tx_count, ty_c...]
    ppermute x3, waiting for transfers between devices: 2.09 us -> 1.5 us  [on_device(): lax.ppermute(partial, 'wave', [(i, i ^ k) for i in range(4)])]
  transfers between devices with their start and end apart: 8 -> 8, of which waited for: 4 -> 5; matrix products, arithmetic and copies ran while one was open for 0% -> 0% of each run, Pallas kernels for 7% -> 13%
where the time goes in v7:
time: 23.3 us; the launch traced here: 23.1 us
  waiting for transfers between devices  7.71 us (33%)
  starting transfers between devices  7.6 us (33%)
  Pallas kernels  6.51 us (28%)
  between operations  0.68 us (3%)
  other arithmetic  0.63 us (3%)
    ppermute x5, waiting for transfers between devices, swap(): return lax.ppermute(value, ('wave', 'tx', 'ty'), pairs)  6.21 us
    ppermute x5, starting transfers between devices, swap(): return lax.ppermute(value, ('wave', 'tx', 'ty'), pairs)  4.08 us
    ppermute x3, starting transfers between devices, on_device(): lax.ppermute(partial, 'wave', [(i, i ^ k) for i in range(4)])  3.52 us
    pallas_call x1, Pallas kernels, on_device(): pl.pallas_call(functools.partial(window_part, False, True, tx_count, ty_c...  1.9 us
    pallas_call x1, Pallas kernels, on_device(): pl.pallas_call(pack_kernel, out_shape=(f32(FIELDS, LINES, ROWS, LANES), f...  1.58 us
    ppermute x3, waiting for transfers between devices, on_device(): lax.ppermute(partial, 'wave', [(i, i ^ k) for i in range(4)])  1.5 us
    pallas_call x1, Pallas kernels, on_device(): pl.pallas_call(functools.partial(window_part, True, False, tx_count, ty_c...  1.23 us
    pallas_call x1, Pallas kernels, on_device(): pl.pallas_call(functools.partial(prepare_kernel, tx_count, ty_count), out...  0.94 us
  transfers between devices with their start and end apart: 8, of which 5 were waited for; matrix products, arithmetic and copies ran while one was open for 0% of the time, Pallas kernels for 13%

profile of v7, /device:TPU:17, one launch (start us, length us, event | category | flops | bytes accessed | tf_op | source)
XLA Modules:
  0.0 23.1 jit_solution(6501340420231538727)
XLA Ops:
  0.6 1.6 %pack.1 = (f32[13,8,16,128]{3,2,1,0:T(8,128)S(1)}, f32[3,8,16,128]{3,2,1,0:T(8,128)S(1)}, f32[46,16,128]{2,1,0:T(8,128)S(1)}, f32[46,16,128]{2,1,0:T(8,128)S(1)}) custom-call(f32[3,4]{1,0:T(4,128)} %table_hbm.3, s32[6]{0:T(128)} %box_hbm.3, f32[1,2,12,16,512]{4,3,2,1,0:T(8,128)} %fields_hbm.1, s32[16,512]{1,0:T(8,128)} %material_hbm.1, f32[16,512]{1,0:T(8,128)} %density_hbm.1), custom_call_target="tpu_custom_call" | custom-call | tf_op jit(solution)/shard_map/pack/pallas_call | solution.py:706
  2.2 1.4 %collective-permute-start.3 = (f32[46,16,128]{2,1,0:T(8,128)S(1)}, f32[46,16,128]{2,1,0:T(8,128)S(1)}, u32[]{:S(2)}, u32[]{:S(2)}) collective-permute-start(f32[46,16,128]{2,1,0:T(8,128)S(1)} %get-tuple-element.40), channel_id=1, source_target_pairs={{0,1},{1,0},{2,3},{3,2},{4,5},{5,4},{6,7},{7,6},{8,9},{9,8},{10,11... | collective-permute-start | bytes 1130504 | tf_op jit(solution)/shard_map/ppermute | solution.py:695
  3.6 0.0 collective-permute-start.4
  3.6 0.0 copy-start
  3.6 0.1 edges.1
  3.7 1.3 %collective-permute-start = (f32[376,128]{1,0:T(8,128)S(1)}, f32[376,128]{1,0:T(8,128)S(1)}, u32[]{:S(2)}, u32[]{:S(2)}) collective-permute-start(f32[376,128]{1,0:T(8,128)S(1)} %get-tuple-element.37), channel_id=1, source_target_pairs={{0,4},{1,5},{2,6},{3,7},{4,0},{5,1},{6,2},{7,3},{8,12},{9,13},{10,... | collective-permute-start | bytes 577544 | tf_op jit(solution)/shard_map/ppermute | solution.py:695
  4.9 1.4 %collective-permute-start.2 = (f32[88,128]{1,0:T(8,128)S(1)}, f32[88,128]{1,0:T(8,128)S(1)}, u32[]{:S(2)}, u32[]{:S(2)}) collective-permute-start(f32[88,128]{1,0:T(8,128)S(1)} %get-tuple-element.39), channel_id=1, source_target_pairs={{0,8},{1,4},{2,5},{3,6},{4,1},{5,2},{6,3},{7,15},{8,0},{9,12},{10,... | collective-permute-start | bytes 135176 | tf_op jit(solution)/shard_map/ppermute | solution.py:695
  6.4 0.0 collective-permute-start.1
  6.4 0.0 copy-done
  6.4 0.9 %prepare.1 = (f32[5,3,24,128]{3,2,1,0:T(8,128)S(1)}, f32[24,128]{1,0:T(8,128)S(1)}, f32[18,24,128]{2,1,0:T(8,128)S(1)}, f32[16,128]{1,0:T(8,128)S(1)}) custom-call(f32[2,5]{1,0:T(2,128)} %bitcast.5, f32[3,4]{1,0:T(4,128)} %table_hbm.3, s32[2]{0:T(128)} %plane_hbm.1, s32[6]{0:T(128)} %box_hbm.3, f32[3,2,2048]{2,1,0:T(2,128)S(1)} %bitcast.4), custom_call_target="tpu_custom_call" | custom-call | tf_op jit(solution)/shard_map/prepare/pallas_call | solution.py:744
  7.3 4.6 %collective-permute-done.3.refs_6_ = f32[46,16,128]{2,1,0:T(8,128)S(1)} collective-permute-done((f32[46,16,128]{2,1,0:T(8,128)S(1)}, f32[46,16,128]{2,1,0:T(8,128)S(1)}, u32[]{:S(2)}, u32[]{:S(2)}) %collective-permute-start.3) | collective-permute-done | bytes 376864 | tf_op jit(solution)/shard_map/ppermute | solution.py:695
  11.9 1.0 %collective-permute-done.4.refs_7_ = f32[46,16,128]{2,1,0:T(8,128)S(1)} collective-permute-done((f32[46,16,128]{2,1,0:T(8,128)S(1)}, f32[46,16,128]{2,1,0:T(8,128)S(1)}, u32[]{:S(2)}, u32[]{:S(2)}) %collective-permute-start.4) | collective-permute-done | bytes 376864 | tf_op jit(solution)/shard_map/ppermute | solution.py:695
  12.9 1.2 %early.1 = (f32[3,18,24,128]{3,2,1,0:T(8,128)S(1)}, f32[3,18,24,128]{3,2,1,0:T(8,128)S(1)}, f32[3,18,24,128]{3,2,1,0:T(8,128)S(1)}, f32[3,18,24,128]{3,2,1,0:T(8...) custom-call(f32[5,3,24,128]{3,2,1,0:T(8,128)S(1)} %get-tuple-element, ...), custom_call_target="tpu_custom_call" | custom-call | tf_op jit(solution)/shard_map/early/pallas_call | solution.py:773
  14.1 0.0 collective-permute-done.1.refs_6_
  14.1 0.6 %collective-permute-done.2.refs_7_ = f32[88,128]{1,0:T(8,128)S(1)} collective-permute-done((f32[88,128]{1,0:T(8,128)S(1)}, f32[88,128]{1,0:T(8,128)S(1)}, u32[]{:S(2)}, u32[]{:S(2)}) %collective-permute-start.2) | collective-permute-done | bytes 45088 | tf_op jit(solution)/shard_map/ppermute | solution.py:695
  14.8 0.0 collective-permute-done.refs_5_
  14.8 1.9 %late.1 = (f32[3,8,16,128]{3,2,1,0:T(8,128)S(1)}, f32[16,512]{1,0:T(8,128)S(1)}, f32[3,18,24,128]{3,2,1,0:T(8,128)S(1)}, f32[3,18,24,128]{3,2,1,0:T(8,128)S(1)},...) custom-call(f32[5,3,24,128]{3,2,1,0:T(8,128)S(1)} %get-tuple-element, ...), custom_call_target="tpu_custom_call", output_to_operand_aliasing={{2}: (8, {}), {3}: (9, {}), {4}: (10, {}), {5}: (11, {}), {... | custom-call | tf_op jit(solution)/shard_map/late/pallas_call | solution.py:783
  16.7 3.0 %collective-permute-start.7 = (f32[16,512]{1,0:T(8,128)S(1)}, f32[16,512]{1,0:T(8,128)S(1)}, u32[]{:S(2)}, u32[]{:S(2)}) collective-permute-start(f32[16,512]{1,0:T(8,128)S(1)} %get-tuple-element.58), channel_id=1, source_target_pairs={{0,24},{8,16},{16,8},{24,0},{1,25},{9,17},{17,9},{25,1},{2,26},{10... | collective-permute-start | bytes 98312 | tf_op jit(solution)/shard_map/ppermute | solution.py:814
  19.7 0.2 collective-permute-start.6
  20.0 0.2 %collective-permute-start.5 = (f32[16,512]{1,0:T(8,128)S(1)}, f32[16,512]{1,0:T(8,128)S(1)}, u32[]{:S(2)}, u32[]{:S(2)}) collective-permute-start(f32[16,512]{1,0:T(8,128)S(1)} %get-tuple-element.58), channel_id=1, source_target_pairs={{0,8},{8,0},{16,24},{24,16},{1,9},{9,1},{17,25},{25,17},{2,10},{10... | collective-permute-start | bytes 98312 | tf_op jit(solution)/shard_map/ppermute | solution.py:814
  20.2 0.8 %emit.1 = f32[1,2,3,16,512]{4,3,2,1,0:T(8,128)} custom-call(f32[3,8,16,128]{3,2,1,0:T(8,128)S(1)} %get-tuple-element.59.electric), custom_call_target="tpu_custom_call" | custom-call | tf_op jit(solution)/shard_map/emit/pallas_call | solution.py:803
  21.0 0.8 %collective-permute-done.7 = f32[16,512]{1,0:T(8,128)S(1)} collective-permute-done((f32[16,512]{1,0:T(8,128)S(1)}, f32[16,512]{1,0:T(8,128)S(1)}, u32[]{:S(2)}, u32[]{:S(2)}) %collective-permute-start.7) | collective-permute-done | bytes 32800 | tf_op jit(solution)/shard_map/ppermute | solution.py:814
  21.8 0.7 %collective-permute-done.6 = f32[16,512]{1,0:T(8,128)S(1)} collective-permute-done((f32[16,512]{1,0:T(8,128)S(1)}, f32[16,512]{1,0:T(8,128)S(1)}, u32[]{:S(2)}, u32[]{:S(2)}) %collective-permute-start.6) | collective-permute-done | bytes 32800 | tf_op jit(solution)/shard_map/ppermute | solution.py:814
  22.5 0.0 collective-permute-done.5
  22.5 0.6 %add_add_fusion = f32[16,512]{1,0:T(8,128)} fusion(f32[16,512]{1,0:T(8,128)S(1)} %collective-permute-done.6, f32[16,512]{1,0:T(8,128)S(1)} %collective-permute-done.7, f32[16,512]{1,0:T(8,128)S(1)} %get-tuple-element.58, f32[16,512]{1,0:T(8,128)S(1)} %collective-permute-done.5), kind=kLoop, calls=%fused_computation | loop fusion | flops 24576 | bytes 163840 | tf_op jit(solution)/shard_map/add | solution.py:816
Async XLA Ops:
  2.2 9.7 %collective-permute-start.3 = (f32[46,16,128]{2,1,0:T(8,128)S(1)}, f32[46,16,128]{2,1,0:T(8,128)S(1)}, u32[]{:S(2)}, u32[]{:S(2)}) collective-permute-start(f32[46,16,128]{2,1,0:T(8,128)S(1)} %get-tuple-element.40), channel_id=1, source_target_pairs={{0,1},{1,0},{2,3},{3,2},{4,5},{5,4},{6,7},{7,6},{8,9},{9,8},{10,11... | collective-permute-start | bytes 1130504 | tf_op jit(solution)/shard_map/ppermute | solution.py:695
  3.6 9.3 %collective-permute-start.4 = (f32[46,16,128]{2,1,0:T(8,128)S(1)}, f32[46,16,128]{2,1,0:T(8,128)S(1)}, u32[]{:S(2)}, u32[]{:S(2)}) collective-permute-start(f32[46,16,128]{2,1,0:T(8,128)S(1)} %get-tuple-element.41), channel_id=1, source_target_pairs={{0,8},{1,2},{2,1},{3,11},{4,12},{5,6},{6,5},{7,15},{8,0},{9,10},{1... | collective-permute-start | bytes 1130504 | tf_op jit(solution)/shard_map/ppermute | solution.py:695
  3.6 2.8 %copy-start = (f32[1,2,3,2048]{3,1,2,0:T(2,128)S(1)}, f32[1,2,3,2048]{3,1,2,0:T(2,128)}, u32[]{:S(2)}) copy-start(f32[1,2,3,2048]{3,1,2,0:T(2,128)} %param.9) | copy-start | bytes 147460
  3.7 11.1 %collective-permute-start = (f32[376,128]{1,0:T(8,128)S(1)}, f32[376,128]{1,0:T(8,128)S(1)}, u32[]{:S(2)}, u32[]{:S(2)}) collective-permute-start(f32[376,128]{1,0:T(8,128)S(1)} %get-tuple-element.37), channel_id=1, source_target_pairs={{0,4},{1,5},{2,6},{3,7},{4,0},{5,1},{6,2},{7,3},{8,12},{9,13},{10,... | collective-permute-start | bytes 577544 | tf_op jit(solution)/shard_map/ppermute | solution.py:695
  4.9 9.8 %collective-permute-start.2 = (f32[88,128]{1,0:T(8,128)S(1)}, f32[88,128]{1,0:T(8,128)S(1)}, u32[]{:S(2)}, u32[]{:S(2)}) collective-permute-start(f32[88,128]{1,0:T(8,128)S(1)} %get-tuple-element.39), channel_id=1, source_target_pairs={{0,8},{1,4},{2,5},{3,6},{4,1},{5,2},{6,3},{7,15},{8,0},{9,12},{10,... | collective-permute-start | bytes 135176 | tf_op jit(solution)/shard_map/ppermute | solution.py:695
  6.4 7.8 %collective-permute-start.1 = (f32[72,128]{1,0:T(8,128)S(1)}, f32[72,128]{1,0:T(8,128)S(1)}, u32[]{:S(2)}, u32[]{:S(2)}) collective-permute-start(f32[72,128]{1,0:T(8,128)S(1)} %get-tuple-element.38), channel_id=1, source_target_pairs={{0,5},{1,6},{2,7},{3,11},{4,12},{5,0},{6,1},{7,2},{8,13},{9,14},{1... | collective-permute-start | bytes 110600 | tf_op jit(solution)/shard_map/ppermute | solution.py:695
  16.7 5.1 %collective-permute-start.7 = (f32[16,512]{1,0:T(8,128)S(1)}, f32[16,512]{1,0:T(8,128)S(1)}, u32[]{:S(2)}, u32[]{:S(2)}) collective-permute-start(f32[16,512]{1,0:T(8,128)S(1)} %get-tuple-element.58), channel_id=1, source_target_pairs={{0,24},{8,16},{16,8},{24,0},{1,25},{9,17},{17,9},{25,1},{2,26},{10... | collective-permute-start | bytes 98312 | tf_op jit(solution)/shard_map/ppermute | solution.py:814
  19.7 2.8 %collective-permute-start.6 = (f32[16,512]{1,0:T(8,128)S(1)}, f32[16,512]{1,0:T(8,128)S(1)}, u32[]{:S(2)}, u32[]{:S(2)}) collective-permute-start(f32[16,512]{1,0:T(8,128)S(1)} %get-tuple-element.58), channel_id=1, source_target_pairs={{0,16},{8,24},{16,0},{24,8},{1,17},{9,25},{17,1},{25,9},{2,18},{10... | collective-permute-start | bytes 98312 | tf_op jit(solution)/shard_map/ppermute | solution.py:814
  20.0 2.5 %collective-permute-start.5 = (f32[16,512]{1,0:T(8,128)S(1)}, f32[16,512]{1,0:T(8,128)S(1)}, u32[]{:S(2)}, u32[]{:S(2)}) collective-permute-start(f32[16,512]{1,0:T(8,128)S(1)} %get-tuple-element.58), channel_id=1, source_target_pairs={{0,8},{8,0},{16,24},{24,16},{1,9},{9,1},{17,25},{25,17},{2,10},{10... | collective-permute-start | bytes 98312 | tf_op jit(solution)/shard_map/ppermute | solution.py:814

commit v8 on v7

--- a/solution.py
+++ b/solution.py
@@ -514,128 +514,132 @@
     first_sub, last_sub = sub == 0, sub == 7
     sent = sub + tx * (7 - 2 * sub) < STEPS
     own = range(tile_row // 8, (tile_row + ROWS) // 8)
+    def make_steps(made):
+        def rows_of(b):
+            return slice(8 * b, 8 * b + 8)
+
+        def blocks(ref, c, line):
+            return {b: ref[c, line, rows_of(b), :] for b in made}
+
+        def turned_blocks(ref, c, line, v, shift, step):
+            turned = {}
+            for b in sorted({*made, *((b + step) % count for b in made)}):
+                if b in made:
+                    turned[b] = pltpu.roll(v[b], shift, 0)
+                elif late or b in own:
+                    turned[b] = pltpu.roll(ref[c, line, rows_of(b), :], shift, 0)
+                else:
+                    turned[b] = jnp.zeros(block, jnp.float32)
+            return turned
+
+        def ahead_row(ref, c, line, v):
+            turned = turned_blocks(ref, c, line, v, 7, 1)
+            return {b: jnp.where(last_sub, turned[(b + 1) % count], turned[b]) for b in made}
+
+        def behind_row(ref, c, line, v):
+            turned = turned_blocks(ref, c, line, v, 1, -1)
+            return {b: jnp.where(first_sub, turned[(b - 1) % count], turned[b]) for b in made}
+
+        def ahead_depth(v):
+            return jnp.where(last_z, 0.0, pltpu.roll(v, LANES - 1, 1))
+
+        def behind_depth(v):
+            return jnp.where(first_z, 0.0, pltpu.roll(v, 1, 1))
+
+        def settle(ref, c, line, b, value):
+            if not wide and b not in own:
+                value = jnp.where(sent, value, 0.0)
+            ref[c, line, rows_of(b), :] = value
+
+        def magnetic_line(n, line):
+            ex, ey, ez = [blocks(E[n], c, line) for c in range(3)]
+            ex_next, ez_next = blocks(E[n], 0, line + 1), blocks(E[n], 2, line + 1)
+            hx, hy, hz = [blocks(H[n], c, line) for c in range(3)]
+            ey_ahead, ez_ahead = ahead_row(E[n], 1, line, ey), ahead_row(E[n], 2, line, ez)
+            for b in made:
+                curls = (
+                    (ez_next[b] - ez[b]) - (ahead_depth(ey[b]) - ey[b]),
+                    (ahead_depth(ex[b]) - ex[b]) - (ez_ahead[b] - ez[b]),
+                    (ey_ahead[b] - ey[b]) - (ex_next[b] - ex[b]),
+                )
+                if line < STEPS:
+                    curls = [curl * line_inside(line) for curl in curls]
+                if wide:
+                    curls = [curl * row_mask[8 * b : 8 * b + 8] for curl in curls]
+                for c, h in enumerate((hx, hy, hz)):
+                    settle(H[n + 1], c, line, b, h[b] - curls[c])
+
+        def electric_line(n, line):
+            field = H[n + 1]
+            hx, hy, hz = [blocks(field, c, line) for c in range(3)]
+            hx_last, hz_last = blocks(field, 0, line - 1), blocks(field, 2, line - 1)
+            hy_behind, hz_behind = behind_row(field, 1, line, hy), behind_row(field, 2, line, hz)
+            for b in [b for b in made if n + 1 < STEPS or b in own]:
+                rows = rows_of(b)
+                curls = (
+                    (hz[b] - hz_last[b]) - (hy[b] - behind_depth(hy[b])),
+                    (hx[b] - behind_depth(hx[b])) - (hz[b] - hz_behind[b]),
+                    (hy[b] - hy_behind[b]) - (hx[b] - hx_last[b]),
+                )
+                reach = coef[0, line, rows, :]
+                for c in range(3):
+                    e = E[n][c, line, rows, :]
+                    curl = curls[c]
+                    if n > 0:
+                        held = 0 if n == 1 else 1
+                        p, j = Pol[held][c, line, rows, :], J[held][c, line, rows, :]
+                        if n == 1:
+                            j = j + coef[3, line, rows, :] * e
+                        else:
+                            j = coef[1, line, rows, :] * j + coef[3, line, rows, :] * e - coef[2, line, rows, :] * p
+                        if n < STEPS - 1:
+                            J[1][c, line, rows, :] = j
+                            Pol[1][c, line, rows, :] = p + j
+                        curl = curl - j
+                    drawn = source_rows[rows, :] * sources[n, c, line : line + 1, :]
+                    settle(E[n + 1], c, line, b, e + reach * (curl - drawn))
+
+        for n in range(STEPS):
+            for line in range(n, EXT_LINES - 1 - n) if n > 0 else ():
+                magnetic_line(n, line)
+            for line in range(n + 1, EXT_LINES - 1 - n):
+                electric_line(n, line)
+
+    def make_gradient():
+        low_tile = low_lanes((ROWS, LANES))
+
+        def turned(line):
+            return [[half_turn(E[n][c, line, middle, :]) for n in (5, 4, 3)] for c in range(3)]
+
+        totals, following = [], turned(STEPS)
+        for own_line in range(LINES):
+            line, (x, y, z) = STEPS + own_line, following
+            if own_line + 1 < LINES:
+                following = turned(line + 1)
+            terms = []
+            for c, (five, four, three) in enumerate((x, y, z)):
+                one, two = E[1][c, line, middle, :], E[2][c, line, middle, :]
+                zero_low = jnp.where(low_tile, start[c, own_line], 0.0)
+                three_low = jnp.where(low_tile, E[3][c, line, middle, :], 0.0)
+                terms.append(five * (one - zero_low) + four * (two - one) + three * (three_low - two))
+                electric_out[c, own_line] = E[STEPS][c, line, middle, :]
+            totals.append((terms[0] + terms[1] + terms[2]) * design[line, middle, :])
+        folded = [total + half_turn(total) for total in totals]
+        for k in range(CHUNKS):
+            gradient_out[:, k * LANES : (k + 1) * LANES] = jnp.where(low_tile, folded[2 * k], folded[2 * k + 1])
+
     if early:
-        made = {b: ((b - 1) % count, (b + 1) % count) for b in (range(count) if late else own)}
-        own_made = list(own)
+        make_steps(list(range(count) if late else own))
     else:
-        beside = 1 - tx
-        made = {2: (1, 0), "beside": (lax.rem(beside + 2, 3), beside + 1)}
-        own_made = ["beside"]
-
-    def rows_of(b):
-        if isinstance(b, int):
-            return slice(8 * b, 8 * b + 8)
-        return pl.ds(pl.multiple_of(8 * (beside if isinstance(b, str) else b), 8), 8)
-
-    def block_of(ref, c, line, b):
-        if isinstance(b, int) and not late and b not in own:
-            return jnp.zeros(block, jnp.float32)
-        return ref[c, line, rows_of(b), :]
-
-    def blocks(ref, c, line):
-        return {b: block_of(ref, c, line, b) for b in made}
-
-    def ahead_row(ref, c, line, v):
-        return {
-            b: jnp.where(last_sub, pltpu.roll(block_of(ref, c, line, made[b][1]), 7, 0), pltpu.roll(v[b], 7, 0))
-            for b in made
-        }
-
-    def behind_row(ref, c, line, v):
-        return {
-            b: jnp.where(first_sub, pltpu.roll(block_of(ref, c, line, made[b][0]), 1, 0), pltpu.roll(v[b], 1, 0))
-            for b in made
-        }
-
-    def ahead_depth(v):
-        return jnp.where(last_z, 0.0, pltpu.roll(v, LANES - 1, 1))
-
-    def behind_depth(v):
-        return jnp.where(first_z, 0.0, pltpu.roll(v, 1, 1))
-
-    def settle(ref, c, line, b, value):
-        if not wide and isinstance(b, int) and b not in own:
-            value = jnp.where(sent, value, 0.0)
-        ref[c, line, rows_of(b), :] = value
-
-    def magnetic_line(n, line):
-        ex, ey, ez = [blocks(E[n], c, line) for c in range(3)]
-        ex_next, ez_next = blocks(E[n], 0, line + 1), blocks(E[n], 2, line + 1)
-        hx, hy, hz = [blocks(H[n], c, line) for c in range(3)]
-        ey_ahead, ez_ahead = ahead_row(E[n], 1, line, ey), ahead_row(E[n], 2, line, ez)
-        for b in made:
-            curls = (
-                (ez_next[b] - ez[b]) - (ahead_depth(ey[b]) - ey[b]),
-                (ahead_depth(ex[b]) - ex[b]) - (ez_ahead[b] - ez[b]),
-                (ey_ahead[b] - ey[b]) - (ex_next[b] - ex[b]),
-            )
-            if line < STEPS:
-                curls = [curl * line_inside(line) for curl in curls]
-            if wide:
-                curls = [curl * row_mask[8 * b : 8 * b + 8] for curl in curls]
-            for c, h in enumerate((hx, hy, hz)):
-                settle(H[n + 1], c, line, b, h[b] - curls[c])
-
-    def electric_line(n, line):
-        field = H[n + 1]
-        hx, hy, hz = [blocks(field, c, line) for c in range(3)]
-        hx_last, hz_last = blocks(field, 0, line - 1), blocks(field, 2, line - 1)
-        hy_behind, hz_behind = behind_row(field, 1, line, hy), behind_row(field, 2, line, hz)
-        for b in made if n + 1 < STEPS else own_made:
-            rows = rows_of(b)
-            curls = (
-                (hz[b] - hz_last[b]) - (hy[b] - behind_depth(hy[b])),
-                (hx[b] - behind_depth(hx[b])) - (hz[b] - hz_behind[b]),
-                (hy[b] - hy_behind[b]) - (hx[b] - hx_last[b]),
-            )
-            reach = coef[0, line, rows, :]
-            for c in range(3):
-                e = E[n][c, line, rows, :]
-                curl = curls[c]
-                if n > 0:
-                    held = 0 if n == 1 else 1
-                    p, j = Pol[held][c, line, rows, :], J[held][c, line, rows, :]
-                    if n == 1:
-                        j = j + coef[3, line, rows, :] * e
-                    else:
-                        j = coef[1, line, rows, :] * j + coef[3, line, rows, :] * e - coef[2, line, rows, :] * p
-                    if n < STEPS - 1:
-                        J[1][c, line, rows, :] = j
-                        Pol[1][c, line, rows, :] = p + j
-                    curl = curl - j
-                drawn = source_rows[rows, :] * sources[n, c, line : line + 1, :]
-                settle(E[n + 1], c, line, b, e + reach * (curl - drawn))
-
-    for n in range(STEPS):
-        for line in range(n, EXT_LINES - 1 - n) if n > 0 else ():
-            magnetic_line(n, line)
-        for line in range(n + 1, EXT_LINES - 1 - n):
-            electric_line(n, line)
-
-    if not late:
+        for side in range(2):
+
+            @pl.when(tx == side)
+            def _(side=side):
+                make_steps([2, 1 - side])
+                make_gradient()
         return
-
-    low_tile = low_lanes((ROWS, LANES))
-
-    def turned(line):
-        return [[half_turn(E[n][c, line, middle, :]) for n in (5, 4, 3)] for c in range(3)]
-
-    totals, following = [], turned(STEPS)
-    for own_line in range(LINES):
-        line, (x, y, z) = STEPS + own_line, following
-        if own_line + 1 < LINES:
-            following = turned(line + 1)
-        terms = []
-        for c, (five, four, three) in enumerate((x, y, z)):
-            one, two = E[1][c, line, middle, :], E[2][c, line, middle, :]
-            zero_low = jnp.where(low_tile, start[c, own_line], 0.0)
-            three_low = jnp.where(low_tile, E[3][c, line, middle, :], 0.0)
-            terms.append(five * (one - zero_low) + four * (two - one) + three * (three_low - two))
-            electric_out[c, own_line] = E[STEPS][c, line, middle, :]
-        totals.append((terms[0] + terms[1] + terms[2]) * design[line, middle, :])
-    folded = [total + half_turn(total) for total in totals]
-    for k in range(CHUNKS):
-        gradient_out[:, k * LANES : (k + 1) * LANES] = jnp.where(low_tile, folded[2 * k], folded[2 * k + 1])
+    if late:
+        make_gradient()
 
 
 def emit_kernel(electric, out):

time: 23.3 us -> 22.9 us (0.983)
  Pallas kernels: 6.51 us -> 6.1 us
    pallas_call x1, Pallas kernels: 1.9 us -> 1.5 us  [on_device(): pl.pallas_call(functools.partial(window_part, False, True, tx_count, ty_c...]
where the time goes in v8:
time: 22.9 us; the launch traced here: 22.7 us
  waiting for transfers between devices  7.72 us (34%)
  starting transfers between devices  7.6 us (33%)
  Pallas kernels  6.1 us (27%)
  between operations  0.68 us (3%)
  other arithmetic  0.63 us (3%)
    ppermute x5, waiting for transfers between devices, swap(): return lax.ppermute(value, ('wave', 'tx', 'ty'), pairs)  6.22 us
    ppermute x5, starting transfers between devices, swap(): return lax.ppermute(value, ('wave', 'tx', 'ty'), pairs)  4.08 us
    ppermute x3, starting transfers between devices, on_device(): lax.ppermute(partial, 'wave', [(i, i ^ k) for i in range(4)])  3.52 us
    pallas_call x1, Pallas kernels, on_device(): pl.pallas_call(pack_kernel, out_shape=(f32(FIELDS, LINES, ROWS, LANES), f...  1.58 us
    pallas_call x1, Pallas kernels, on_device(): pl.pallas_call(functools.partial(window_part, False, True, tx_count, ty_c...  1.5 us
    ppermute x3, waiting for transfers between devices, on_device(): lax.ppermute(partial, 'wave', [(i, i ^ k) for i in range(4)])  1.5 us
    pallas_call x1, Pallas kernels, on_device(): pl.pallas_call(functools.partial(window_part, True, False, tx_count, ty_c...  1.23 us
    pallas_call x1, Pallas kernels, on_device(): pl.pallas_call(functools.partial(prepare_kernel, tx_count, ty_count), out...  0.94 us
  transfers between devices with their start and end apart: 8, of which 5 were waited for; matrix products, arithmetic and copies ran while one was open for 0% of the time, Pallas kernels for 13%

profile of v8, /device:TPU:17, one launch (start us, length us, event | category | flops | bytes accessed | tf_op | source)
XLA Modules:
  0.0 22.7 jit_solution(11615503631524297208)
XLA Ops:
  0.6 1.6 %pack.1 = (f32[13,8,16,128]{3,2,1,0:T(8,128)S(1)}, f32[3,8,16,128]{3,2,1,0:T(8,128)S(1)}, f32[46,16,128]{2,1,0:T(8,128)S(1)}, f32[46,16,128]{2,1,0:T(8,128)S(1)}) custom-call(f32[3,4]{1,0:T(4,128)} %table_hbm.3, s32[6]{0:T(128)} %box_hbm.3, f32[1,2,12,16,512]{4,3,2,1,0:T(8,128)} %fields_hbm.1, s32[16,512]{1,0:T(8,128)} %material_hbm.1, f32[16,512]{1,0:T(8,128)} %density_hbm.1), custom_call_target="tpu_custom_call" | custom-call | tf_op jit(solution)/shard_map/pack/pallas_call | solution.py:710
  2.2 1.4 %collective-permute-start.3 = (f32[46,16,128]{2,1,0:T(8,128)S(1)}, f32[46,16,128]{2,1,0:T(8,128)S(1)}, u32[]{:S(2)}, u32[]{:S(2)}) collective-permute-start(f32[46,16,128]{2,1,0:T(8,128)S(1)} %get-tuple-element.40), channel_id=1, source_target_pairs={{0,1},{1,0},{2,3},{3,2},{4,5},{5,4},{6,7},{7,6},{8,9},{9,8},{10,11... | collective-permute-start | bytes 1130504 | tf_op jit(solution)/shard_map/ppermute | solution.py:699
  3.6 0.0 collective-permute-start.4
  3.6 0.0 copy-start
  3.6 0.1 edges.1
  3.7 1.3 %collective-permute-start = (f32[376,128]{1,0:T(8,128)S(1)}, f32[376,128]{1,0:T(8,128)S(1)}, u32[]{:S(2)}, u32[]{:S(2)}) collective-permute-start(f32[376,128]{1,0:T(8,128)S(1)} %get-tuple-element.37), channel_id=1, source_target_pairs={{0,4},{1,5},{2,6},{3,7},{4,0},{5,1},{6,2},{7,3},{8,12},{9,13},{10,... | collective-permute-start | bytes 577544 | tf_op jit(solution)/shard_map/ppermute | solution.py:699
  4.9 1.4 %collective-permute-start.2 = (f32[88,128]{1,0:T(8,128)S(1)}, f32[88,128]{1,0:T(8,128)S(1)}, u32[]{:S(2)}, u32[]{:S(2)}) collective-permute-start(f32[88,128]{1,0:T(8,128)S(1)} %get-tuple-element.39), channel_id=1, source_target_pairs={{0,8},{1,4},{2,5},{3,6},{4,1},{5,2},{6,3},{7,15},{8,0},{9,12},{10,... | collective-permute-start | bytes 135176 | tf_op jit(solution)/shard_map/ppermute | solution.py:699
  6.4 0.0 collective-permute-start.1
  6.4 0.0 copy-done
  6.4 0.9 %prepare.1 = (f32[5,3,24,128]{3,2,1,0:T(8,128)S(1)}, f32[24,128]{1,0:T(8,128)S(1)}, f32[18,24,128]{2,1,0:T(8,128)S(1)}, f32[16,128]{1,0:T(8,128)S(1)}) custom-call(f32[2,5]{1,0:T(2,128)} %bitcast.5, f32[3,4]{1,0:T(4,128)} %table_hbm.3, s32[2]{0:T(128)} %plane_hbm.1, s32[6]{0:T(128)} %box_hbm.3, f32[3,2,2048]{2,1,0:T(2,128)S(1)} %bitcast.4), custom_call_target="tpu_custom_call" | custom-call | tf_op jit(solution)/shard_map/prepare/pallas_call | solution.py:748
  7.3 4.6 %collective-permute-done.3.refs_6_ = f32[46,16,128]{2,1,0:T(8,128)S(1)} collective-permute-done((f32[46,16,128]{2,1,0:T(8,128)S(1)}, f32[46,16,128]{2,1,0:T(8,128)S(1)}, u32[]{:S(2)}, u32[]{:S(2)}) %collective-permute-start.3) | collective-permute-done | bytes 376864 | tf_op jit(solution)/shard_map/ppermute | solution.py:699
  11.9 1.0 %collective-permute-done.4.refs_7_ = f32[46,16,128]{2,1,0:T(8,128)S(1)} collective-permute-done((f32[46,16,128]{2,1,0:T(8,128)S(1)}, f32[46,16,128]{2,1,0:T(8,128)S(1)}, u32[]{:S(2)}, u32[]{:S(2)}) %collective-permute-start.4) | collective-permute-done | bytes 376864 | tf_op jit(solution)/shard_map/ppermute | solution.py:699
  12.9 1.2 %early.1 = (f32[3,18,24,128]{3,2,1,0:T(8,128)S(1)}, f32[3,18,24,128]{3,2,1,0:T(8,128)S(1)}, f32[3,18,24,128]{3,2,1,0:T(8,128)S(1)}, f32[3,18,24,128]{3,2,1,0:T(8...) custom-call(f32[5,3,24,128]{3,2,1,0:T(8,128)S(1)} %get-tuple-element, ...), custom_call_target="tpu_custom_call" | custom-call | tf_op jit(solution)/shard_map/early/pallas_call | solution.py:777
  14.1 0.0 collective-permute-done.1.refs_6_
  14.1 0.6 %collective-permute-done.2.refs_7_ = f32[88,128]{1,0:T(8,128)S(1)} collective-permute-done((f32[88,128]{1,0:T(8,128)S(1)}, f32[88,128]{1,0:T(8,128)S(1)}, u32[]{:S(2)}, u32[]{:S(2)}) %collective-permute-start.2) | collective-permute-done | bytes 45088 | tf_op jit(solution)/shard_map/ppermute | solution.py:699
  14.8 0.0 collective-permute-done.refs_5_
  14.8 1.5 %late.1 = (f32[3,8,16,128]{3,2,1,0:T(8,128)S(1)}, f32[16,512]{1,0:T(8,128)S(1)}, f32[3,18,24,128]{3,2,1,0:T(8,128)S(1)}, f32[3,18,24,128]{3,2,1,0:T(8,128)S(1)},...) custom-call(f32[5,3,24,128]{3,2,1,0:T(8,128)S(1)} %get-tuple-element, ...), custom_call_target="tpu_custom_call", output_to_operand_aliasing={{2}: (8, {}), {3}: (9, {}), {4}: (10, {}), {5}: (11, {}), {... | custom-call | tf_op jit(solution)/shard_map/late/pallas_call | solution.py:787
  16.3 3.0 %collective-permute-start.7 = (f32[16,512]{1,0:T(8,128)S(1)}, f32[16,512]{1,0:T(8,128)S(1)}, u32[]{:S(2)}, u32[]{:S(2)}) collective-permute-start(f32[16,512]{1,0:T(8,128)S(1)} %get-tuple-element.58), channel_id=1, source_target_pairs={{0,24},{8,16},{16,8},{24,0},{1,25},{9,17},{17,9},{25,1},{2,26},{10... | collective-permute-start | bytes 98312 | tf_op jit(solution)/shard_map/ppermute | solution.py:818
  19.3 0.2 collective-permute-start.6
  19.6 0.2 %collective-permute-start.5 = (f32[16,512]{1,0:T(8,128)S(1)}, f32[16,512]{1,0:T(8,128)S(1)}, u32[]{:S(2)}, u32[]{:S(2)}) collective-permute-start(f32[16,512]{1,0:T(8,128)S(1)} %get-tuple-element.58), channel_id=1, source_target_pairs={{0,8},{8,0},{16,24},{24,16},{1,9},{9,1},{17,25},{25,17},{2,10},{10... | collective-permute-start | bytes 98312 | tf_op jit(solution)/shard_map/ppermute | solution.py:818
  19.8 0.8 %emit.1 = f32[1,2,3,16,512]{4,3,2,1,0:T(8,128)} custom-call(f32[3,8,16,128]{3,2,1,0:T(8,128)S(1)} %get-tuple-element.59.electric), custom_call_target="tpu_custom_call" | custom-call | tf_op jit(solution)/shard_map/emit/pallas_call | solution.py:807
  20.6 0.8 %collective-permute-done.7 = f32[16,512]{1,0:T(8,128)S(1)} collective-permute-done((f32[16,512]{1,0:T(8,128)S(1)}, f32[16,512]{1,0:T(8,128)S(1)}, u32[]{:S(2)}, u32[]{:S(2)}) %collective-permute-start.7) | collective-permute-done | bytes 32800 | tf_op jit(solution)/shard_map/ppermute | solution.py:818
  21.4 0.7 %collective-permute-done.6 = f32[16,512]{1,0:T(8,128)S(1)} collective-permute-done((f32[16,512]{1,0:T(8,128)S(1)}, f32[16,512]{1,0:T(8,128)S(1)}, u32[]{:S(2)}, u32[]{:S(2)}) %collective-permute-start.6) | collective-permute-done | bytes 32800 | tf_op jit(solution)/shard_map/ppermute | solution.py:818
  22.1 0.0 collective-permute-done.5
  22.1 0.6 %add_add_fusion = f32[16,512]{1,0:T(8,128)} fusion(f32[16,512]{1,0:T(8,128)S(1)} %collective-permute-done.6, f32[16,512]{1,0:T(8,128)S(1)} %collective-permute-done.7, f32[16,512]{1,0:T(8,128)S(1)} %get-tuple-element.58, f32[16,512]{1,0:T(8,128)S(1)} %collective-permute-done.5), kind=kLoop, calls=%fused_computation | loop fusion | flops 24576 | bytes 163840 | tf_op jit(solution)/shard_map/add | solution.py:820
Async XLA Ops:
  2.2 9.7 %collective-permute-start.3 = (f32[46,16,128]{2,1,0:T(8,128)S(1)}, f32[46,16,128]{2,1,0:T(8,128)S(1)}, u32[]{:S(2)}, u32[]{:S(2)}) collective-permute-start(f32[46,16,128]{2,1,0:T(8,128)S(1)} %get-tuple-element.40), channel_id=1, source_target_pairs={{0,1},{1,0},{2,3},{3,2},{4,5},{5,4},{6,7},{7,6},{8,9},{9,8},{10,11... | collective-permute-start | bytes 1130504 | tf_op jit(solution)/shard_map/ppermute | solution.py:699
  3.6 9.3 %collective-permute-start.4 = (f32[46,16,128]{2,1,0:T(8,128)S(1)}, f32[46,16,128]{2,1,0:T(8,128)S(1)}, u32[]{:S(2)}, u32[]{:S(2)}) collective-permute-start(f32[46,16,128]{2,1,0:T(8,128)S(1)} %get-tuple-element.41), channel_id=1, source_target_pairs={{0,8},{1,2},{2,1},{3,11},{4,12},{5,6},{6,5},{7,15},{8,0},{9,10},{1... | collective-permute-start | bytes 1130504 | tf_op jit(solution)/shard_map/ppermute | solution.py:699
  3.6 2.8 %copy-start = (f32[1,2,3,2048]{3,1,2,0:T(2,128)S(1)}, f32[1,2,3,2048]{3,1,2,0:T(2,128)}, u32[]{:S(2)}) copy-start(f32[1,2,3,2048]{3,1,2,0:T(2,128)} %param.9) | copy-start | bytes 147460
  3.7 11.1 %collective-permute-start = (f32[376,128]{1,0:T(8,128)S(1)}, f32[376,128]{1,0:T(8,128)S(1)}, u32[]{:S(2)}, u32[]{:S(2)}) collective-permute-start(f32[376,128]{1,0:T(8,128)S(1)} %get-tuple-element.37), channel_id=1, source_target_pairs={{0,4},{1,5},{2,6},{3,7},{4,0},{5,1},{6,2},{7,3},{8,12},{9,13},{10,... | collective-permute-start | bytes 577544 | tf_op jit(solution)/shard_map/ppermute | solution.py:699
  4.9 9.8 %collective-permute-start.2 = (f32[88,128]{1,0:T(8,128)S(1)}, f32[88,128]{1,0:T(8,128)S(1)}, u32[]{:S(2)}, u32[]{:S(2)}) collective-permute-start(f32[88,128]{1,0:T(8,128)S(1)} %get-tuple-element.39), channel_id=1, source_target_pairs={{0,8},{1,4},{2,5},{3,6},{4,1},{5,2},{6,3},{7,15},{8,0},{9,12},{10,... | collective-permute-start | bytes 135176 | tf_op jit(solution)/shard_map/ppermute | solution.py:699
  6.4 7.8 %collective-permute-start.1 = (f32[72,128]{1,0:T(8,128)S(1)}, f32[72,128]{1,0:T(8,128)S(1)}, u32[]{:S(2)}, u32[]{:S(2)}) collective-permute-start(f32[72,128]{1,0:T(8,128)S(1)} %get-tuple-element.38), channel_id=1, source_target_pairs={{0,5},{1,6},{2,7},{3,11},{4,12},{5,0},{6,1},{7,2},{8,13},{9,14},{1... | collective-permute-start | bytes 110600 | tf_op jit(solution)/shard_map/ppermute | solution.py:699
  16.3 5.1 %collective-permute-start.7 = (f32[16,512]{1,0:T(8,128)S(1)}, f32[16,512]{1,0:T(8,128)S(1)}, u32[]{:S(2)}, u32[]{:S(2)}) collective-permute-start(f32[16,512]{1,0:T(8,128)S(1)} %get-tuple-element.58), channel_id=1, source_target_pairs={{0,24},{8,16},{16,8},{24,0},{1,25},{9,17},{17,9},{25,1},{2,26},{10... | collective-permute-start | bytes 98312 | tf_op jit(solution)/shard_map/ppermute | solution.py:818
  19.3 2.8 %collective-permute-start.6 = (f32[16,512]{1,0:T(8,128)S(1)}, f32[16,512]{1,0:T(8,128)S(1)}, u32[]{:S(2)}, u32[]{:S(2)}) collective-permute-start(f32[16,512]{1,0:T(8,128)S(1)} %get-tuple-element.58), channel_id=1, source_target_pairs={{0,16},{8,24},{16,0},{24,8},{1,17},{9,25},{17,1},{25,9},{2,18},{10... | collective-permute-start | bytes 98312 | tf_op jit(solution)/shard_map/ppermute | solution.py:818
  19.6 2.5 %collective-permute-start.5 = (f32[16,512]{1,0:T(8,128)S(1)}, f32[16,512]{1,0:T(8,128)S(1)}, u32[]{:S(2)}, u32[]{:S(2)}) collective-permute-start(f32[16,512]{1,0:T(8,128)S(1)} %get-tuple-element.58), channel_id=1, source_target_pairs={{0,8},{8,0},{16,24},{24,16},{1,9},{9,1},{17,25},{25,17},{2,10},{10... | collective-permute-start | bytes 98312 | tf_op jit(solution)/shard_map/ppermute | solution.py:818

commit v9 on v8

--- a/solution.py
+++ b/solution.py
@@ -514,7 +514,7 @@
     first_sub, last_sub = sub == 0, sub == 7
     sent = sub + tx * (7 - 2 * sub) < STEPS
     own = range(tile_row // 8, (tile_row + ROWS) // 8)
-    def make_steps(made):
+    def make_steps(made, side=None):
         def rows_of(b):
             return slice(8 * b, 8 * b + 8)
 
@@ -557,6 +557,8 @@
             hx, hy, hz = [blocks(H[n], c, line) for c in range(3)]
             ey_ahead, ez_ahead = ahead_row(E[n], 1, line, ey), ahead_row(E[n], 2, line, ez)
             for b in made:
+                if side is not None and b not in own and (line == n or side == 0 and line == EXT_LINES - 2 - n):
+                    continue
                 curls = (
                     (ez_next[b] - ez[b]) - (ahead_depth(ey[b]) - ey[b]),
                     (ahead_depth(ex[b]) - ex[b]) - (ez_ahead[b] - ez[b]),
@@ -575,6 +577,8 @@
             hx_last, hz_last = blocks(field, 0, line - 1), blocks(field, 2, line - 1)
             hy_behind, hz_behind = behind_row(field, 1, line, hy), behind_row(field, 2, line, hz)
             for b in [b for b in made if n + 1 < STEPS or b in own]:
+                if side is not None and b not in own and line == (EXT_LINES - 2 - n if side == 0 else n + 1):
+                    continue
                 rows = rows_of(b)
                 curls = (
                     (hz[b] - hz_last[b]) - (hy[b] - behind_depth(hy[b])),
@@ -635,7 +639,7 @@
 
             @pl.when(tx == side)
             def _(side=side):
-                make_steps([2, 1 - side])
+                make_steps([2, 1 - side], side)
                 make_gradient()
         return
     if late:

time: 22.9 us -> 22.9 us (level)
  no operation moved by 1% of the time
where the time goes in v9:
time: 22.9 us; the launch traced here: 22.7 us
  waiting for transfers between devices  7.72 us (34%)
  starting transfers between devices  7.6 us (33%)
  Pallas kernels  6.05 us (26%)
  between operations  0.68 us (3%)
  other arithmetic  0.63 us (3%)
    ppermute x5, waiting for transfers between devices, swap(): return lax.ppermute(value, ('wave', 'tx', 'ty'), pairs)  6.22 us
    ppermute x5, starting transfers between devices, swap(): return lax.ppermute(value, ('wave', 'tx', 'ty'), pairs)  4.08 us
    ppermute x3, starting transfers between devices, on_device(): lax.ppermute(partial, 'wave', [(i, i ^ k) for i in range(4)])  3.52 us
    pallas_call x1, Pallas kernels, on_device(): pl.pallas_call(pack_kernel, out_shape=(f32(FIELDS, LINES, ROWS, LANES), f...  1.58 us
    ppermute x3, waiting for transfers between devices, on_device(): lax.ppermute(partial, 'wave', [(i, i ^ k) for i in range(4)])  1.5 us
    pallas_call x1, Pallas kernels, on_device(): pl.pallas_call(functools.partial(window_part, False, True, tx_count, ty_c...  1.45 us
    pallas_call x1, Pallas kernels, on_device(): pl.pallas_call(functools.partial(window_part, True, False, tx_count, ty_c...  1.23 us
    pallas_call x1, Pallas kernels, on_device(): pl.pallas_call(functools.partial(prepare_kernel, tx_count, ty_count), out...  0.94 us
  transfers between devices with their start and end apart: 8, of which 5 were waited for; matrix products, arithmetic and copies ran while one was open for 0% of the time, Pallas kernels for 13%

profile of v9, /device:TPU:17, one launch (start us, length us, event | category | flops | bytes accessed | tf_op | source)
XLA Modules:
  0.0 22.7 jit_solution(13786073793057128876)
XLA Ops:
  0.6 1.6 %pack.1 = (f32[13,8,16,128]{3,2,1,0:T(8,128)S(1)}, f32[3,8,16,128]{3,2,1,0:T(8,128)S(1)}, f32[46,16,128]{2,1,0:T(8,128)S(1)}, f32[46,16,128]{2,1,0:T(8,128)S(1)}) custom-call(f32[3,4]{1,0:T(4,128)} %table_hbm.3, s32[6]{0:T(128)} %box_hbm.3, f32[1,2,12,16,512]{4,3,2,1,0:T(8,128)} %fields_hbm.1, s32[16,512]{1,0:T(8,128)} %material_hbm.1, f32[16,512]{1,0:T(8,128)} %density_hbm.1), custom_call_target="tpu_custom_call" | custom-call | tf_op jit(solution)/shard_map/pack/pallas_call | solution.py:714
  2.2 1.4 %collective-permute-start.3 = (f32[46,16,128]{2,1,0:T(8,128)S(1)}, f32[46,16,128]{2,1,0:T(8,128)S(1)}, u32[]{:S(2)}, u32[]{:S(2)}) collective-permute-start(f32[46,16,128]{2,1,0:T(8,128)S(1)} %get-tuple-element.40), channel_id=1, source_target_pairs={{0,1},{1,0},{2,3},{3,2},{4,5},{5,4},{6,7},{7,6},{8,9},{9,8},{10,11... | collective-permute-start | bytes 1130504 | tf_op jit(solution)/shard_map/ppermute | solution.py:703
  3.6 0.0 collective-permute-start.4
  3.6 0.0 copy-start
  3.6 0.1 edges.1
  3.7 1.3 %collective-permute-start = (f32[376,128]{1,0:T(8,128)S(1)}, f32[376,128]{1,0:T(8,128)S(1)}, u32[]{:S(2)}, u32[]{:S(2)}) collective-permute-start(f32[376,128]{1,0:T(8,128)S(1)} %get-tuple-element.37), channel_id=1, source_target_pairs={{0,4},{1,5},{2,6},{3,7},{4,0},{5,1},{6,2},{7,3},{8,12},{9,13},{10,... | collective-permute-start | bytes 577544 | tf_op jit(solution)/shard_map/ppermute | solution.py:703
  4.9 1.4 %collective-permute-start.2 = (f32[88,128]{1,0:T(8,128)S(1)}, f32[88,128]{1,0:T(8,128)S(1)}, u32[]{:S(2)}, u32[]{:S(2)}) collective-permute-start(f32[88,128]{1,0:T(8,128)S(1)} %get-tuple-element.39), channel_id=1, source_target_pairs={{0,8},{1,4},{2,5},{3,6},{4,1},{5,2},{6,3},{7,15},{8,0},{9,12},{10,... | collective-permute-start | bytes 135176 | tf_op jit(solution)/shard_map/ppermute | solution.py:703
  6.4 0.0 collective-permute-start.1
  6.4 0.0 copy-done
  6.4 0.9 %prepare.1 = (f32[5,3,24,128]{3,2,1,0:T(8,128)S(1)}, f32[24,128]{1,0:T(8,128)S(1)}, f32[18,24,128]{2,1,0:T(8,128)S(1)}, f32[16,128]{1,0:T(8,128)S(1)}) custom-call(f32[2,5]{1,0:T(2,128)} %bitcast.5, f32[3,4]{1,0:T(4,128)} %table_hbm.3, s32[2]{0:T(128)} %plane_hbm.1, s32[6]{0:T(128)} %box_hbm.3, f32[3,2,2048]{2,1,0:T(2,128)S(1)} %bitcast.4), custom_call_target="tpu_custom_call" | custom-call | tf_op jit(solution)/shard_map/prepare/pallas_call | solution.py:752
  7.3 4.6 %collective-permute-done.3.refs_6_ = f32[46,16,128]{2,1,0:T(8,128)S(1)} collective-permute-done((f32[46,16,128]{2,1,0:T(8,128)S(1)}, f32[46,16,128]{2,1,0:T(8,128)S(1)}, u32[]{:S(2)}, u32[]{:S(2)}) %collective-permute-start.3) | collective-permute-done | bytes 376864 | tf_op jit(solution)/shard_map/ppermute | solution.py:703
  11.9 1.0 %collective-permute-done.4.refs_7_ = f32[46,16,128]{2,1,0:T(8,128)S(1)} collective-permute-done((f32[46,16,128]{2,1,0:T(8,128)S(1)}, f32[46,16,128]{2,1,0:T(8,128)S(1)}, u32[]{:S(2)}, u32[]{:S(2)}) %collective-permute-start.4) | collective-permute-done | bytes 376864 | tf_op jit(solution)/shard_map/ppermute | solution.py:703
  12.9 1.2 %early.1 = (f32[3,18,24,128]{3,2,1,0:T(8,128)S(1)}, f32[3,18,24,128]{3,2,1,0:T(8,128)S(1)}, f32[3,18,24,128]{3,2,1,0:T(8,128)S(1)}, f32[3,18,24,128]{3,2,1,0:T(8...) custom-call(f32[5,3,24,128]{3,2,1,0:T(8,128)S(1)} %get-tuple-element, ...), custom_call_target="tpu_custom_call" | custom-call | tf_op jit(solution)/shard_map/early/pallas_call | solution.py:781
  14.1 0.0 collective-permute-done.1.refs_6_
  14.1 0.6 %collective-permute-done.2.refs_7_ = f32[88,128]{1,0:T(8,128)S(1)} collective-permute-done((f32[88,128]{1,0:T(8,128)S(1)}, f32[88,128]{1,0:T(8,128)S(1)}, u32[]{:S(2)}, u32[]{:S(2)}) %collective-permute-start.2) | collective-permute-done | bytes 45088 | tf_op jit(solution)/shard_map/ppermute | solution.py:703
  14.8 0.0 collective-permute-done.refs_5_
  14.8 1.4 %late.1 = (f32[3,8,16,128]{3,2,1,0:T(8,128)S(1)}, f32[16,512]{1,0:T(8,128)S(1)}, f32[3,18,24,128]{3,2,1,0:T(8,128)S(1)}, f32[3,18,24,128]{3,2,1,0:T(8,128)S(1)},...) custom-call(f32[5,3,24,128]{3,2,1,0:T(8,128)S(1)} %get-tuple-element, ...), custom_call_target="tpu_custom_call", output_to_operand_aliasing={{2}: (8, {}), {3}: (9, {}), {4}: (10, {}), {5}: (11, {}), {... | custom-call | tf_op jit(solution)/shard_map/late/pallas_call | solution.py:791
  16.2 3.0 %collective-permute-start.7 = (f32[16,512]{1,0:T(8,128)S(1)}, f32[16,512]{1,0:T(8,128)S(1)}, u32[]{:S(2)}, u32[]{:S(2)}) collective-permute-start(f32[16,512]{1,0:T(8,128)S(1)} %get-tuple-element.58), channel_id=1, source_target_pairs={{0,24},{8,16},{16,8},{24,0},{1,25},{9,17},{17,9},{25,1},{2,26},{10... | collective-permute-start | bytes 98312 | tf_op jit(solution)/shard_map/ppermute | solution.py:822
  19.3 0.2 collective-permute-start.6
  19.5 0.2 %collective-permute-start.5 = (f32[16,512]{1,0:T(8,128)S(1)}, f32[16,512]{1,0:T(8,128)S(1)}, u32[]{:S(2)}, u32[]{:S(2)}) collective-permute-start(f32[16,512]{1,0:T(8,128)S(1)} %get-tuple-element.58), channel_id=1, source_target_pairs={{0,8},{8,0},{16,24},{24,16},{1,9},{9,1},{17,25},{25,17},{2,10},{10... | collective-permute-start | bytes 98312 | tf_op jit(solution)/shard_map/ppermute | solution.py:822
  19.8 0.8 %emit.1 = f32[1,2,3,16,512]{4,3,2,1,0:T(8,128)} custom-call(f32[3,8,16,128]{3,2,1,0:T(8,128)S(1)} %get-tuple-element.59.electric), custom_call_target="tpu_custom_call" | custom-call | tf_op jit(solution)/shard_map/emit/pallas_call | solution.py:811
  20.5 0.8 %collective-permute-done.7 = f32[16,512]{1,0:T(8,128)S(1)} collective-permute-done((f32[16,512]{1,0:T(8,128)S(1)}, f32[16,512]{1,0:T(8,128)S(1)}, u32[]{:S(2)}, u32[]{:S(2)}) %collective-permute-start.7) | collective-permute-done | bytes 32800 | tf_op jit(solution)/shard_map/ppermute | solution.py:822
  21.4 0.7 %collective-permute-done.6 = f32[16,512]{1,0:T(8,128)S(1)} collective-permute-done((f32[16,512]{1,0:T(8,128)S(1)}, f32[16,512]{1,0:T(8,128)S(1)}, u32[]{:S(2)}, u32[]{:S(2)}) %collective-permute-start.6) | collective-permute-done | bytes 32800 | tf_op jit(solution)/shard_map/ppermute | solution.py:822
  22.0 0.0 collective-permute-done.5
  22.0 0.6 %add_add_fusion = f32[16,512]{1,0:T(8,128)} fusion(f32[16,512]{1,0:T(8,128)S(1)} %collective-permute-done.6, f32[16,512]{1,0:T(8,128)S(1)} %collective-permute-done.7, f32[16,512]{1,0:T(8,128)S(1)} %get-tuple-element.58, f32[16,512]{1,0:T(8,128)S(1)} %collective-permute-done.5), kind=kLoop, calls=%fused_computation | loop fusion | flops 24576 | bytes 163840 | tf_op jit(solution)/shard_map/add | solution.py:824
Async XLA Ops:
  2.2 9.7 %collective-permute-start.3 = (f32[46,16,128]{2,1,0:T(8,128)S(1)}, f32[46,16,128]{2,1,0:T(8,128)S(1)}, u32[]{:S(2)}, u32[]{:S(2)}) collective-permute-start(f32[46,16,128]{2,1,0:T(8,128)S(1)} %get-tuple-element.40), channel_id=1, source_target_pairs={{0,1},{1,0},{2,3},{3,2},{4,5},{5,4},{6,7},{7,6},{8,9},{9,8},{10,11... | collective-permute-start | bytes 1130504 | tf_op jit(solution)/shard_map/ppermute | solution.py:703
  3.6 9.3 %collective-permute-start.4 = (f32[46,16,128]{2,1,0:T(8,128)S(1)}, f32[46,16,128]{2,1,0:T(8,128)S(1)}, u32[]{:S(2)}, u32[]{:S(2)}) collective-permute-start(f32[46,16,128]{2,1,0:T(8,128)S(1)} %get-tuple-element.41), channel_id=1, source_target_pairs={{0,8},{1,2},{2,1},{3,11},{4,12},{5,6},{6,5},{7,15},{8,0},{9,10},{1... | collective-permute-start | bytes 1130504 | tf_op jit(solution)/shard_map/ppermute | solution.py:703
  3.6 2.8 %copy-start = (f32[1,2,3,2048]{3,1,2,0:T(2,128)S(1)}, f32[1,2,3,2048]{3,1,2,0:T(2,128)}, u32[]{:S(2)}) copy-start(f32[1,2,3,2048]{3,1,2,0:T(2,128)} %param.9) | copy-start | bytes 147460
  3.7 11.1 %collective-permute-start = (f32[376,128]{1,0:T(8,128)S(1)}, f32[376,128]{1,0:T(8,128)S(1)}, u32[]{:S(2)}, u32[]{:S(2)}) collective-permute-start(f32[376,128]{1,0:T(8,128)S(1)} %get-tuple-element.37), channel_id=1, source_target_pairs={{0,4},{1,5},{2,6},{3,7},{4,0},{5,1},{6,2},{7,3},{8,12},{9,13},{10,... | collective-permute-start | bytes 577544 | tf_op jit(solution)/shard_map/ppermute | solution.py:703
  4.9 9.8 %collective-permute-start.2 = (f32[88,128]{1,0:T(8,128)S(1)}, f32[88,128]{1,0:T(8,128)S(1)}, u32[]{:S(2)}, u32[]{:S(2)}) collective-permute-start(f32[88,128]{1,0:T(8,128)S(1)} %get-tuple-element.39), channel_id=1, source_target_pairs={{0,8},{1,4},{2,5},{3,6},{4,1},{5,2},{6,3},{7,15},{8,0},{9,12},{10,... | collective-permute-start | bytes 135176 | tf_op jit(solution)/shard_map/ppermute | solution.py:703
  6.4 7.8 %collective-permute-start.1 = (f32[72,128]{1,0:T(8,128)S(1)}, f32[72,128]{1,0:T(8,128)S(1)}, u32[]{:S(2)}, u32[]{:S(2)}) collective-permute-start(f32[72,128]{1,0:T(8,128)S(1)} %get-tuple-element.38), channel_id=1, source_target_pairs={{0,5},{1,6},{2,7},{3,11},{4,12},{5,0},{6,1},{7,2},{8,13},{9,14},{1... | collective-permute-start | bytes 110600 | tf_op jit(solution)/shard_map/ppermute | solution.py:703
  16.2 5.1 %collective-permute-start.7 = (f32[16,512]{1,0:T(8,128)S(1)}, f32[16,512]{1,0:T(8,128)S(1)}, u32[]{:S(2)}, u32[]{:S(2)}) collective-permute-start(f32[16,512]{1,0:T(8,128)S(1)} %get-tuple-element.58), channel_id=1, source_target_pairs={{0,24},{8,16},{16,8},{24,0},{1,25},{9,17},{17,9},{25,1},{2,26},{10... | collective-permute-start | bytes 98312 | tf_op jit(solution)/shard_map/ppermute | solution.py:822
  19.3 2.8 %collective-permute-start.6 = (f32[16,512]{1,0:T(8,128)S(1)}, f32[16,512]{1,0:T(8,128)S(1)}, u32[]{:S(2)}, u32[]{:S(2)}) collective-permute-start(f32[16,512]{1,0:T(8,128)S(1)} %get-tuple-element.58), channel_id=1, source_target_pairs={{0,16},{8,24},{16,0},{24,8},{1,17},{9,25},{17,1},{25,9},{2,18},{10... | collective-permute-start | bytes 98312 | tf_op jit(solution)/shard_map/ppermute | solution.py:822
  19.5 2.5 %collective-permute-start.5 = (f32[16,512]{1,0:T(8,128)S(1)}, f32[16,512]{1,0:T(8,128)S(1)}, u32[]{:S(2)}, u32[]{:S(2)}) collective-permute-start(f32[16,512]{1,0:T(8,128)S(1)} %get-tuple-element.58), channel_id=1, source_target_pairs={{0,8},{8,0},{16,24},{24,16},{1,9},{9,1},{17,25},{25,17},{2,10},{10... | collective-permute-start | bytes 98312 | tf_op jit(solution)/shard_map/ppermute | solution.py:822
